TPU v7x, 256 devices: a whole 4x4x8 slice. The times are simulated.
256 devices in a mesh: fsdp: 16 (over z, core), expert: 16 (over y, x).
Axes of the slice: x: 4, y: 4, z: 8, core: 2. Of those that a mesh axis runs over, the one named last changes fastest.
Arguments:
- tokens: bfloat16 [32768, 4096], P(('fsdp', 'expert')), may hold values from -6 to 6
- cotangent: bfloat16 [32768, 4096], P(('fsdp', 'expert')), may hold values from -24 to 24
- routed_expert_index: int32 [32768, 2], P(('fsdp', 'expert')), may hold values from 0 to 15, all different within a row; in each aligned block of 128 rows (0 to 127, 128 to 255, ...) at most 20 rows name the same one
- router_gate_weights: bfloat16 [32768, 2], P(('fsdp', 'expert')), may hold values from 0.049804688 to 1
- token_tenant_index: int32 [32768], P(('fsdp', 'expert')), may hold values from 0 to 3
- frozen_gate_weight: bfloat16 [16, 4096, 768], P('expert', 'fsdp'), may hold values from -0.09375 to 0.09375
- frozen_up_weight: bfloat16 [16, 4096, 768], P('expert', 'fsdp'), may hold values from -0.09375 to 0.09375
- frozen_down_weight: bfloat16 [16, 768, 4096], P('expert', None, 'fsdp'), may hold values from -0.21875 to 0.21875
- adapter_first_factors: bfloat16 [16, 768, 128], P('expert', 'fsdp'), may hold values from -0.21875 to 0.21875
- adapter_second_factors: bfloat16 [16, 128, 4096], P('expert', None, 'fsdp'), may hold values from -1 to 1
Outputs:
- token_input_gradient: bfloat16 [32768, 4096], P(('fsdp', 'expert'))
- gate_weight_gradient: bfloat16 [32768, 2], P(('fsdp', 'expert'))
- adapter_first_gradient: float32 [16, 768, 128], P('expert', 'fsdp')
- adapter_second_gradient: float32 [16, 128, 4096], P('expert', None, 'fsdp')
Inputs may be any that keep to these rules, and one draw needn't show every extreme that they name: `routed_expert_index`: within each aligned block of 128 tokens (the tokens of one device) no expert is named more than 20 times, a bound that some block reaches; the 2 experts of a token differ.
All inputs are finite; a program needn't handle non-finite values.
Results may differ from a plain program's by a relative error of at most 0.0069.
Values may be sent and summed in bfloat16 or wider, within the bound.
No kernel may reach another device: no remote copies, remote signals or barrier semaphores. Data moves between devices by JAX's collectives and lax.ppermute only.
A program may use at most 128 MiB of HBM per device.

v0:
```python
import jax
import jax.numpy as jnp
from jax import lax
from jax.experimental import pallas as pl
from jax.experimental.pallas import tpu as pltpu
from jax.sharding import PartitionSpec as P

RANK = 32
TENANTS = 4
ADAPTER_SCALE = 2.0
CAPACITY = 20
MAIN = 16
SPARE = CAPACITY - MAIN
QUARTERS = MAIN // SPARE
LANES = 128
SPARE_LANE = 8
TILE = 256

bf16 = jnp.bfloat16
f32 = jnp.float32


def contract(left, right, left_dim, right_dim):
    return lax.dot_general(
        left, right, (((left_dim,), (right_dim,)), ((), ())), preferred_element_type=f32
    )


def iota(shape, dim):
    return lax.broadcasted_iota(jnp.int32, shape, dim)


def slot_places(ids, experts):
    rows, top = ids.shape
    lower = (iota((rows, rows), 1) < iota((rows, rows), 0)).astype(f32).astype(bf16)
    named = iota((rows, LANES), 1)
    total = jnp.zeros((1, LANES), f32)
    places = []
    for j in range(top):
        expert = ids[:, j : j + 1]
        onehot = (named == expert).astype(f32)
        before = contract(lower, onehot.astype(bf16), 1, 0) + total
        total = total + jnp.sum(onehot, axis=0, keepdims=True)
        rank = jnp.sum(before * onehot, axis=1, keepdims=True).astype(jnp.int32)
        main = jnp.where(rank < MAIN, expert * MAIN + rank, -1)
        spare = jnp.where(rank < MAIN, -MAIN * experts, expert * MAIN + rank - MAIN)
        places.append((main, spare))
    return places


def placed(place, slots):
    return (iota((place.shape[0], slots), 1) == place).astype(f32).astype(bf16)


def dispatch_kernel(ids_ref, gate_ref, tenant_ref, tok_ref, cot_ref, x_ref, c_ref, experts):
    width = tok_ref.shape[1]
    part = width // QUARTERS
    slots = experts * MAIN
    places = slot_places(ids_ref[...], experts)
    main = sum(placed(m, slots) for m, _ in places)
    spare = [sum(placed(s + SPARE * q, slots) for _, s in places) for q in range(QUARTERS)]
    for src, dst in ((tok_ref, x_ref), (cot_ref, c_ref)):
        for q in range(QUARTERS):
            cols = slice(q * part, (q + 1) * part)
            dst[:, cols] = contract(main, src[:, cols], 0, 0).astype(bf16)
        last = jnp.zeros((slots, part), f32)
        for q in range(QUARTERS):
            last = last + contract(spare[q], src[:, q * part : (q + 1) * part], 0, 0)
        dst[:, width : width + part] = last.astype(bf16)
    lane = iota((tok_ref.shape[0], LANES), 1)
    tenant = tenant_ref[...]
    meta = jnp.zeros((slots, LANES), f32)
    for j, (m, s) in enumerate(places):
        gate = gate_ref[:, j : j + 1].astype(f32)
        for place, base in ((m, 0), (s, SPARE_LANE)):
            cols = jnp.where(lane == base, gate, (lane - base - 1 == tenant).astype(f32))
            meta = meta + contract(placed(place, slots), cols.astype(bf16), 0, 0)
    c_ref[:, width + part :] = meta.astype(bf16)


def combine_kernel(ids_ref, r_ref, tok_ref, gate_ref, experts):
    width = tok_ref.shape[1]
    part = width // QUARTERS
    slots = experts * MAIN
    places = slot_places(ids_ref[...], experts)
    main = sum(placed(m, slots) for m, _ in places)
    for q in range(QUARTERS):
        spare = sum(placed(s + SPARE * q, slots) for _, s in places)
        cols = slice(q * part, (q + 1) * part)
        both = contract(main, r_ref[:, cols], 1, 0) + contract(
            spare, r_ref[:, width : width + part], 1, 0
        )
        tok_ref[:, cols] = both.astype(bf16)
    meta = r_ref[:, width + part :]
    for j, (m, s) in enumerate(places):
        a = contract(placed(m, slots), meta, 1, 0)[:, 0:1]
        b = contract(placed(s, slots), meta, 1, 0)[:, SPARE_LANE : SPARE_LANE + 1]
        gate_ref[:, j : j + 1] = (a + b).astype(bf16)


def expert_kernel(
    where_ref, x_hbm, c_hbm, w_hbm, a1_ref,
    rg_ref, own_ref, other_ref,
    xs, cs, xo, co, meta_ref, w, acc, hid, hga, parts, spare_rows, first, lowt, sems,
):
    width = w.shape[0]
    half = hid.shape[1]
    rank_all = a1_ref.shape[1]
    part = width // QUARTERS
    slots = x_hbm.shape[0]
    spares = slots // QUARTERS
    rows = slots + spares
    wide = 2 * half

    copies = {}

    def begin(name, src, dst):
        copies[name] = pltpu.make_async_copy(src, dst, sems.at[len(copies)])
        copies[name].start()

    begin("xo", x_hbm.at[:, pl.ds(width, part)], xo)
    begin("co", c_hbm.at[:, pl.ds(width, part)], co)
    for q in range(QUARTERS):
        cols = pl.ds(q * part, part)
        begin(("x", q), x_hbm.at[:, cols], xs.at[pl.ds(0, slots), cols])
        begin(("w", q), w_hbm.at[cols, :], w.at[cols, :])
        begin(("c", q), c_hbm.at[:, cols], cs.at[pl.ds(0, slots), cols])
    begin("meta", c_hbm.at[:, pl.ds(width + part, LANES)], meta_ref)

    def chosen(q):
        row = iota((spares, slots), 0)
        return (
            iota((spares, slots), 1) == (row >> 2) * MAIN + q * SPARE + (row & 3)
        ).astype(f32).astype(bf16)

    copies["xo"].wait()
    copies["co"].wait()
    for q in range(QUARTERS):
        cols = slice(q * part, (q + 1) * part)
        sel = chosen(q)
        xs[slots:, cols] = contract(sel, xo[...], 1, 0).astype(bf16)
        cs[slots:, cols] = contract(sel, co[...], 1, 0).astype(bf16)
    for q in range(QUARTERS):
        cols = slice(q * part, (q + 1) * part)

        def product(rows_ref, at, size):
            out = pl.ds(at, size)
            got = contract(rows_ref[:, cols], w[cols, out], 1, 0)
            if q == 0:
                acc[:, out] = got
            else:
                acc[:, out] += got

        copies[("x", q)].wait()
        copies[("w", q)].wait()

        @pl.loop(0, wide // TILE)
        def _(n):
            product(xs, pl.multiple_of(n * TILE, TILE), TILE)

        copies[("c", q)].wait()

        @pl.loop(0, half // TILE)
        def _(n):
            product(cs, pl.multiple_of(wide + n * TILE, TILE), TILE)

        product(cs, wide + half, rank_all)

    copies["meta"].wait()
    meta = meta_ref[...]
    meta_spare = contract(chosen(0), meta, 1, 0).astype(bf16)
    lane_in, lane_out = iota((LANES, rank_all), 0), iota((LANES, rank_all), 1)

    def spread(base):
        mask = (lane_in - base - 1 == lane_out // RANK).astype(f32).astype(bf16)
        gate = (lane_in == base).astype(f32).astype(bf16)
        return mask, gate

    mask_0, gate_0 = spread(0)
    mask_s, gate_s = spread(SPARE_LANE)
    mask = jnp.concatenate(
        [contract(meta, mask_0, 1, 0), contract(meta_spare, mask_s, 1, 0)], axis=0
    )
    gate = jnp.concatenate(
        [contract(meta, gate_0, 1, 0), contract(meta_spare, gate_s, 1, 0)], axis=0
    )

    step = 32

    @pl.loop(0, rows // step)
    def _(i):
        r = pl.ds(pl.multiple_of(i * step, step), step)
        pre_gate, pre_up = acc[r, :half], acc[r, half:wide]
        hid[r, :] = (pre_gate * jax.nn.sigmoid(pre_gate) * pre_up).astype(bf16)

    a1 = a1_ref[...]
    cot_low = acc[:, wide + half :] * mask
    low = (contract(hid[...], a1, 1, 0) * mask).astype(bf16)
    low_grad = (ADAPTER_SCALE * gate * cot_low).astype(bf16)
    hga[...] = contract(low_grad, a1, 1, 1)
    acc[:, wide + half :] = ADAPTER_SCALE * low.astype(f32) * cot_low
    lowt[...] = (ADAPTER_SCALE * gate * low.astype(f32)).astype(bf16)
    first[...] = contract(hid[...], low_grad, 0, 0)
    xs[:, :LANES] = gate.astype(bf16)

    @pl.loop(0, rows // step)
    def _(i):
        r = pl.ds(pl.multiple_of(i * step, step), step)
        pre_gate, pre_up, cot_down = acc[r, :half], acc[r, half:wide], acc[r, wide : wide + half]
        s = jax.nn.sigmoid(pre_gate)
        grad = xs[r, 0:1].astype(f32) * cot_down + hga[r, :]
        parts[r, half:] = (grad * (pre_gate * s)).astype(bf16)
        parts[r, :half] = (grad * pre_up * s * (1.0 + pre_gate * (1.0 - s))).astype(bf16)
        dot = jnp.sum(hid[r, :].astype(f32) * cot_down, axis=1, keepdims=True) + jnp.sum(
            acc[r, wide + half :], axis=1, keepdims=True
        )
        xs[r, LANES : 2 * LANES] = jnp.broadcast_to(dot, (step, LANES)).astype(bf16)

    @pl.loop(0, width // TILE)
    def _(d):
        cols = pl.ds(pl.multiple_of(d * TILE, TILE), TILE)
        got = contract(parts[...], w[cols, :wide], 1, 1).astype(bf16)
        rg_ref[:, cols] = got[:slots]
        spare_rows[:, cols] = got[slots:]

    last = jnp.zeros((slots, part), f32)
    for q in range(QUARTERS):
        last = last + contract(chosen(q), spare_rows[:, q * part : (q + 1) * part], 0, 0)
    rg_ref[:, width : width + part] = last.astype(bf16)
    dots = xs[:, LANES : 2 * LANES].astype(f32)
    lane = iota((slots, LANES), 1)
    spare_dots = contract(chosen(0), dots[slots:].astype(bf16), 0, 0)
    rg_ref[:, width + part :] = jnp.where(
        lane == 0, dots[:slots], jnp.where(lane == SPARE_LANE, spare_dots, 0.0)
    ).astype(bf16)

    z, core = where_ref[0], where_ref[1]
    zs = own_ref.shape[0]
    share = first.shape[0] // (2 * zs)

    @pl.loop(0, zs)
    def _(dz):
        for ref, side in ((own_ref, core), (other_ref, 1 - core)):
            f = lax.rem(z + dz, zs) * 2 + side
            cols = pl.ds(pl.multiple_of(f * TILE, TILE), TILE)
            ref[dz, :rank_all, :] = contract(lowt[...], cs[:, cols], 0, 0).astype(bf16)
            at = pl.multiple_of(f * share, 16)
            block = first[pl.ds(at, share), :].astype(bf16)
            ref[dz, rank_all : rank_all + 16, :rank_all] = block[:16]
            ref[dz, rank_all : rank_all + 16, rank_all:] = block[16:32]
            ref[dz, rank_all + 16 :, :rank_all] = block[32:48]
            ref[dz, rank_all + 16 :, rank_all:] = jnp.zeros((16, TILE - rank_all), bf16)


VMEM = pl.BlockSpec(memory_space=pltpu.VMEM)
ANY = pl.BlockSpec(memory_space=pl.ANY)
SMEM = pl.BlockSpec(memory_space=pltpu.SMEM)


def shards(
    tokens,
    cotangent,
    routed_expert_index,
    router_gate_weights,
    token_tenant_index,
    frozen_gate_weight,
    frozen_up_weight,
    frozen_down_weight,
    adapter_first_factors,
    adapter_second_factors,
):
    experts, spread = lax.axis_size("expert"), lax.axis_size("fsdp")
    tok_rows, top = routed_expert_index.shape
    width = tokens.shape[1]
    half = frozen_gate_weight.shape[2]
    ranks = adapter_first_factors.shape[2]
    part = width // QUARTERS
    slots = experts * MAIN
    spares = slots // QUARTERS
    rows = slots + spares
    cols = 3 * half + ranks
    zs = spread // 2
    here = lax.axis_index("fsdp")
    where = jnp.stack([here // 2, here % 2]).astype(jnp.int32)

    packed = jnp.concatenate(
        [
            frozen_gate_weight[0],
            frozen_up_weight[0],
            frozen_down_weight[0].T,
            adapter_second_factors[0].T,
        ],
        axis=1,
    )
    weights = lax.all_gather(packed, "fsdp", axis=0, tiled=True)

    x_send, c_send = pl.pallas_call(
        lambda *refs: dispatch_kernel(*refs, experts=experts),
        out_shape=(
            jax.ShapeDtypeStruct((slots, width + part), bf16),
            jax.ShapeDtypeStruct((slots, width + part + LANES), bf16),
        ),
        in_specs=[VMEM] * 5,
        out_specs=(VMEM, VMEM),
        compiler_params=pltpu.CompilerParams(vmem_limit_bytes=40 << 20),
    )(
        routed_expert_index,
        router_gate_weights,
        token_tenant_index.reshape(tok_rows, 1),
        tokens,
        cotangent,
    )

    def exchange(rows_2d):
        block = rows_2d.reshape(experts, MAIN, rows_2d.shape[1])
        return lax.all_to_all(block, "expert", split_axis=0, concat_axis=0, tiled=True).reshape(
            rows_2d.shape
        )

    x_rows, c_rows = exchange(x_send), exchange(c_send)
    first_full = lax.all_to_all(
        jnp.broadcast_to(adapter_first_factors, (spread,) + adapter_first_factors.shape[1:]),
        "fsdp",
        split_axis=0,
        concat_axis=0,
        tiled=True,
    ).reshape(half, ranks)

    back, own, other = pl.pallas_call(
        expert_kernel,
        out_shape=(
            jax.ShapeDtypeStruct((slots, width + part + LANES), bf16),
            jax.ShapeDtypeStruct((zs, ranks + 32, TILE), bf16),
            jax.ShapeDtypeStruct((zs, ranks + 32, TILE), bf16),
        ),
        in_specs=[SMEM, ANY, ANY, ANY, VMEM],
        out_specs=(VMEM, VMEM, VMEM),
        scratch_shapes=[
            pltpu.VMEM((rows, width), bf16),
            pltpu.VMEM((rows, width), bf16),
            pltpu.VMEM((slots, part), bf16),
            pltpu.VMEM((slots, part), bf16),
            pltpu.VMEM((slots, LANES), bf16),
            pltpu.VMEM((width, cols), bf16),
            pltpu.VMEM((rows, cols), f32),
            pltpu.VMEM((rows, half), bf16),
            pltpu.VMEM((rows, half), f32),
            pltpu.VMEM((rows, 2 * half), bf16),
            pltpu.VMEM((spares, width), bf16),
            pltpu.VMEM((half, ranks), f32),
            pltpu.VMEM((rows, ranks), bf16),
            pltpu.SemaphoreType.DMA((3 + 3 * QUARTERS,)),
        ],
        compiler_params=pltpu.CompilerParams(vmem_limit_bytes=52 << 20),
    )(where, x_rows, c_rows, weights, first_full)

    returned = exchange(back)

    swap = [(f, f ^ 1) for f in range(spread)]
    pair = own.astype(f32) + lax.ppermute(other, "fsdp", swap).astype(f32)
    halved = pair.astype(bf16)
    total = pair[0]
    for dz in range(1, zs):
        moves = [(f, (f + 2 * dz) % spread) for f in range(spread)]
        total = total + lax.ppermute(halved[dz], "fsdp", moves).astype(f32)
    adapter_second_gradient = total[None, :ranks]
    adapter_first_gradient = jnp.concatenate(
        [
            total[ranks : ranks + 16, :ranks],
            total[ranks : ranks + 16, ranks:],
            total[ranks + 16 :, :ranks],
        ],
        axis=0,
    )[None]

    token_input_gradient, gate_weight_gradient = pl.pallas_call(
        lambda *refs: combine_kernel(*refs, experts=experts),
        out_shape=(
            jax.ShapeDtypeStruct((tok_rows, width), bf16),
            jax.ShapeDtypeStruct((tok_rows, top), bf16),
        ),
        in_specs=[VMEM] * 2,
        out_specs=(VMEM, VMEM),
        compiler_params=pltpu.CompilerParams(vmem_limit_bytes=32 << 20),
    )(routed_expert_index, returned)
    return (
        token_input_gradient,
        gate_weight_gradient,
        adapter_first_gradient,
        adapter_second_gradient,
    )


def solution(mesh):
    in_specs = (
        P(("fsdp", "expert"), None),
        P(("fsdp", "expert"), None),
        P(("fsdp", "expert"), None),
        P(("fsdp", "expert"), None),
        P(("fsdp", "expert")),
        P("expert", "fsdp", None),
        P("expert", "fsdp", None),
        P("expert", None, "fsdp"),
        P("expert", "fsdp", None),
        P("expert", None, "fsdp"),
    )
    out_specs = (
        P(("fsdp", "expert"), None),
        P(("fsdp", "expert"), None),
        P("expert", "fsdp", None),
        P("expert", None, "fsdp"),
    )
    return jax.shard_map(shards, mesh=mesh, in_specs=in_specs, out_specs=out_specs, check_vma=False)
```

profile of v0, /device:TPU:1, one launch (start us, length us, event | category | flops | bytes accessed | tf_op | source)
XLA Modules:
  0.0 216.2 jit_solution(15353215737907152320)
XLA Ops:
  7.2 0.9 copy.18
  8.2 1.2 copy.17
  9.4 2.3 %pad_maximum_fusion = bf16[256,2432]{1,0:T(8,128)(2,1)} fusion(bf16[256,128]{1,0:T(8,128)(2,1)S(1)} %bitcast.62, bf16[256,768]{1,0:T(8,128)(2,1)S(1)} %bitcast.59, bf16[256,768]{1,0:T(8,128)(2,1)} %bitcast.60, bf16[256,768]{1,0:T(8,128)(2,1)} %bitcast.61), kind=kLoop, calls=%fused_computation.1 | loop fusion | flops 4980736 | bytes 2490368 | tf_op jit(solution)/shard_map/concatenate | solution.py:286
  11.7 0.7 broadcast_in_dim.14
  12.4 10.0 %all-to-all-start.2 = ((bf16[16,48,128]{2,1,0:T(8,128)(2,1)}), bf16[16,48,128]{2,1,0:T(8,128)(2,1)S(1)}, u32[]{:S(2)}, u32[]{:S(2)}) async-start(bf16[16,48,128]{2,1,0:T(8,128)(2,1)} %broadcast_in_dim.14), calls=%async_computation.2 | async-start | bytes 393216 | tf_op jit(solution)/shard_map/all_to_all | solution.py:321
  22.8 1.2 copy-done
  24.0 1.2 copy-done.1
  25.2 4.4 %shard_map.129 = (bf16[256,5120]{1,0:T(8,128)(2,1)S(1)}, bf16[256,5248]{1,0:T(8,128)(2,1)}) custom-call(s32[128,2]{1,0:T(8,128)S(1)} %copy.19.refs_0_, bf16[128,2]{1,0:T(8,128)(2,1)S(1)} %copy.15.refs_1_, s32[128,1]{1,0:T(8,128)S(1)} %copy.16.refs_2_, bf16[128,4096]{1,0:T(8,128)(2,1)S(1)} %copy-done, bf16[128,4096]{1,0:T(8,128)(2,1)S(1)} %copy-done.1), custom_call_target="tpu_custom_call" | custom-call | tf_op jit(solution)/shard_map/pallas_call | solution.py:297
  29.6 3.1 %all-to-all-done.2 = bf16[16,48,128]{2,1,0:T(8,128)(2,1)S(1)} async-done(((bf16[16,48,128]{2,1,0:T(8,128)(2,1)}), bf16[16,48,128]{2,1,0:T(8,128)(2,1)S(1)}, u32[]{:S(2)}, u32[]{:S(2)}) %all-to-all-start.2) | async-done | bytes 196640 | tf_op jit(solution)/shard_map/all_to_all | solution.py:321
  32.7 40.7 %all_to_all.20 = bf16[16,16,5120]{2,1,0:T(8,128)(2,1)} all-to-all(bf16[16,16,5120]{2,1,0:T(8,128)(2,1)S(1)} %bitcast.54), channel_id=1, replica_groups=mesh['fsdp'=16,'expert'=16] {'expert'}, dimensions={0} | all-to-all | bytes 5242880 | tf_op jit(solution)/shard_map/all_to_all | solution.py:316
  73.4 3.7 %all-to-all-start.1 = ((bf16[16,16,5248]{2,1,0:T(8,128)(2,1)}), bf16[16,16,5248]{2,1,0:T(8,128)(2,1)S(1)}, u32[]{:S(2)}, u32[]{:S(2)}) async-start(bf16[16,16,5248]{2,1,0:T(8,128)(2,1)} %bitcast.5), calls=%async_computation.1 | async-start | bytes 5373952 | tf_op jit(solution)/shard_map/all_to_all | solution.py:316
  77.2 39.3 %all-to-all-done.1 = bf16[16,16,5248]{2,1,0:T(8,128)(2,1)S(1)} async-done(((bf16[16,16,5248]{2,1,0:T(8,128)(2,1)}), bf16[16,16,5248]{2,1,0:T(8,128)(2,1)S(1)}, u32[]{:S(2)}, u32[]{:S(2)}) %all-to-all-start.1) | async-done | bytes 2687008 | tf_op jit(solution)/shard_map/all_to_all | solution.py:316
  116.5 10.1 %all-gather.2.cloned.1.call-done.w_hbm = bf16[4096,2432]{1,0:T(8,128)(2,1)} async-done(((bf16[256,2432]{1,0:T(8,128)(2,1)}), bf16[4096,2432]{1,0:T(8,128)(2,1)}) %all-gather.2.cloned.1.call-update) | async-done | bytes 19922960 | tf_op jit(solution)/shard_map/all_gather | solution.py:295
  126.7 31.4 %shard_map.130 = (bf16[256,5248]{1,0:T(8,128)(2,1)}, bf16[8,160,256]{2,1,0:T(8,128)(2,1)S(1)}, bf16[8,160,256]{2,1,0:T(8,128)(2,1)S(1)}) custom-call(s32[2]{0:T(128)S(1)} %pad_add_fusion.where_ref, bf16[256,5120]{1,0:T(8,128)(2,1)} %bitcast.57, bf16[256,5248]{1,0:T(8,128)(2,1)} %bitcast.56, bf16[4096,2432]{1,0:T(8,128)(2,1)} %all-gather.2.cloned.1.call-done.w_hbm, ...), custom_call_target="tpu_custom_call" | custom-call | tf_op jit(solution)/shard_map/pallas_call | solution.py:329
  158.1 0.8 copy-done.2
  158.9 6.8 %all-to-all-start.3 = ((bf16[16,16,5248]{2,1,0:T(8,128)(2,1)}), bf16[16,16,5248]{2,1,0:T(8,128)(2,1)S(1)}, u32[]{:S(2)}, u32[]{:S(2)}) async-start(bf16[16,16,5248]{2,1,0:T(8,128)(2,1)} %bitcast.58), calls=%async_computation.3 | async-start | bytes 5373952 | tf_op jit(solution)/shard_map/all_to_all | solution.py:316
  165.6 0.6 collective-permute-start
  166.3 1.9 collective-permute-done
  168.5 2.7 %collective-permute-start.7 = (bf16[160,256]{1,0:T(8,128)(2,1)S(1)}, bf16[160,256]{1,0:T(8,128)(2,1)S(1)}, u32[]{:S(2)}, u32[]{:S(2)}) collective-permute-start(bf16[160,256]{1,0:T(8,128)(2,1)S(1)} %get-tuple-element.25), channel_id=1, source_target_pairs={{0,224},{16,240},{32,0},{48,16},{64,32},{80,48},{96,64},{112,80},{... | collective-permute-start | bytes 245768 | tf_op jit(solution)/shard_map/ppermute | solution.py:365
  171.2 0.7 collective-permute-start.6
  171.9 2.7 %collective-permute-start.5 = (bf16[160,256]{1,0:T(8,128)(2,1)S(1)}, bf16[160,256]{1,0:T(8,128)(2,1)S(1)}, u32[]{:S(2)}, u32[]{:S(2)}) collective-permute-start(bf16[160,256]{1,0:T(8,128)(2,1)S(1)} %get-tuple-element.27), channel_id=1, source_target_pairs={{0,160},{16,176},{32,192},{48,208},{64,224},{80,240},{96,0},{112,1... | collective-permute-start | bytes 245768 | tf_op jit(solution)/shard_map/ppermute | solution.py:365
  174.6 2.0 collective-permute-start.4
  176.6 1.0 collective-permute-start.3
  177.6 2.9 %collective-permute-start.2 = (bf16[160,256]{1,0:T(8,128)(2,1)S(1)}, bf16[160,256]{1,0:T(8,128)(2,1)S(1)}, u32[]{:S(2)}, u32[]{:S(2)}) collective-permute-start(bf16[160,256]{1,0:T(8,128)(2,1)S(1)} %get-tuple-element.30), channel_id=1, source_target_pairs={{0,64},{16,80},{32,96},{48,112},{64,128},{80,144},{96,160},{112,17... | collective-permute-start | bytes 245768 | tf_op jit(solution)/shard_map/ppermute | solution.py:365
  180.5 2.1 collective-permute-done.4
  182.6 6.3 %collective-permute-done.3 = bf16[160,256]{1,0:T(8,128)(2,1)S(1)} collective-permute-done((bf16[160,256]{1,0:T(8,128)(2,1)S(1)}, bf16[160,256]{1,0:T(8,128)(2,1)S(1)}, u32[]{:S(2)}, u32[]{:S(2)}) %collective-permute-start.3) | collective-permute-done | bytes 81952 | tf_op jit(solution)/shard_map/ppermute | solution.py:365
  188.9 1.2 collective-permute-done.2
  190.2 0.6 maximum_bitcast_fusion
  190.8 0.7 slice_bitcast_fusion.1
  191.5 15.2 %all-to-all-done.3 = bf16[16,16,5248]{2,1,0:T(8,128)(2,1)S(1)} async-done(((bf16[16,16,5248]{2,1,0:T(8,128)(2,1)}), bf16[16,16,5248]{2,1,0:T(8,128)(2,1)S(1)}, u32[]{:S(2)}, u32[]{:S(2)}) %all-to-all-start.3) | async-done | bytes 2687008 | tf_op jit(solution)/shard_map/all_to_all | solution.py:316
  206.7 2.1 shard_map.131
  208.8 0.6 copy.20
  (28 shorter events, 0.9 us)
Async XLA Ops:
  7.2 4.5 %copy-start.4 = (bf16[1,48,128]{2,1,0:T(8,128)(2,1)S(1)}, bf16[1,48,128]{2,1,0:T(8,128)(2,1)}, u32[]{:S(2)}) copy-start(bf16[1,48,128]{2,1,0:T(8,128)(2,1)} %param.18) | copy-start | bytes 36868
  7.2 119.5 %all-gather.2.cloned.1.call-start = ((), (), s32[]{:S(2)}) async-start(), calls=%async_computation.4 | async-start | bytes 21168128 | tf_op jit(solution)/shard_map/all_gather | solution.py:295
  8.2 14.2 %copy-start.6 = (bf16[128,2]{0,1:T(2,128)(2,1)S(1)}, bf16[128,2]{0,1:T(2,128)(2,1)}, u32[]{:S(2)}) copy-start(bf16[128,2]{0,1:T(2,128)(2,1)} %param.13) | copy-start | bytes 1540
  8.2 14.4 %copy-start.5 = (s32[128,2]{0,1:T(2,128)S(1)}, s32[128,2]{0,1:T(2,128)}, u32[]{:S(2)}) copy-start(s32[128,2]{0,1:T(2,128)} %param.12) | copy-start | bytes 3076
  8.2 14.5 %copy-start.7 = (s32[128]{0:T(128)S(1)}, s32[128]{0:T(128)}, u32[]{:S(2)}) copy-start(s32[128]{0:T(128)} %param.14) | copy-start | bytes 1540
  12.4 20.3 %all-to-all-start.2 = ((bf16[16,48,128]{2,1,0:T(8,128)(2,1)}), bf16[16,48,128]{2,1,0:T(8,128)(2,1)S(1)}, u32[]{:S(2)}, u32[]{:S(2)}) async-start(bf16[16,48,128]{2,1,0:T(8,128)(2,1)} %broadcast_in_dim.14), calls=%async_computation.2 | async-start | bytes 393216 | tf_op jit(solution)/shard_map/all_to_all | solution.py:321
  22.8 1.2 copy-start
  24.0 1.2 copy-start.1
  73.4 43.1 %all-to-all-start.1 = ((bf16[16,16,5248]{2,1,0:T(8,128)(2,1)}), bf16[16,16,5248]{2,1,0:T(8,128)(2,1)S(1)}, u32[]{:S(2)}, u32[]{:S(2)}) async-start(bf16[16,16,5248]{2,1,0:T(8,128)(2,1)} %bitcast.5), calls=%async_computation.1 | async-start | bytes 5373952 | tf_op jit(solution)/shard_map/all_to_all | solution.py:316
  116.5 10.1 %copy-start.3 = (bf16[16,16,5248]{2,1,0:T(8,128)(2,1)}, bf16[16,16,5248]{2,1,0:T(8,128)(2,1)S(1)}, u32[]{:S(2)}) copy-start(bf16[16,16,5248]{2,1,0:T(8,128)(2,1)S(1)} %all-to-all-done.1) | copy-start | bytes 8060932
  158.0 0.8 copy-start.2
  158.9 47.8 %all-to-all-start.3 = ((bf16[16,16,5248]{2,1,0:T(8,128)(2,1)}), bf16[16,16,5248]{2,1,0:T(8,128)(2,1)S(1)}, u32[]{:S(2)}, u32[]{:S(2)}) async-start(bf16[16,16,5248]{2,1,0:T(8,128)(2,1)} %bitcast.58), calls=%async_computation.3 | async-start | bytes 5373952 | tf_op jit(solution)/shard_map/all_to_all | solution.py:316
  165.6 2.6 %collective-permute-start = (bf16[8,160,256]{2,1,0:T(8,128)(2,1)}, bf16[8,160,256]{2,1,0:T(8,128)(2,1)S(1)}, u32[]{:S(2)}, u32[]{:S(2)}) collective-permute-start(bf16[8,160,256]{2,1,0:T(8,128)(2,1)} %copy-done.2), channel_id=1, source_target_pairs={{0,16},{16,0},{32,48},{48,32},{64,80},{80,64},{96,112},{112,96},{1... | collective-permute-start | bytes 1966088 | tf_op jit(solution)/shard_map/ppermute | solution.py:360
  168.4 8.1 %collective-permute-start.1 = (bf16[160,256]{1,0:T(8,128)(2,1)S(1)}, bf16[160,256]{1,0:T(8,128)(2,1)S(1)}, u32[]{:S(2)}, u32[]{:S(2)}) collective-permute-start(bf16[160,256]{1,0:T(8,128)(2,1)S(1)} %get-tuple-element.24), channel_id=1, source_target_pairs={{0,32},{16,48},{32,64},{48,80},{64,96},{80,112},{96,128},{112,144}... | collective-permute-start | bytes 245768 | tf_op jit(solution)/shard_map/ppermute | solution.py:365
  168.5 9.1 %collective-permute-start.7 = (bf16[160,256]{1,0:T(8,128)(2,1)S(1)}, bf16[160,256]{1,0:T(8,128)(2,1)S(1)}, u32[]{:S(2)}, u32[]{:S(2)}) collective-permute-start(bf16[160,256]{1,0:T(8,128)(2,1)S(1)} %get-tuple-element.25), channel_id=1, source_target_pairs={{0,224},{16,240},{32,0},{48,16},{64,32},{80,48},{96,64},{112,80},{... | collective-permute-start | bytes 245768 | tf_op jit(solution)/shard_map/ppermute | solution.py:365
  171.2 9.3 %collective-permute-start.6 = (bf16[160,256]{1,0:T(8,128)(2,1)S(1)}, bf16[160,256]{1,0:T(8,128)(2,1)S(1)}, u32[]{:S(2)}, u32[]{:S(2)}) collective-permute-start(bf16[160,256]{1,0:T(8,128)(2,1)S(1)} %get-tuple-element.26), channel_id=1, source_target_pairs={{0,192},{16,208},{32,224},{48,240},{64,0},{80,16},{96,32},{112,48}... | collective-permute-start | bytes 245768 | tf_op jit(solution)/shard_map/ppermute | solution.py:365
  171.9 8.6 %collective-permute-start.5 = (bf16[160,256]{1,0:T(8,128)(2,1)S(1)}, bf16[160,256]{1,0:T(8,128)(2,1)S(1)}, u32[]{:S(2)}, u32[]{:S(2)}) collective-permute-start(bf16[160,256]{1,0:T(8,128)(2,1)S(1)} %get-tuple-element.27), channel_id=1, source_target_pairs={{0,160},{16,176},{32,192},{48,208},{64,224},{80,240},{96,0},{112,1... | collective-permute-start | bytes 245768 | tf_op jit(solution)/shard_map/ppermute | solution.py:365
  174.6 8.0 %collective-permute-start.4 = (bf16[160,256]{1,0:T(8,128)(2,1)S(1)}, bf16[160,256]{1,0:T(8,128)(2,1)S(1)}, u32[]{:S(2)}, u32[]{:S(2)}) collective-permute-start(bf16[160,256]{1,0:T(8,128)(2,1)S(1)} %get-tuple-element.28), channel_id=1, source_target_pairs={{0,128},{16,144},{32,160},{48,176},{64,192},{80,208},{96,224},{112... | collective-permute-start | bytes 245768 | tf_op jit(solution)/shard_map/ppermute | solution.py:365
  176.6 12.3 %collective-permute-start.3 = (bf16[160,256]{1,0:T(8,128)(2,1)S(1)}, bf16[160,256]{1,0:T(8,128)(2,1)S(1)}, u32[]{:S(2)}, u32[]{:S(2)}) collective-permute-start(bf16[160,256]{1,0:T(8,128)(2,1)S(1)} %get-tuple-element.29), channel_id=1, source_target_pairs={{0,96},{16,112},{32,128},{48,144},{64,160},{80,176},{96,192},{112,... | collective-permute-start | bytes 245768 | tf_op jit(solution)/shard_map/ppermute | solution.py:365
  177.6 12.5 %collective-permute-start.2 = (bf16[160,256]{1,0:T(8,128)(2,1)S(1)}, bf16[160,256]{1,0:T(8,128)(2,1)S(1)}, u32[]{:S(2)}, u32[]{:S(2)}) collective-permute-start(bf16[160,256]{1,0:T(8,128)(2,1)S(1)} %get-tuple-element.30), channel_id=1, source_target_pairs={{0,64},{16,80},{32,96},{48,112},{64,128},{80,144},{96,160},{112,17... | collective-permute-start | bytes 245768 | tf_op jit(solution)/shard_map/ppermute | solution.py:365
Sparse Core Ops, SparseCore 0:
  11.8 114.7 all-gather.1
where the time goes:
time: 217 us; the launch traced here: 216 us
  waiting for transfers between devices  79.3 us (37%)
  blocking collectives  40.7 us (19%)
  Pallas kernels  37.8 us (17%)
  starting transfers between devices  33.2 us (15%)
  between operations  14.2 us (7%)
  local copies, waits for them, and re-layouts  7.8 us (4%)
  other arithmetic  3.24 us (1%)
    all_to_all x2, waiting for transfers between devices, exchange(): lax.all_to_all(block, 'expert', split_axis=0, concat_axis=0, tiled=True)  54.5 us
    all_to_all x1, blocking collectives, exchange(): lax.all_to_all(block, 'expert', split_axis=0, concat_axis=0, tiled=True)  40.7 us
    pallas_call x1, Pallas kernels, shards(): pl.pallas_call(expert_kernel, out_shape=(jax.ShapeDtypeStruct((slots, wid...  31.4 us
    ppermute x7, starting transfers between devices, shards(): total = total + lax.ppermute(halved[dz], 'fsdp', moves).astype(f32)  12 us
    all_to_all x2, starting transfers between devices, exchange(): lax.all_to_all(block, 'expert', split_axis=0, concat_axis=0, tiled=True)  10.5 us
    all_gather x1, waiting for transfers between devices, shards(): weights = lax.all_gather(packed, 'fsdp', axis=0, tiled=True)  10.1 us
    all_to_all x1, starting transfers between devices, shards(): lax.all_to_all(jnp.broadcast_to(adapter_first_factors, (spread,) + adapte...  9.98 us
    ppermute x7, waiting for transfers between devices, shards(): total = total + lax.ppermute(halved[dz], 'fsdp', moves).astype(f32)  9.61 us
  transfers between devices with their start and end apart: 12, of which 8 were waited for; matrix products, arithmetic and copies ran while one was open for 1% of the time, Pallas kernels for 2%

commit v1 on v0

--- a/solution.py
+++ b/solution.py
@@ -15,6 +15,9 @@
 LANES = 128
 SPARE_LANE = 8
 TILE = 256
+CHUNKS = 4
+LIMIT = 54
+BACK = 1024
 
 bf16 = jnp.bfloat16
 f32 = jnp.float32
@@ -50,6 +53,26 @@
 
 def placed(place, slots):
     return (iota((place.shape[0], slots), 1) == place).astype(f32).astype(bf16)
+
+
+def pack_kernel(gate_hbm, up_hbm, down_hbm, second_hbm, out_hbm, down, second, turned, sems):
+    half = gate_hbm.shape[1]
+    cols = out_hbm.shape[1]
+    load_down = pltpu.make_async_copy(down_hbm, down, sems.at[0])
+    load_second = pltpu.make_async_copy(second_hbm, second, sems.at[1])
+    gate = pltpu.make_async_copy(gate_hbm, out_hbm.at[:, pl.ds(0, half)], sems.at[2])
+    up = pltpu.make_async_copy(up_hbm, out_hbm.at[:, pl.ds(half, half)], sems.at[3])
+    store = pltpu.make_async_copy(turned, out_hbm.at[:, pl.ds(2 * half, cols - 2 * half)], sems.at[4])
+    for copy in (load_down, load_second, gate, up):
+        copy.start()
+    load_down.wait()
+    turned[:, :half] = down[...].T
+    load_second.wait()
+    turned[:, half:] = second[...].T
+    store.start()
+    gate.wait()
+    up.wait()
+    store.wait()
 
 
 def dispatch_kernel(ids_ref, gate_ref, tenant_ref, tok_ref, cot_ref, x_ref, c_ref, experts):
@@ -98,94 +121,91 @@
         gate_ref[:, j : j + 1] = (a + b).astype(bf16)
 
 
+def chosen(q, spares, slots):
+    row = iota((spares, slots), 0)
+    return (
+        (iota((spares, slots), 1) == (row >> 2) * MAIN + q * SPARE + (row & 3))
+        .astype(f32)
+        .astype(bf16)
+    )
+
+
+def unfold_rows(src_ref, dst_ref):
+    width = dst_ref.shape[1]
+    part = width // QUARTERS
+    slots = src_ref.shape[0]
+    spares = slots // QUARTERS
+    dst_ref[:slots, :] = src_ref[:, :width]
+    for q in range(QUARTERS):
+        dst_ref[slots:, q * part : (q + 1) * part] = contract(
+            chosen(q, spares, slots), src_ref[:, width : width + part], 1, 0
+        ).astype(bf16)
+
+
+def unfold_cot_kernel(src_ref, dst_ref, mask_ref, gate_ref):
+    unfold_rows(src_ref, dst_ref)
+    slots = src_ref.shape[0]
+    spares = slots // QUARTERS
+    lanes = mask_ref.shape[1]
+    meta = src_ref[:, src_ref.shape[1] - LANES :]
+    meta_spare = contract(chosen(0, spares, slots), meta, 1, 0).astype(bf16)
+    lane_in, lane_out = iota((LANES, lanes), 0), iota((LANES, lanes), 1)
+    for rows, block, base in ((slice(0, slots), meta, 0), (slice(slots, None), meta_spare, SPARE_LANE)):
+        tenant = (lane_in - base - 1 == lane_out // RANK).astype(f32).astype(bf16)
+        weight = (lane_in == base).astype(f32).astype(bf16)
+        mask_ref[rows, :] = contract(block, tenant, 1, 0)
+        gate_ref[rows, :] = contract(block, weight, 1, 0)
+
+
 def expert_kernel(
-    where_ref, x_hbm, c_hbm, w_hbm, a1_ref,
-    rg_ref, own_ref, other_ref,
-    xs, cs, xo, co, meta_ref, w, acc, hid, hga, parts, spare_rows, first, lowt, sems,
+    x_hbm, c_hbm, w_hbm, a1_hbm, mask_hbm, gate_hbm,
+    rg_hbm, hid_hbm, low_grad_hbm, lowt_hbm,
+    xs, cs, w, a1_ref, mask_ref, gate_ref,
+    rg_ref, hid, low_grad_ref, lowt_ref,
+    acc, hga, parts, spare_rows, dots, sems,
 ):
-    width = w.shape[0]
+    rows, width = xs.shape
     half = hid.shape[1]
-    rank_all = a1_ref.shape[1]
     part = width // QUARTERS
-    slots = x_hbm.shape[0]
-    spares = slots // QUARTERS
-    rows = slots + spares
+    slots = rg_ref.shape[0]
+    spares = rows - slots
     wide = 2 * half
-
-    copies = {}
-
-    def begin(name, src, dst):
-        copies[name] = pltpu.make_async_copy(src, dst, sems.at[len(copies)])
-        copies[name].start()
-
-    begin("xo", x_hbm.at[:, pl.ds(width, part)], xo)
-    begin("co", c_hbm.at[:, pl.ds(width, part)], co)
-    for q in range(QUARTERS):
-        cols = pl.ds(q * part, part)
-        begin(("x", q), x_hbm.at[:, cols], xs.at[pl.ds(0, slots), cols])
-        begin(("w", q), w_hbm.at[cols, :], w.at[cols, :])
-        begin(("c", q), c_hbm.at[:, cols], cs.at[pl.ds(0, slots), cols])
-    begin("meta", c_hbm.at[:, pl.ds(width + part, LANES)], meta_ref)
-
-    def chosen(q):
-        row = iota((spares, slots), 0)
-        return (
-            iota((spares, slots), 1) == (row >> 2) * MAIN + q * SPARE + (row & 3)
-        ).astype(f32).astype(bf16)
-
-    copies["xo"].wait()
-    copies["co"].wait()
-    for q in range(QUARTERS):
-        cols = slice(q * part, (q + 1) * part)
-        sel = chosen(q)
-        xs[slots:, cols] = contract(sel, xo[...], 1, 0).astype(bf16)
-        cs[slots:, cols] = contract(sel, co[...], 1, 0).astype(bf16)
-    for q in range(QUARTERS):
-        cols = slice(q * part, (q + 1) * part)
-
-        def product(rows_ref, at, size):
-            out = pl.ds(at, size)
+    depth = width // CHUNKS
+
+    pending = []
+
+    def begin(src, dst):
+        copy = pltpu.make_async_copy(src, dst, sems.at[len(pending)])
+        copy.start()
+        pending.append(copy)
+        return copy
+
+    chunks = []
+    for q in range(CHUNKS):
+        cols = pl.ds(q * depth, depth)
+        chunks.append(
+            (
+                begin(x_hbm.at[:, cols], xs.at[:, cols]),
+                begin(w_hbm.at[cols, :], w.at[cols, :]),
+                begin(c_hbm.at[:, cols], cs.at[:, cols]),
+            )
+        )
+    small = [begin(a1_hbm, a1_ref), begin(mask_hbm, mask_ref), begin(gate_hbm, gate_ref)]
+
+    for q in range(CHUNKS):
+        cols = slice(q * depth, (q + 1) * depth)
+        for copy in chunks[q]:
+            copy.wait()
+        for rows_ref, out in ((xs, slice(0, wide)), (cs, slice(wide, None))):
             got = contract(rows_ref[:, cols], w[cols, out], 1, 0)
             if q == 0:
                 acc[:, out] = got
             else:
                 acc[:, out] += got
-
-        copies[("x", q)].wait()
-        copies[("w", q)].wait()
-
-        @pl.loop(0, wide // TILE)
-        def _(n):
-            product(xs, pl.multiple_of(n * TILE, TILE), TILE)
-
-        copies[("c", q)].wait()
-
-        @pl.loop(0, half // TILE)
-        def _(n):
-            product(cs, pl.multiple_of(wide + n * TILE, TILE), TILE)
-
-        product(cs, wide + half, rank_all)
-
-    copies["meta"].wait()
-    meta = meta_ref[...]
-    meta_spare = contract(chosen(0), meta, 1, 0).astype(bf16)
-    lane_in, lane_out = iota((LANES, rank_all), 0), iota((LANES, rank_all), 1)
-
-    def spread(base):
-        mask = (lane_in - base - 1 == lane_out // RANK).astype(f32).astype(bf16)
-        gate = (lane_in == base).astype(f32).astype(bf16)
-        return mask, gate
-
-    mask_0, gate_0 = spread(0)
-    mask_s, gate_s = spread(SPARE_LANE)
-    mask = jnp.concatenate(
-        [contract(meta, mask_0, 1, 0), contract(meta_spare, mask_s, 1, 0)], axis=0
-    )
-    gate = jnp.concatenate(
-        [contract(meta, gate_0, 1, 0), contract(meta_spare, gate_s, 1, 0)], axis=0
-    )
-
-    step = 32
+    for copy in small:
+        copy.wait()
+
+    step = 320
 
     @pl.loop(0, rows // step)
     def _(i):
@@ -193,63 +213,79 @@
         pre_gate, pre_up = acc[r, :half], acc[r, half:wide]
         hid[r, :] = (pre_gate * jax.nn.sigmoid(pre_gate) * pre_up).astype(bf16)
 
+    mask, gate = mask_ref[...], gate_ref[...]
     a1 = a1_ref[...]
     cot_low = acc[:, wide + half :] * mask
-    low = (contract(hid[...], a1, 1, 0) * mask).astype(bf16)
     low_grad = (ADAPTER_SCALE * gate * cot_low).astype(bf16)
+    low_grad_ref[...] = low_grad
     hga[...] = contract(low_grad, a1, 1, 1)
-    acc[:, wide + half :] = ADAPTER_SCALE * low.astype(f32) * cot_low
-    lowt[...] = (ADAPTER_SCALE * gate * low.astype(f32)).astype(bf16)
-    first[...] = contract(hid[...], low_grad, 0, 0)
-    xs[:, :LANES] = gate.astype(bf16)
+    low = (contract(hid[...], a1, 1, 0) * mask).astype(bf16).astype(f32)
+    acc[:, wide + half :] = ADAPTER_SCALE * low * cot_low
+    lowt_ref[...] = (ADAPTER_SCALE * gate * low).astype(bf16)
 
     @pl.loop(0, rows // step)
     def _(i):
         r = pl.ds(pl.multiple_of(i * step, step), step)
         pre_gate, pre_up, cot_down = acc[r, :half], acc[r, half:wide], acc[r, wide : wide + half]
         s = jax.nn.sigmoid(pre_gate)
-        grad = xs[r, 0:1].astype(f32) * cot_down + hga[r, :]
+        grad = gate_ref[r, 0:1] * cot_down + hga[r, :]
         parts[r, half:] = (grad * (pre_gate * s)).astype(bf16)
         parts[r, :half] = (grad * pre_up * s * (1.0 + pre_gate * (1.0 - s))).astype(bf16)
         dot = jnp.sum(hid[r, :].astype(f32) * cot_down, axis=1, keepdims=True) + jnp.sum(
             acc[r, wide + half :], axis=1, keepdims=True
         )
-        xs[r, LANES : 2 * LANES] = jnp.broadcast_to(dot, (step, LANES)).astype(bf16)
-
-    @pl.loop(0, width // TILE)
-    def _(d):
-        cols = pl.ds(pl.multiple_of(d * TILE, TILE), TILE)
+        dots[r, :] = jnp.broadcast_to(dot, (step, LANES)).astype(bf16)
+
+    sent = [
+        begin(hid, hid_hbm),
+        begin(low_grad_ref, low_grad_hbm),
+        begin(lowt_ref, lowt_hbm),
+    ]
+    lane = iota((slots, LANES), 1)
+    spare_dots = contract(chosen(0, spares, slots), dots[slots:, :], 0, 0)
+    rg_ref[:, width + part :] = jnp.where(
+        lane == 0, dots[:slots, :].astype(f32), jnp.where(lane == SPARE_LANE, spare_dots, 0.0)
+    ).astype(bf16)
+    for d in range(width // BACK):
+        cols = slice(d * BACK, (d + 1) * BACK)
         got = contract(parts[...], w[cols, :wide], 1, 1).astype(bf16)
         rg_ref[:, cols] = got[:slots]
         spare_rows[:, cols] = got[slots:]
+        place = pl.ds(d * BACK, BACK)
+        sent.append(begin(rg_ref.at[:, place], rg_hbm.at[:, place]))
 
     last = jnp.zeros((slots, part), f32)
     for q in range(QUARTERS):
-        last = last + contract(chosen(q), spare_rows[:, q * part : (q + 1) * part], 0, 0)
+        last = last + contract(
+            chosen(q, spares, slots), spare_rows[:, q * part : (q + 1) * part], 0, 0
+        )
     rg_ref[:, width : width + part] = last.astype(bf16)
-    dots = xs[:, LANES : 2 * LANES].astype(f32)
-    lane = iota((slots, LANES), 1)
-    spare_dots = contract(chosen(0), dots[slots:].astype(bf16), 0, 0)
-    rg_ref[:, width + part :] = jnp.where(
-        lane == 0, dots[:slots], jnp.where(lane == SPARE_LANE, spare_dots, 0.0)
-    ).astype(bf16)
-
+    place = pl.ds(width, part + LANES)
+    sent.append(begin(rg_ref.at[:, place], rg_hbm.at[:, place]))
+    for copy in sent:
+        copy.wait()
+
+
+def adapter_kernel(where_ref, hid_ref, low_grad_ref, lowt_ref, c_ref, own_ref, other_ref, first):
+    ranks = low_grad_ref.shape[1]
     z, core = where_ref[0], where_ref[1]
     zs = own_ref.shape[0]
     share = first.shape[0] // (2 * zs)
+    first[...] = contract(hid_ref[...], low_grad_ref[...], 0, 0)
+    lowt = lowt_ref[...].T
 
     @pl.loop(0, zs)
     def _(dz):
-        for ref, side in ((own_ref, core), (other_ref, 1 - core)):
+        for ref, side in ((other_ref, 1 - core), (own_ref, core)):
             f = lax.rem(z + dz, zs) * 2 + side
             cols = pl.ds(pl.multiple_of(f * TILE, TILE), TILE)
-            ref[dz, :rank_all, :] = contract(lowt[...], cs[:, cols], 0, 0).astype(bf16)
+            ref[dz, :ranks, :] = contract(lowt, c_ref[:, cols], 1, 0).astype(bf16)
             at = pl.multiple_of(f * share, 16)
             block = first[pl.ds(at, share), :].astype(bf16)
-            ref[dz, rank_all : rank_all + 16, :rank_all] = block[:16]
-            ref[dz, rank_all : rank_all + 16, rank_all:] = block[16:32]
-            ref[dz, rank_all + 16 :, :rank_all] = block[32:48]
-            ref[dz, rank_all + 16 :, rank_all:] = jnp.zeros((16, TILE - rank_all), bf16)
+            ref[dz, ranks : ranks + 16, :ranks] = block[:16]
+            ref[dz, ranks : ranks + 16, ranks:] = block[16:32]
+            ref[dz, ranks + 16 :, :ranks] = block[32:48]
+            ref[dz, ranks + 16 :, ranks:] = jnp.zeros((16, TILE - ranks), bf16)
 
 
 VMEM = pl.BlockSpec(memory_space=pltpu.VMEM)
@@ -279,18 +315,29 @@
     spares = slots // QUARTERS
     rows = slots + spares
     cols = 3 * half + ranks
+    shard = frozen_gate_weight.shape[1]
     zs = spread // 2
     here = lax.axis_index("fsdp")
     where = jnp.stack([here // 2, here % 2]).astype(jnp.int32)
 
-    packed = jnp.concatenate(
-        [
-            frozen_gate_weight[0],
-            frozen_up_weight[0],
-            frozen_down_weight[0].T,
-            adapter_second_factors[0].T,
+    packed = pl.pallas_call(
+        pack_kernel,
+        name="pack_weights",
+        out_shape=jax.ShapeDtypeStruct((shard, cols), bf16),
+        in_specs=[ANY] * 4,
+        out_specs=ANY,
+        scratch_shapes=[
+            pltpu.VMEM((half, shard), bf16),
+            pltpu.VMEM((ranks, shard), bf16),
+            pltpu.VMEM((shard, half + ranks), bf16),
+            pltpu.SemaphoreType.DMA((5,)),
         ],
-        axis=1,
+        compiler_params=pltpu.CompilerParams(vmem_limit_bytes=60 << 20),
+    )(
+        frozen_gate_weight[0],
+        frozen_up_weight[0],
+        frozen_down_weight[0],
+        adapter_second_factors[0],
     )
     weights = lax.all_gather(packed, "fsdp", axis=0, tiled=True)
 
@@ -326,33 +373,72 @@
         tiled=True,
     ).reshape(half, ranks)
 
-    back, own, other = pl.pallas_call(
+    x_all = pl.pallas_call(
+        unfold_rows,
+        name="unfold_tokens",
+        out_shape=jax.ShapeDtypeStruct((rows, width), bf16),
+        in_specs=[VMEM],
+        out_specs=VMEM,
+        compiler_params=pltpu.CompilerParams(vmem_limit_bytes=24 << 20),
+    )(x_rows)
+    c_all, mask, gate = pl.pallas_call(
+        unfold_cot_kernel,
+        name="unfold_cotangent",
+        out_shape=(
+            jax.ShapeDtypeStruct((rows, width), bf16),
+            jax.ShapeDtypeStruct((rows, ranks), f32),
+            jax.ShapeDtypeStruct((rows, ranks), f32),
+        ),
+        in_specs=[VMEM],
+        out_specs=(VMEM, VMEM, VMEM),
+        compiler_params=pltpu.CompilerParams(vmem_limit_bytes=24 << 20),
+    )(c_rows)
+
+    back, hidden, low_grad, low_rank = pl.pallas_call(
         expert_kernel,
+        name="expert",
         out_shape=(
             jax.ShapeDtypeStruct((slots, width + part + LANES), bf16),
+            jax.ShapeDtypeStruct((rows, half), bf16),
+            jax.ShapeDtypeStruct((rows, ranks), bf16),
+            jax.ShapeDtypeStruct((rows, ranks), bf16),
+        ),
+        in_specs=[ANY] * 6,
+        out_specs=(ANY, ANY, ANY, ANY),
+        scratch_shapes=[
+            pltpu.VMEM((rows, width), bf16),
+            pltpu.VMEM((rows, width), bf16),
+            pltpu.VMEM((width, cols), bf16),
+            pltpu.VMEM((half, ranks), bf16),
+            pltpu.VMEM((rows, ranks), f32),
+            pltpu.VMEM((rows, ranks), f32),
+            pltpu.VMEM((slots, width + part + LANES), bf16),
+            pltpu.VMEM((rows, half), bf16),
+            pltpu.VMEM((rows, ranks), bf16),
+            pltpu.VMEM((rows, ranks), bf16),
+            pltpu.VMEM((rows, cols), f32),
+            pltpu.VMEM((rows, half), f32),
+            pltpu.VMEM((rows, 2 * half), bf16),
+            pltpu.VMEM((spares, width), bf16),
+            pltpu.VMEM((rows, LANES), bf16),
+            pltpu.SemaphoreType.DMA((3 * CHUNKS + 7 + width // BACK,)),
+        ],
+        compiler_params=pltpu.CompilerParams(vmem_limit_bytes=LIMIT << 20),
+    )(x_all, c_all, weights, first_full, mask, gate)
+
+    own, other = pl.pallas_call(
+        adapter_kernel,
+        name="adapters",
+        out_shape=(
             jax.ShapeDtypeStruct((zs, ranks + 32, TILE), bf16),
             jax.ShapeDtypeStruct((zs, ranks + 32, TILE), bf16),
         ),
-        in_specs=[SMEM, ANY, ANY, ANY, VMEM],
-        out_specs=(VMEM, VMEM, VMEM),
-        scratch_shapes=[
-            pltpu.VMEM((rows, width), bf16),
-            pltpu.VMEM((rows, width), bf16),
-            pltpu.VMEM((slots, part), bf16),
-            pltpu.VMEM((slots, part), bf16),
-            pltpu.VMEM((slots, LANES), bf16),
-            pltpu.VMEM((width, cols), bf16),
-            pltpu.VMEM((rows, cols), f32),
-            pltpu.VMEM((rows, half), bf16),
-            pltpu.VMEM((rows, half), f32),
-            pltpu.VMEM((rows, 2 * half), bf16),
-            pltpu.VMEM((spares, width), bf16),
-            pltpu.VMEM((half, ranks), f32),
-            pltpu.VMEM((rows, ranks), bf16),
-            pltpu.SemaphoreType.DMA((3 + 3 * QUARTERS,)),
-        ],
-        compiler_params=pltpu.CompilerParams(vmem_limit_bytes=52 << 20),
-    )(where, x_rows, c_rows, weights, first_full)
+        in_specs=[SMEM, VMEM, VMEM, VMEM, VMEM],
+        out_specs=(VMEM, VMEM),
+        scratch_shapes=[pltpu.VMEM((half, ranks), f32)],
+        compiler_params=pltpu.CompilerParams(vmem_limit_bytes=24 << 20),
+        cost_estimate=pl.CostEstimate(flops=400_000_000, bytes_accessed=6_000_000, transcendentals=0),
+    )(where, hidden, low_grad, low_rank, c_all)
 
     returned = exchange(back)
 

time: 217 us -> 226 us (1.041)
  waiting for transfers between devices: 79.3 us -> 41.1 us
  blocking collectives: 40.7 us -> 76.9 us
  Pallas kernels: 37.8 us -> 51.6 us
  starting transfers between devices: 33.2 us -> 30.6 us
  local copies, waits for them, and re-layouts: 7.8 us -> 10.4 us
  other arithmetic: 3.24 us -> 0.97 us
    all_to_all x2 -> x1, waiting for transfers between devices: 54.5 us -> 7.6 us  [exchange(): lax.all_to_all(block, 'expert', split_axis=0, concat_axis=0, tiled=True)]
    all_to_all x1 -> x2, blocking collectives: 40.7 us -> 76.9 us  [exchange(): lax.all_to_all(block, 'expert', split_axis=0, concat_axis=0, tiled=True)]
    pallas_call x1 -> x5, Pallas kernels: 31.4 us -> 46.6 us  [the longest x1 25 us: shards(): pl.pallas_call(pack_kernel, name='pack_weights', out_shape=jax.ShapeDtype...]
    all_gather x1, waiting for transfers between devices: 10.1 us -> 14.1 us  [shards(): weights = lax.all_gather(packed, 'fsdp', axis=0, tiled=True)]
    all_to_all x2 -> x1, starting transfers between devices: 10.5 us -> 6.71 us  [exchange(): lax.all_to_all(block, 'expert', split_axis=0, concat_axis=0, tiled=True)]
    ppermute x7, waiting for transfers between devices: 9.61 us -> 12.8 us  [shards(): total = total + lax.ppermute(halved[dz], 'fsdp', moves).astype(f32)]
    unnamed x21 -> x35, local copies, waits for them, and re-layouts: 6.28 us -> 8.88 us
    concatenate x1 -> x0, other arithmetic: 2.28 us -> none  [shards(): jnp.concatenate([frozen_gate_weight[0], frozen_up_weight[0], frozen_down_...]
  transfers between devices with their start and end apart: 12 -> 11, of which waited for: 8 -> 7; matrix products, arithmetic and copies ran while one was open for 1% -> 1% of each run, Pallas kernels for 2% -> 3%
where the time goes in v1:
time: 226 us
  blocking collectives  76.9 us (34%)
  Pallas kernels  51.6 us (23%)
  waiting for transfers between devices  41.1 us (18%)
  starting transfers between devices  30.6 us (14%)
  between operations  14.2 us (6%)
  local copies, waits for them, and re-layouts  10.4 us (5%)
    all_to_all x2, blocking collectives, exchange(): lax.all_to_all(block, 'expert', split_axis=0, concat_axis=0, tiled=True)  76.9 us
    pallas_call x1, Pallas kernels, shards(): pl.pallas_call(pack_kernel, name='pack_weights', out_shape=jax.ShapeDtype...  25 us
    pallas_call x1, Pallas kernels, shards(): pl.pallas_call(expert_kernel, name='expert', out_shape=(jax.ShapeDtypeStr...  17.4 us
    all_gather x1, waiting for transfers between devices, shards(): weights = lax.all_gather(packed, 'fsdp', axis=0, tiled=True)  14.1 us
    ppermute x7, waiting for transfers between devices, shards(): total = total + lax.ppermute(halved[dz], 'fsdp', moves).astype(f32)  12.8 us
    ppermute x7, starting transfers between devices, shards(): total = total + lax.ppermute(halved[dz], 'fsdp', moves).astype(f32)  11.8 us
    all_to_all x1, starting transfers between devices, shards(): lax.all_to_all(jnp.broadcast_to(adapter_first_factors, (spread,) + adapte...  11.2 us
    unnamed x35, local copies, waits for them, and re-layouts  8.88 us
  transfers between devices with their start and end apart: 11, of which 7 were waited for; matrix products, arithmetic and copies ran while one was open for 1% of the time, Pallas kernels for 3%

profile of v1, /device:TPU:1, one launch (start us, length us, event | category | flops | bytes accessed | tf_op | source)
XLA Modules:
  0.0 225.8 jit_solution(1105583324267852200)
XLA Ops:
  7.3 25.0 %pack_weights.1 = bf16[256,2432]{1,0:T(8,128)(2,1)} custom-call(bf16[256,768]{1,0:T(8,128)(2,1)} %bitcast.56, bf16[256,768]{1,0:T(8,128)(2,1)} %bitcast.57, bf16[768,256]{1,0:T(8,128)(2,1)} %bitcast.58, bf16[128,256]{1,0:T(8,128)(2,1)} %bitcast.59), custom_call_target="tpu_custom_call" | custom-call | tf_op jit(solution)/shard_map/pack_weights/pallas_call | solution.py:323
  32.7 2.9 %shard_map.129 = (bf16[256,5120]{1,0:T(8,128)(2,1)S(1)}, bf16[256,5248]{1,0:T(8,128)(2,1)S(1)}) custom-call(s32[128,2]{1,0:T(8,128)S(1)} %copy.17.refs_0_, bf16[128,2]{1,0:T(8,128)(2,1)S(1)} %copy.15.refs_1_, s32[128,1]{1,0:T(8,128)S(1)} %copy.16.refs_2_, bf16[128,4096]{1,0:T(8,128)(2,1)S(1)} %copy-done.4, bf16[128,4096]{1,0:T(8,128)(2,1)S(1)} %copy-done.5), custom_call_target="tpu_custom_call" | custom-call | tf_op jit(solution)/shard_map/pallas_call | solution.py:344
  35.5 40.5 %all_to_all.20 = bf16[16,16,5120]{2,1,0:T(8,128)(2,1)} all-to-all(bf16[16,16,5120]{2,1,0:T(8,128)(2,1)S(1)} %bitcast.53), channel_id=1, replica_groups=mesh['fsdp'=16,'expert'=16] {'expert'}, dimensions={0} | all-to-all | bytes 5242880 | tf_op jit(solution)/shard_map/all_to_all | solution.py:363
  76.0 36.5 %all_to_all.21 = bf16[16,16,5248]{2,1,0:T(8,128)(2,1)S(1)} all-to-all(bf16[16,16,5248]{2,1,0:T(8,128)(2,1)S(1)} %bitcast.52), channel_id=1, replica_groups=mesh['fsdp'=16,'expert'=16] {'expert'}, dimensions={0} | all-to-all | bytes 5373952 | tf_op jit(solution)/shard_map/all_to_all | solution.py:363
  112.5 0.7 broadcast_in_dim.14
  113.2 11.2 %all-to-all-start.2 = ((bf16[16,48,128]{2,1,0:T(8,128)(2,1)}), bf16[16,48,128]{2,1,0:T(8,128)(2,1)S(1)}, u32[]{:S(2)}, u32[]{:S(2)}) async-start(bf16[16,48,128]{2,1,0:T(8,128)(2,1)} %broadcast_in_dim.14), calls=%async_computation.2 | async-start | bytes 393216 | tf_op jit(solution)/shard_map/all_to_all | solution.py:368
  124.4 1.9 copy-done.3
  126.2 0.7 unfold_tokens.1.x_hbm
  126.9 1.6 copy-done.2
  128.5 0.8 unfold_cotangent.1
  129.3 1.5 copy-done
  130.8 0.7 copy-done.7
  131.5 0.7 copy-done.8
  132.1 4.8 %all-to-all-done.2 = bf16[16,48,128]{2,1,0:T(8,128)(2,1)S(1)} async-done(((bf16[16,48,128]{2,1,0:T(8,128)(2,1)}), bf16[16,48,128]{2,1,0:T(8,128)(2,1)S(1)}, u32[]{:S(2)}, u32[]{:S(2)}) %all-to-all-start.2) | async-done | bytes 196640 | tf_op jit(solution)/shard_map/all_to_all | solution.py:368
  137.0 14.1 %all-gather.2.cloned.1.call-done.w_hbm = bf16[4096,2432]{1,0:T(8,128)(2,1)} async-done(((bf16[256,2432]{1,0:T(8,128)(2,1)}), bf16[4096,2432]{1,0:T(8,128)(2,1)}) %all-gather.2.cloned.1.call-update) | async-done | bytes 19922960 | tf_op jit(solution)/shard_map/all_gather | solution.py:342
  151.1 17.4 %expert.1 = (bf16[256,5248]{1,0:T(8,128)(2,1)}, bf16[320,768]{1,0:T(8,128)(2,1)}, bf16[320,128]{1,0:T(8,128)(2,1)}, bf16[320,128]{1,0:T(8,128)(2,1)}) custom-call(bf16[320,4096]{1,0:T(8,128)(2,1)} %copy-done.2, bf16[320,4096]{1,0:T(8,128)(2,1)} %copy-done, bf16[4096,2432]{1,0:T(8,128)(2,1)} %all-gather.2.cloned.1.call-done.w_hbm, bf16[768,128]{1,0:T(8,128)(2,1)} %bitcast.55, ...), custom_call_target="tpu_custom_call" | custom-call | tf_op jit(solution)/shard_map/expert/pallas_call | solution.py:397
  168.5 6.7 %all-to-all-start.3 = ((bf16[16,16,5248]{2,1,0:T(8,128)(2,1)}), bf16[16,16,5248]{2,1,0:T(8,128)(2,1)S(1)}, u32[]{:S(2)}, u32[]{:S(2)}) async-start(bf16[16,16,5248]{2,1,0:T(8,128)(2,1)} %bitcast.54), calls=%async_computation.3 | async-start | bytes 5373952 | tf_op jit(solution)/shard_map/all_to_all | solution.py:363
  175.3 1.7 copy-done.1
  177.0 2.8 %adapters.1 = (bf16[8,160,256]{2,1,0:T(8,128)(2,1)S(1)}, bf16[8,160,256]{2,1,0:T(8,128)(2,1)S(1)}) custom-call(s32[2]{0:T(128)S(1)} %pad_add_fusion.where_ref, bf16[320,768]{1,0:T(8,128)(2,1)S(1)} %copy-done.6, bf16[320,128]{1,0:T(8,128)(2,1)S(1)} %copy-done.9, bf16[320,128]{1,0:T(8,128)(2,1)S(1)} %copy-done.10, bf16[320,4096]{1,0:T(8,128)(2,1)S(1)} %copy-done.1), custom_call_target="tpu_custom_call" | custom-call | flops 400000000 | bytes 6000000 | tf_op jit(solution)/shard_map/adapters/pallas_call | solution.py:429
  179.8 0.8 collective-permute-start
  180.7 1.7 collective-permute-done
  182.6 1.2 collective-permute-start.7
  183.8 1.9 collective-permute-start.6
  185.7 2.0 collective-permute-start.5
  187.7 2.6 %collective-permute-start.4 = (bf16[160,256]{1,0:T(8,128)(2,1)S(1)}, bf16[160,256]{1,0:T(8,128)(2,1)S(1)}, u32[]{:S(2)}, u32[]{:S(2)}) collective-permute-start(bf16[160,256]{1,0:T(8,128)(2,1)S(1)} %get-tuple-element.40), channel_id=1, source_target_pairs={{0,128},{16,144},{32,160},{48,176},{64,192},{80,208},{96,224},{112... | collective-permute-start | bytes 245768 | tf_op jit(solution)/shard_map/ppermute | solution.py:451
  190.9 3.6 %collective-permute-start.2 = (bf16[160,256]{1,0:T(8,128)(2,1)S(1)}, bf16[160,256]{1,0:T(8,128)(2,1)S(1)}, u32[]{:S(2)}, u32[]{:S(2)}) collective-permute-start(bf16[160,256]{1,0:T(8,128)(2,1)S(1)} %get-tuple-element.42), channel_id=1, source_target_pairs={{0,64},{16,80},{32,96},{48,112},{64,128},{80,144},{96,160},{112,17... | collective-permute-start | bytes 245768 | tf_op jit(solution)/shard_map/ppermute | solution.py:451
  194.5 1.6 collective-permute-done.4
  196.1 7.4 %collective-permute-done.3 = bf16[160,256]{1,0:T(8,128)(2,1)S(1)} collective-permute-done((bf16[160,256]{1,0:T(8,128)(2,1)S(1)}, bf16[160,256]{1,0:T(8,128)(2,1)S(1)}, u32[]{:S(2)}, u32[]{:S(2)}) %collective-permute-start.3) | collective-permute-done | bytes 81952 | tf_op jit(solution)/shard_map/ppermute | solution.py:451
  203.5 3.7 %collective-permute-done.1 = bf16[160,256]{1,0:T(8,128)(2,1)S(1)} collective-permute-done((bf16[160,256]{1,0:T(8,128)(2,1)S(1)}, bf16[160,256]{1,0:T(8,128)(2,1)S(1)}, u32[]{:S(2)}, u32[]{:S(2)}) %collective-permute-start.1) | collective-permute-done | bytes 81952 | tf_op jit(solution)/shard_map/ppermute | solution.py:451
  208.0 0.7 slice_bitcast_fusion.1
  208.6 7.6 %all-to-all-done.3 = bf16[16,16,5248]{2,1,0:T(8,128)(2,1)S(1)} async-done(((bf16[16,16,5248]{2,1,0:T(8,128)(2,1)}), bf16[16,16,5248]{2,1,0:T(8,128)(2,1)S(1)}, u32[]{:S(2)}, u32[]{:S(2)}) %all-to-all-start.3) | async-done | bytes 2687008 | tf_op jit(solution)/shard_map/all_to_all | solution.py:363
  216.2 2.1 shard_map.130
  (44 shorter events, 2.7 us)
Async XLA Ops:
  7.2 25.1 %copy-start.13 = (s32[128,2]{0,1:T(2,128)S(1)}, s32[128,2]{0,1:T(2,128)}, u32[]{:S(2)}) copy-start(s32[128,2]{0,1:T(2,128)} %param.12) | copy-start | bytes 3076
  7.2 25.2 %copy-start.14 = (bf16[128,2]{0,1:T(2,128)(2,1)S(1)}, bf16[128,2]{0,1:T(2,128)(2,1)}, u32[]{:S(2)}) copy-start(bf16[128,2]{0,1:T(2,128)(2,1)} %param.13) | copy-start | bytes 1540
  7.2 25.3 %copy-start.15 = (s32[128]{0:T(128)S(1)}, s32[128]{0:T(128)}, u32[]{:S(2)}) copy-start(s32[128]{0:T(128)} %param.14) | copy-start | bytes 1540
  7.2 25.5 %copy-start.4 = (bf16[128,4096]{1,0:T(8,128)(2,1)S(1)}, bf16[128,4096]{1,0:T(8,128)(2,1)}, u32[]{:S(2)}) copy-start(bf16[128,4096]{1,0:T(8,128)(2,1)} %refs_3_.1) | copy-start | bytes 3145732
  7.2 25.4 %copy-start.5 = (bf16[128,4096]{1,0:T(8,128)(2,1)S(1)}, bf16[128,4096]{1,0:T(8,128)(2,1)}, u32[]{:S(2)}) copy-start(bf16[128,4096]{1,0:T(8,128)(2,1)} %refs_4_.1) | copy-start | bytes 3145732
  7.2 143.8 %all-gather.2.cloned.1.call-start = ((), (), s32[]{:S(2)}) async-start(), calls=%async_computation.4 | async-start | bytes 21168128 | tf_op jit(solution)/shard_map/all_gather | solution.py:342
  76.0 36.5 %copy-start.12 = (bf16[1,48,128]{2,1,0:T(8,128)(2,1)S(1)}, bf16[1,48,128]{2,1,0:T(8,128)(2,1)}, u32[]{:S(2)}) copy-start(bf16[1,48,128]{2,1,0:T(8,128)(2,1)} %param.18) | copy-start | bytes 36868
  113.2 23.8 %all-to-all-start.2 = ((bf16[16,48,128]{2,1,0:T(8,128)(2,1)}), bf16[16,48,128]{2,1,0:T(8,128)(2,1)S(1)}, u32[]{:S(2)}, u32[]{:S(2)}) async-start(bf16[16,48,128]{2,1,0:T(8,128)(2,1)} %broadcast_in_dim.14), calls=%async_computation.2 | async-start | bytes 393216 | tf_op jit(solution)/shard_map/all_to_all | solution.py:368
  124.4 1.9 copy-start.3
  126.9 1.6 copy-start.2
  129.3 1.5 copy-start
  130.8 0.7 copy-start.7
  131.5 0.7 copy-start.8
  137.0 14.1 %copy-start.11 = (bf16[16,48,128]{2,1,0:T(8,128)(2,1)}, bf16[16,48,128]{2,1,0:T(8,128)(2,1)S(1)}, u32[]{:S(2)}) copy-start(bf16[16,48,128]{2,1,0:T(8,128)(2,1)S(1)} %all-to-all-done.2) | copy-start | bytes 589828
  168.4 6.8 %copy-start.6 = (bf16[320,768]{1,0:T(8,128)(2,1)S(1)}, bf16[320,768]{1,0:T(8,128)(2,1)}, u32[]{:S(2)}) copy-start(bf16[320,768]{1,0:T(8,128)(2,1)} %get-tuple-element.25.hid_ref) | copy-start | bytes 1474564
  168.4 6.8 %copy-start.9 = (bf16[320,128]{1,0:T(8,128)(2,1)S(1)}, bf16[320,128]{1,0:T(8,128)(2,1)}, u32[]{:S(2)}) copy-start(bf16[320,128]{1,0:T(8,128)(2,1)} %get-tuple-element.26.low_grad_ref) | copy-start | bytes 245764
  168.5 6.8 %copy-start.10 = (bf16[320,128]{1,0:T(8,128)(2,1)S(1)}, bf16[320,128]{1,0:T(8,128)(2,1)}, u32[]{:S(2)}) copy-start(bf16[320,128]{1,0:T(8,128)(2,1)} %get-tuple-element.27.lowt_ref) | copy-start | bytes 245764
  168.5 47.8 %all-to-all-start.3 = ((bf16[16,16,5248]{2,1,0:T(8,128)(2,1)}), bf16[16,16,5248]{2,1,0:T(8,128)(2,1)S(1)}, u32[]{:S(2)}, u32[]{:S(2)}) async-start(bf16[16,16,5248]{2,1,0:T(8,128)(2,1)} %bitcast.54), calls=%async_computation.3 | async-start | bytes 5373952 | tf_op jit(solution)/shard_map/all_to_all | solution.py:363
  175.3 1.7 copy-start.1
  179.8 2.6 %collective-permute-start = (bf16[8,160,256]{2,1,0:T(8,128)(2,1)S(1)}, bf16[8,160,256]{2,1,0:T(8,128)(2,1)S(1)}, u32[]{:S(2)}, u32[]{:S(2)}) collective-permute-start(bf16[8,160,256]{2,1,0:T(8,128)(2,1)S(1)} %get-tuple-element.29), channel_id=1, source_target_pairs={{0,16},{16,0},{32,48},{48,32},{64,80},{80,64},{96,112},{112,96},{1... | collective-permute-start | bytes 1966088 | tf_op jit(solution)/shard_map/ppermute | solution.py:446
  182.6 8.2 %collective-permute-start.7 = (bf16[160,256]{1,0:T(8,128)(2,1)S(1)}, bf16[160,256]{1,0:T(8,128)(2,1)S(1)}, u32[]{:S(2)}, u32[]{:S(2)}) collective-permute-start(bf16[160,256]{1,0:T(8,128)(2,1)S(1)} %get-tuple-element.37), channel_id=1, source_target_pairs={{0,224},{16,240},{32,0},{48,16},{64,32},{80,48},{96,64},{112,80},{... | collective-permute-start | bytes 245768 | tf_op jit(solution)/shard_map/ppermute | solution.py:451
  183.8 10.6 %collective-permute-start.6 = (bf16[160,256]{1,0:T(8,128)(2,1)S(1)}, bf16[160,256]{1,0:T(8,128)(2,1)S(1)}, u32[]{:S(2)}, u32[]{:S(2)}) collective-permute-start(bf16[160,256]{1,0:T(8,128)(2,1)S(1)} %get-tuple-element.38), channel_id=1, source_target_pairs={{0,192},{16,208},{32,224},{48,240},{64,0},{80,16},{96,32},{112,48}... | collective-permute-start | bytes 245768 | tf_op jit(solution)/shard_map/ppermute | solution.py:451
  185.7 8.8 %collective-permute-start.5 = (bf16[160,256]{1,0:T(8,128)(2,1)S(1)}, bf16[160,256]{1,0:T(8,128)(2,1)S(1)}, u32[]{:S(2)}, u32[]{:S(2)}) collective-permute-start(bf16[160,256]{1,0:T(8,128)(2,1)S(1)} %get-tuple-element.39), channel_id=1, source_target_pairs={{0,160},{16,176},{32,192},{48,208},{64,224},{80,240},{96,0},{112,1... | collective-permute-start | bytes 245768 | tf_op jit(solution)/shard_map/ppermute | solution.py:451
  187.7 8.4 %collective-permute-start.4 = (bf16[160,256]{1,0:T(8,128)(2,1)S(1)}, bf16[160,256]{1,0:T(8,128)(2,1)S(1)}, u32[]{:S(2)}, u32[]{:S(2)}) collective-permute-start(bf16[160,256]{1,0:T(8,128)(2,1)S(1)} %get-tuple-element.40), channel_id=1, source_target_pairs={{0,128},{16,144},{32,160},{48,176},{64,192},{80,208},{96,224},{112... | collective-permute-start | bytes 245768 | tf_op jit(solution)/shard_map/ppermute | solution.py:451
  190.3 13.2 %collective-permute-start.3 = (bf16[160,256]{1,0:T(8,128)(2,1)S(1)}, bf16[160,256]{1,0:T(8,128)(2,1)S(1)}, u32[]{:S(2)}, u32[]{:S(2)}) collective-permute-start(bf16[160,256]{1,0:T(8,128)(2,1)S(1)} %get-tuple-element.41), channel_id=1, source_target_pairs={{0,96},{16,112},{32,128},{48,144},{64,160},{80,176},{96,192},{112,... | collective-permute-start | bytes 245768 | tf_op jit(solution)/shard_map/ppermute | solution.py:451
  190.9 12.6 %collective-permute-start.2 = (bf16[160,256]{1,0:T(8,128)(2,1)S(1)}, bf16[160,256]{1,0:T(8,128)(2,1)S(1)}, u32[]{:S(2)}, u32[]{:S(2)}) collective-permute-start(bf16[160,256]{1,0:T(8,128)(2,1)S(1)} %get-tuple-element.42), channel_id=1, source_target_pairs={{0,64},{16,80},{32,96},{48,112},{64,128},{80,144},{96,160},{112,17... | collective-permute-start | bytes 245768 | tf_op jit(solution)/shard_map/ppermute | solution.py:451
  194.4 12.8 %collective-permute-start.1 = (bf16[160,256]{1,0:T(8,128)(2,1)S(1)}, bf16[160,256]{1,0:T(8,128)(2,1)S(1)}, u32[]{:S(2)}, u32[]{:S(2)}) collective-permute-start(bf16[160,256]{1,0:T(8,128)(2,1)S(1)} %get-tuple-element.36), channel_id=1, source_target_pairs={{0,32},{16,48},{32,64},{48,80},{64,96},{80,112},{96,128},{112,144}... | collective-permute-start | bytes 245768 | tf_op jit(solution)/shard_map/ppermute | solution.py:451
Sparse Core Ops, SparseCore 0:
  32.4 118.6 all-gather.1

commit v2 on v1

--- a/solution.py
+++ b/solution.py
@@ -55,24 +55,33 @@
     return (iota((place.shape[0], slots), 1) == place).astype(f32).astype(bf16)
 
 
-def pack_kernel(gate_hbm, up_hbm, down_hbm, second_hbm, out_hbm, down, second, turned, sems):
+def pack_kernel(gate_hbm, up_hbm, down_hbm, second_hbm, out_hbm, down, second, held, sems):
     half = gate_hbm.shape[1]
     cols = out_hbm.shape[1]
-    load_down = pltpu.make_async_copy(down_hbm, down, sems.at[0])
-    load_second = pltpu.make_async_copy(second_hbm, second, sems.at[1])
-    gate = pltpu.make_async_copy(gate_hbm, out_hbm.at[:, pl.ds(0, half)], sems.at[2])
-    up = pltpu.make_async_copy(up_hbm, out_hbm.at[:, pl.ds(half, half)], sems.at[3])
-    store = pltpu.make_async_copy(turned, out_hbm.at[:, pl.ds(2 * half, cols - 2 * half)], sems.at[4])
-    for copy in (load_down, load_second, gate, up):
+    spans = (pl.ds(0, half), pl.ds(half, half), pl.ds(2 * half, cols - 2 * half))
+    loads = [
+        pltpu.make_async_copy(down_hbm, down, sems.at[0]),
+        pltpu.make_async_copy(second_hbm, second, sems.at[1]),
+        pltpu.make_async_copy(gate_hbm, held.at[:, spans[0]], sems.at[2]),
+        pltpu.make_async_copy(up_hbm, held.at[:, spans[1]], sems.at[3]),
+    ]
+    stores = [
+        pltpu.make_async_copy(held.at[:, span], out_hbm.at[:, span], sems.at[4 + a])
+        for a, span in enumerate(spans)
+    ]
+    for copy in loads:
         copy.start()
-    load_down.wait()
-    turned[:, :half] = down[...].T
-    load_second.wait()
-    turned[:, half:] = second[...].T
-    store.start()
-    gate.wait()
-    up.wait()
-    store.wait()
+    loads[0].wait()
+    held[:, 2 * half : 3 * half] = down[...].T
+    loads[1].wait()
+    held[:, 3 * half :] = second[...].T
+    stores[2].start()
+    loads[2].wait()
+    stores[0].start()
+    loads[3].wait()
+    stores[1].start()
+    for copy in stores:
+        copy.wait()
 
 
 def dispatch_kernel(ids_ref, gate_ref, tenant_ref, tok_ref, cot_ref, x_ref, c_ref, experts):
@@ -329,8 +338,8 @@
         scratch_shapes=[
             pltpu.VMEM((half, shard), bf16),
             pltpu.VMEM((ranks, shard), bf16),
-            pltpu.VMEM((shard, half + ranks), bf16),
-            pltpu.SemaphoreType.DMA((5,)),
+            pltpu.VMEM((shard, cols), bf16),
+            pltpu.SemaphoreType.DMA((7,)),
         ],
         compiler_params=pltpu.CompilerParams(vmem_limit_bytes=60 << 20),
     )(
@@ -364,7 +373,6 @@
             rows_2d.shape
         )
 
-    x_rows, c_rows = exchange(x_send), exchange(c_send)
     first_full = lax.all_to_all(
         jnp.broadcast_to(adapter_first_factors, (spread,) + adapter_first_factors.shape[1:]),
         "fsdp",
@@ -372,6 +380,8 @@
         concat_axis=0,
         tiled=True,
     ).reshape(half, ranks)
+    x_send, c_send, first_full = lax.optimization_barrier((x_send, c_send, first_full))
+    x_rows, c_rows = exchange(x_send), exchange(c_send)
 
     x_all = pl.pallas_call(
         unfold_rows,

time: 226 us -> 200 us (0.88)
  blocking collectives: 76.9 us -> 40.9 us
  waiting for transfers between devices: 41.1 us -> 66.8 us
  Pallas kernels: 51.6 us -> 29 us
  local copies, waits for them, and re-layouts: 10.4 us -> 14.4 us
  starting transfers between devices: 30.6 us -> 33.2 us
    all_to_all x2 -> x1, blocking collectives: 76.9 us -> 40.9 us  [exchange(): lax.all_to_all(block, 'expert', split_axis=0, concat_axis=0, tiled=True)]
    all_to_all x1 -> x2, waiting for transfers between devices: 7.6 us -> 43.1 us  [exchange(): lax.all_to_all(block, 'expert', split_axis=0, concat_axis=0, tiled=True)]
    pallas_call x1, Pallas kernels: 25 us -> 2.39 us  [shards(): pl.pallas_call(pack_kernel, name='pack_weights', out_shape=jax.ShapeDtype...]
    all_gather x1, waiting for transfers between devices: 14.1 us -> 6.12 us  [shards(): weights = lax.all_gather(packed, 'fsdp', axis=0, tiled=True)]
    all_to_all x1 -> x2, starting transfers between devices: 6.71 us -> 10.8 us  [exchange(): lax.all_to_all(block, 'expert', split_axis=0, concat_axis=0, tiled=True)]
    unnamed x35 -> x39, local copies, waits for them, and re-layouts: 8.88 us -> 12.9 us
  transfers between devices with their start and end apart: 11 -> 12, of which waited for: 7 -> 8; matrix products, arithmetic and copies ran while one was open for 1% -> 1% of each run, Pallas kernels for 3% -> 4%
where the time goes in v2:
time: 200 us
  waiting for transfers between devices  66.8 us (33%)
  blocking collectives  40.9 us (20%)
  starting transfers between devices  33.2 us (17%)
  Pallas kernels  29 us (14%)
  local copies, waits for them, and re-layouts  14.4 us (7%)
  between operations  14.3 us (7%)
    all_to_all x2, waiting for transfers between devices, exchange(): lax.all_to_all(block, 'expert', split_axis=0, concat_axis=0, tiled=True)  43.1 us
    all_to_all x1, blocking collectives, exchange(): lax.all_to_all(block, 'expert', split_axis=0, concat_axis=0, tiled=True)  40.9 us
    pallas_call x1, Pallas kernels, shards(): pl.pallas_call(expert_kernel, name='expert', out_shape=(jax.ShapeDtypeStr...  17.4 us
    unnamed x39, local copies, waits for them, and re-layouts  12.9 us
    ppermute x7, waiting for transfers between devices, shards(): total = total + lax.ppermute(halved[dz], 'fsdp', moves).astype(f32)  12.8 us
    ppermute x7, starting transfers between devices, shards(): total = total + lax.ppermute(halved[dz], 'fsdp', moves).astype(f32)  11.6 us
    all_to_all x2, starting transfers between devices, exchange(): lax.all_to_all(block, 'expert', split_axis=0, concat_axis=0, tiled=True)  10.8 us
    all_to_all x1, starting transfers between devices, shards(): lax.all_to_all(jnp.broadcast_to(adapter_first_factors, (spread,) + adapte...  9.98 us
  transfers between devices with their start and end apart: 12, of which 8 were waited for; matrix products, arithmetic and copies ran while one was open for 1% of the time, Pallas kernels for 4%

profile of v2, /device:TPU:1, one launch (start us, length us, event | category | flops | bytes accessed | tf_op | source)
XLA Modules:
  0.0 199.5 jit_solution(18115162866230637728)
XLA Ops:
  7.3 2.4 %pack_weights.1 = bf16[256,2432]{1,0:T(8,128)(2,1)} custom-call(bf16[256,768]{1,0:T(8,128)(2,1)} %bitcast.56, bf16[256,768]{1,0:T(8,128)(2,1)} %bitcast.57, bf16[768,256]{1,0:T(8,128)(2,1)} %bitcast.58, bf16[128,256]{1,0:T(8,128)(2,1)} %bitcast.59), custom_call_target="tpu_custom_call" | custom-call | tf_op jit(solution)/shard_map/pack_weights/pallas_call | solution.py:332
  9.7 0.7 broadcast_in_dim.14
  10.4 10.0 %all-to-all-start = ((bf16[16,48,128]{2,1,0:T(8,128)(2,1)}), bf16[16,48,128]{2,1,0:T(8,128)(2,1)S(1)}, u32[]{:S(2)}, u32[]{:S(2)}) async-start(bf16[16,48,128]{2,1,0:T(8,128)(2,1)} %broadcast_in_dim.14), calls=%async_computation | async-start | bytes 393216 | tf_op jit(solution)/shard_map/all_to_all | solution.py:376
  20.8 1.2 copy-done.6
  22.0 1.2 copy-done.7
  23.2 2.9 %shard_map.129 = (bf16[256,5120]{1,0:T(8,128)(2,1)S(1)}, bf16[256,5248]{1,0:T(8,128)(2,1)S(1)}) custom-call(s32[128,2]{1,0:T(8,128)S(1)} %copy.17.refs_0_, bf16[128,2]{1,0:T(8,128)(2,1)S(1)} %copy.15.refs_1_, s32[128,1]{1,0:T(8,128)S(1)} %copy.16.refs_2_, bf16[128,4096]{1,0:T(8,128)(2,1)S(1)} %copy-done.6, bf16[128,4096]{1,0:T(8,128)(2,1)S(1)} %copy-done.7), custom_call_target="tpu_custom_call" | custom-call | tf_op jit(solution)/shard_map/pallas_call | solution.py:353
  26.1 1.5 copy-done.5
  27.6 3.1 %all-to-all-done = bf16[16,48,128]{2,1,0:T(8,128)(2,1)S(1)} async-done(((bf16[16,48,128]{2,1,0:T(8,128)(2,1)}), bf16[16,48,128]{2,1,0:T(8,128)(2,1)S(1)}, u32[]{:S(2)}, u32[]{:S(2)}) %all-to-all-start) | async-done | bytes 196640 | tf_op jit(solution)/shard_map/all_to_all | solution.py:376
  30.7 40.9 %all_to_all.20 = bf16[16,16,5120]{2,1,0:T(8,128)(2,1)} all-to-all(bf16[16,16,5120]{2,1,0:T(8,128)(2,1)} %bitcast.53), channel_id=1, replica_groups=mesh['fsdp'=16,'expert'=16] {'expert'}, dimensions={0} | all-to-all | bytes 5242880 | tf_op jit(solution)/shard_map/all_to_all | solution.py:372
  71.6 3.9 %all-to-all-start.2 = ((bf16[16,16,5248]{2,1,0:T(8,128)(2,1)}), bf16[16,16,5248]{2,1,0:T(8,128)(2,1)S(1)}, u32[]{:S(2)}, u32[]{:S(2)}) async-start(bf16[16,16,5248]{2,1,0:T(8,128)(2,1)} %bitcast.52), calls=%async_computation.2 | async-start | bytes 5373952 | tf_op jit(solution)/shard_map/all_to_all | solution.py:372
  75.6 1.9 copy-done.3
  77.4 0.7 unfold_tokens.1.x_hbm
  78.1 1.5 copy-done.2
  79.6 35.2 %all-to-all-done.2 = bf16[16,16,5248]{2,1,0:T(8,128)(2,1)S(1)} async-done(((bf16[16,16,5248]{2,1,0:T(8,128)(2,1)}), bf16[16,16,5248]{2,1,0:T(8,128)(2,1)S(1)}, u32[]{:S(2)}, u32[]{:S(2)}) %all-to-all-start.2) | async-done | bytes 2687008 | tf_op jit(solution)/shard_map/all_to_all | solution.py:372
  114.8 0.8 unfold_cotangent.1
  115.6 1.6 copy-done
  118.5 6.1 %all-gather.2.cloned.1.call-done.w_hbm = bf16[4096,2432]{1,0:T(8,128)(2,1)} async-done(((bf16[256,2432]{1,0:T(8,128)(2,1)}), bf16[4096,2432]{1,0:T(8,128)(2,1)}) %all-gather.2.cloned.1.call-update) | async-done | bytes 19922960 | tf_op jit(solution)/shard_map/all_gather | solution.py:351
  124.7 17.4 %expert.1 = (bf16[256,5248]{1,0:T(8,128)(2,1)}, bf16[320,768]{1,0:T(8,128)(2,1)}, bf16[320,128]{1,0:T(8,128)(2,1)}, bf16[320,128]{1,0:T(8,128)(2,1)}) custom-call(bf16[320,4096]{1,0:T(8,128)(2,1)} %copy-done.2, bf16[320,4096]{1,0:T(8,128)(2,1)} %copy-done, bf16[4096,2432]{1,0:T(8,128)(2,1)} %all-gather.2.cloned.1.call-done.w_hbm, bf16[768,128]{1,0:T(8,128)(2,1)} %bitcast.55, ...), custom_call_target="tpu_custom_call" | custom-call | tf_op jit(solution)/shard_map/expert/pallas_call | solution.py:407
  142.1 6.9 %all-to-all-start.3 = ((bf16[16,16,5248]{2,1,0:T(8,128)(2,1)}), bf16[16,16,5248]{2,1,0:T(8,128)(2,1)S(1)}, u32[]{:S(2)}, u32[]{:S(2)}) async-start(bf16[16,16,5248]{2,1,0:T(8,128)(2,1)} %bitcast.54), calls=%async_computation.3 | async-start | bytes 5373952 | tf_op jit(solution)/shard_map/all_to_all | solution.py:372
  149.1 1.7 copy-done.1
  150.8 2.8 %adapters.1 = (bf16[8,160,256]{2,1,0:T(8,128)(2,1)S(1)}, bf16[8,160,256]{2,1,0:T(8,128)(2,1)S(1)}) custom-call(s32[2]{0:T(128)S(1)} %pad_add_fusion.where_ref, bf16[320,768]{1,0:T(8,128)(2,1)S(1)} %copy-done.8, bf16[320,128]{1,0:T(8,128)(2,1)S(1)} %copy-done.11, bf16[320,128]{1,0:T(8,128)(2,1)S(1)} %copy-done.12, bf16[320,4096]{1,0:T(8,128)(2,1)S(1)} %copy-done.1), custom_call_target="tpu_custom_call" | custom-call | flops 400000000 | bytes 6000000 | tf_op jit(solution)/shard_map/adapters/pallas_call | solution.py:439
  153.6 0.8 collective-permute-start
  154.4 1.7 collective-permute-done
  156.4 1.1 collective-permute-start.7
  157.5 1.7 collective-permute-start.6
  159.2 2.0 collective-permute-start.5
  161.2 2.9 %collective-permute-start.4 = (bf16[160,256]{1,0:T(8,128)(2,1)S(1)}, bf16[160,256]{1,0:T(8,128)(2,1)S(1)}, u32[]{:S(2)}, u32[]{:S(2)}) collective-permute-start(bf16[160,256]{1,0:T(8,128)(2,1)S(1)} %get-tuple-element.46), channel_id=1, source_target_pairs={{0,128},{16,144},{32,160},{48,176},{64,192},{80,208},{96,224},{112... | collective-permute-start | bytes 245768 | tf_op jit(solution)/shard_map/ppermute | solution.py:461
  164.4 3.6 %collective-permute-start.2 = (bf16[160,256]{1,0:T(8,128)(2,1)S(1)}, bf16[160,256]{1,0:T(8,128)(2,1)S(1)}, u32[]{:S(2)}, u32[]{:S(2)}) collective-permute-start(bf16[160,256]{1,0:T(8,128)(2,1)S(1)} %get-tuple-element.48), channel_id=1, source_target_pairs={{0,64},{16,80},{32,96},{48,112},{64,128},{80,144},{96,160},{112,17... | collective-permute-start | bytes 245768 | tf_op jit(solution)/shard_map/ppermute | solution.py:461
  168.6 8.5 %collective-permute-done.3 = bf16[160,256]{1,0:T(8,128)(2,1)S(1)} collective-permute-done((bf16[160,256]{1,0:T(8,128)(2,1)S(1)}, bf16[160,256]{1,0:T(8,128)(2,1)S(1)}, u32[]{:S(2)}, u32[]{:S(2)}) %collective-permute-start.3) | collective-permute-done | bytes 81952 | tf_op jit(solution)/shard_map/ppermute | solution.py:461
  177.0 3.7 %collective-permute-done.1 = bf16[160,256]{1,0:T(8,128)(2,1)S(1)} collective-permute-done((bf16[160,256]{1,0:T(8,128)(2,1)S(1)}, bf16[160,256]{1,0:T(8,128)(2,1)S(1)}, u32[]{:S(2)}, u32[]{:S(2)}) %collective-permute-start.1) | collective-permute-done | bytes 81952 | tf_op jit(solution)/shard_map/ppermute | solution.py:461
  182.1 7.9 %all-to-all-done.3 = bf16[16,16,5248]{2,1,0:T(8,128)(2,1)S(1)} async-done(((bf16[16,16,5248]{2,1,0:T(8,128)(2,1)}), bf16[16,16,5248]{2,1,0:T(8,128)(2,1)S(1)}, u32[]{:S(2)}, u32[]{:S(2)}) %all-to-all-start.3) | async-done | bytes 2687008 | tf_op jit(solution)/shard_map/all_to_all | solution.py:372
  190.0 2.1 %shard_map.130 = (bf16[128,4096]{1,0:T(8,128)(2,1)}, bf16[128,2]{1,0:T(8,128)(2,1)S(1)}) custom-call(s32[128,2]{1,0:T(8,128)S(1)} %copy.17.refs_0_, bf16[256,5248]{1,0:T(8,128)(2,1)S(1)} %bitcast.49), custom_call_target="tpu_custom_call" | custom-call | tf_op jit(solution)/shard_map/pallas_call | solution.py:472
  (49 shorter events, 5.0 us)
Async XLA Ops:
  7.2 2.5 %copy-start.14 = (bf16[1,48,128]{2,1,0:T(8,128)(2,1)S(1)}, bf16[1,48,128]{2,1,0:T(8,128)(2,1)}, u32[]{:S(2)}) copy-start(bf16[1,48,128]{2,1,0:T(8,128)(2,1)} %param.18) | copy-start | bytes 36868
  7.2 13.2 %copy-start.15 = (s32[128,2]{0,1:T(2,128)S(1)}, s32[128,2]{0,1:T(2,128)}, u32[]{:S(2)}) copy-start(s32[128,2]{0,1:T(2,128)} %param.12) | copy-start | bytes 3076
  7.2 13.3 %copy-start.16 = (bf16[128,2]{0,1:T(2,128)(2,1)S(1)}, bf16[128,2]{0,1:T(2,128)(2,1)}, u32[]{:S(2)}) copy-start(bf16[128,2]{0,1:T(2,128)(2,1)} %param.13) | copy-start | bytes 1540
  7.2 13.4 %copy-start.17 = (s32[128]{0:T(128)S(1)}, s32[128]{0:T(128)}, u32[]{:S(2)}) copy-start(s32[128]{0:T(128)} %param.14) | copy-start | bytes 1540
  7.2 117.4 %all-gather.2.cloned.1.call-start = ((), (), s32[]{:S(2)}) async-start(), calls=%async_computation.4 | async-start | bytes 21168128 | tf_op jit(solution)/shard_map/all_gather | solution.py:351
  10.4 20.3 %all-to-all-start = ((bf16[16,48,128]{2,1,0:T(8,128)(2,1)}), bf16[16,48,128]{2,1,0:T(8,128)(2,1)S(1)}, u32[]{:S(2)}, u32[]{:S(2)}) async-start(bf16[16,48,128]{2,1,0:T(8,128)(2,1)} %broadcast_in_dim.14), calls=%async_computation | async-start | bytes 393216 | tf_op jit(solution)/shard_map/all_to_all | solution.py:376
  20.7 1.2 copy-start.6
  22.0 1.2 copy-start.7
  26.1 1.5 copy-start.5
  27.6 44.0 %copy-start.4 = (bf16[256,5248]{1,0:T(8,128)(2,1)}, bf16[256,5248]{1,0:T(8,128)(2,1)S(1)}, u32[]{:S(2)}) copy-start(bf16[256,5248]{1,0:T(8,128)(2,1)S(1)} %get-tuple-element.23) | copy-start | bytes 8060932
  30.7 40.9 %copy-start.13 = (bf16[16,48,128]{2,1,0:T(8,128)(2,1)}, bf16[16,48,128]{2,1,0:T(8,128)(2,1)S(1)}, u32[]{:S(2)}) copy-start(bf16[16,48,128]{2,1,0:T(8,128)(2,1)S(1)} %all-to-all-done) | copy-start | bytes 589828
  71.6 43.2 %all-to-all-start.2 = ((bf16[16,16,5248]{2,1,0:T(8,128)(2,1)}), bf16[16,16,5248]{2,1,0:T(8,128)(2,1)S(1)}, u32[]{:S(2)}, u32[]{:S(2)}) async-start(bf16[16,16,5248]{2,1,0:T(8,128)(2,1)} %bitcast.52), calls=%async_computation.2 | async-start | bytes 5373952 | tf_op jit(solution)/shard_map/all_to_all | solution.py:372
  75.5 1.9 copy-start.3
  78.1 1.5 copy-start.2
  115.6 1.6 copy-start
  117.2 0.7 copy-start.9
  117.9 0.7 copy-start.10
  142.0 7.0 %copy-start.8 = (bf16[320,768]{1,0:T(8,128)(2,1)S(1)}, bf16[320,768]{1,0:T(8,128)(2,1)}, u32[]{:S(2)}) copy-start(bf16[320,768]{1,0:T(8,128)(2,1)} %get-tuple-element.31.hid_ref) | copy-start | bytes 1474564
  142.0 7.0 %copy-start.11 = (bf16[320,128]{1,0:T(8,128)(2,1)S(1)}, bf16[320,128]{1,0:T(8,128)(2,1)}, u32[]{:S(2)}) copy-start(bf16[320,128]{1,0:T(8,128)(2,1)} %get-tuple-element.32.low_grad_ref) | copy-start | bytes 245764
  142.0 7.0 %copy-start.12 = (bf16[320,128]{1,0:T(8,128)(2,1)S(1)}, bf16[320,128]{1,0:T(8,128)(2,1)}, u32[]{:S(2)}) copy-start(bf16[320,128]{1,0:T(8,128)(2,1)} %get-tuple-element.33.lowt_ref) | copy-start | bytes 245764
  142.1 47.9 %all-to-all-start.3 = ((bf16[16,16,5248]{2,1,0:T(8,128)(2,1)}), bf16[16,16,5248]{2,1,0:T(8,128)(2,1)S(1)}, u32[]{:S(2)}, u32[]{:S(2)}) async-start(bf16[16,16,5248]{2,1,0:T(8,128)(2,1)} %bitcast.54), calls=%async_computation.3 | async-start | bytes 5373952 | tf_op jit(solution)/shard_map/all_to_all | solution.py:372
  149.0 1.7 copy-start.1
  153.6 2.6 %collective-permute-start = (bf16[8,160,256]{2,1,0:T(8,128)(2,1)S(1)}, bf16[8,160,256]{2,1,0:T(8,128)(2,1)S(1)}, u32[]{:S(2)}, u32[]{:S(2)}) collective-permute-start(bf16[8,160,256]{2,1,0:T(8,128)(2,1)S(1)} %get-tuple-element.35), channel_id=1, source_target_pairs={{0,16},{16,0},{32,48},{48,32},{64,80},{80,64},{96,112},{112,96},{1... | collective-permute-start | bytes 1966088 | tf_op jit(solution)/shard_map/ppermute | solution.py:456
  156.4 8.0 %collective-permute-start.7 = (bf16[160,256]{1,0:T(8,128)(2,1)S(1)}, bf16[160,256]{1,0:T(8,128)(2,1)S(1)}, u32[]{:S(2)}, u32[]{:S(2)}) collective-permute-start(bf16[160,256]{1,0:T(8,128)(2,1)S(1)} %get-tuple-element.43), channel_id=1, source_target_pairs={{0,224},{16,240},{32,0},{48,16},{64,32},{80,48},{96,64},{112,80},{... | collective-permute-start | bytes 245768 | tf_op jit(solution)/shard_map/ppermute | solution.py:461
  157.5 10.5 %collective-permute-start.6 = (bf16[160,256]{1,0:T(8,128)(2,1)S(1)}, bf16[160,256]{1,0:T(8,128)(2,1)S(1)}, u32[]{:S(2)}, u32[]{:S(2)}) collective-permute-start(bf16[160,256]{1,0:T(8,128)(2,1)S(1)} %get-tuple-element.44), channel_id=1, source_target_pairs={{0,192},{16,208},{32,224},{48,240},{64,0},{80,16},{96,32},{112,48}... | collective-permute-start | bytes 245768 | tf_op jit(solution)/shard_map/ppermute | solution.py:461
  159.2 8.7 %collective-permute-start.5 = (bf16[160,256]{1,0:T(8,128)(2,1)S(1)}, bf16[160,256]{1,0:T(8,128)(2,1)S(1)}, u32[]{:S(2)}, u32[]{:S(2)}) collective-permute-start(bf16[160,256]{1,0:T(8,128)(2,1)S(1)} %get-tuple-element.45), channel_id=1, source_target_pairs={{0,160},{16,176},{32,192},{48,208},{64,224},{80,240},{96,0},{112,1... | collective-permute-start | bytes 245768 | tf_op jit(solution)/shard_map/ppermute | solution.py:461
  161.2 7.4 %collective-permute-start.4 = (bf16[160,256]{1,0:T(8,128)(2,1)S(1)}, bf16[160,256]{1,0:T(8,128)(2,1)S(1)}, u32[]{:S(2)}, u32[]{:S(2)}) collective-permute-start(bf16[160,256]{1,0:T(8,128)(2,1)S(1)} %get-tuple-element.46), channel_id=1, source_target_pairs={{0,128},{16,144},{32,160},{48,176},{64,192},{80,208},{96,224},{112... | collective-permute-start | bytes 245768 | tf_op jit(solution)/shard_map/ppermute | solution.py:461
  164.1 12.9 %collective-permute-start.3 = (bf16[160,256]{1,0:T(8,128)(2,1)S(1)}, bf16[160,256]{1,0:T(8,128)(2,1)S(1)}, u32[]{:S(2)}, u32[]{:S(2)}) collective-permute-start(bf16[160,256]{1,0:T(8,128)(2,1)S(1)} %get-tuple-element.47), channel_id=1, source_target_pairs={{0,96},{16,112},{32,128},{48,144},{64,160},{80,176},{96,192},{112,... | collective-permute-start | bytes 245768 | tf_op jit(solution)/shard_map/ppermute | solution.py:461
  164.4 12.7 %collective-permute-start.2 = (bf16[160,256]{1,0:T(8,128)(2,1)S(1)}, bf16[160,256]{1,0:T(8,128)(2,1)S(1)}, u32[]{:S(2)}, u32[]{:S(2)}) collective-permute-start(bf16[160,256]{1,0:T(8,128)(2,1)S(1)} %get-tuple-element.48), channel_id=1, source_target_pairs={{0,64},{16,80},{32,96},{48,112},{64,128},{80,144},{96,160},{112,17... | collective-permute-start | bytes 245768 | tf_op jit(solution)/shard_map/ppermute | solution.py:461
  168.0 12.8 %collective-permute-start.1 = (bf16[160,256]{1,0:T(8,128)(2,1)S(1)}, bf16[160,256]{1,0:T(8,128)(2,1)S(1)}, u32[]{:S(2)}, u32[]{:S(2)}) collective-permute-start(bf16[160,256]{1,0:T(8,128)(2,1)S(1)} %get-tuple-element.42), channel_id=1, source_target_pairs={{0,32},{16,48},{32,64},{48,80},{64,96},{80,112},{96,128},{112,144}... | collective-permute-start | bytes 245768 | tf_op jit(solution)/shard_map/ppermute | solution.py:461
Sparse Core Ops, SparseCore 0:
  9.9 114.7 all-gather.1

commit v3 on v2

--- a/solution.py
+++ b/solution.py
@@ -55,30 +55,26 @@
     return (iota((place.shape[0], slots), 1) == place).astype(f32).astype(bf16)
 
 
-def pack_kernel(gate_hbm, up_hbm, down_hbm, second_hbm, out_hbm, down, second, held, sems):
+def pack_kernel(gate_hbm, up_hbm, down_hbm, out_hbm, down, held, sems):
     half = gate_hbm.shape[1]
-    cols = out_hbm.shape[1]
-    spans = (pl.ds(0, half), pl.ds(half, half), pl.ds(2 * half, cols - 2 * half))
+    spans = [pl.ds(a * half, half) for a in range(3)]
     loads = [
         pltpu.make_async_copy(down_hbm, down, sems.at[0]),
-        pltpu.make_async_copy(second_hbm, second, sems.at[1]),
-        pltpu.make_async_copy(gate_hbm, held.at[:, spans[0]], sems.at[2]),
-        pltpu.make_async_copy(up_hbm, held.at[:, spans[1]], sems.at[3]),
+        pltpu.make_async_copy(gate_hbm, held.at[:, spans[0]], sems.at[1]),
+        pltpu.make_async_copy(up_hbm, held.at[:, spans[1]], sems.at[2]),
     ]
     stores = [
-        pltpu.make_async_copy(held.at[:, span], out_hbm.at[:, span], sems.at[4 + a])
+        pltpu.make_async_copy(held.at[:, span], out_hbm.at[:, span], sems.at[3 + a])
         for a, span in enumerate(spans)
     ]
     for copy in loads:
         copy.start()
     loads[0].wait()
-    held[:, 2 * half : 3 * half] = down[...].T
+    held[:, 2 * half :] = down[...].T
+    stores[2].start()
     loads[1].wait()
-    held[:, 3 * half :] = second[...].T
-    stores[2].start()
+    stores[0].start()
     loads[2].wait()
-    stores[0].start()
-    loads[3].wait()
     stores[1].start()
     for copy in stores:
         copy.wait()
@@ -151,7 +147,24 @@
         ).astype(bf16)
 
 
-def unfold_cot_kernel(src_ref, dst_ref, mask_ref, gate_ref):
+def assemble_kernel(where_ref, own_ref, other_ref, a1_ref, a2_ref):
+    z, core = where_ref[0], where_ref[1]
+    zs = own_ref.shape[0]
+    ranks = a2_ref.shape[0]
+    share = a1_ref.shape[0] // (2 * zs)
+    for i in range(zs):
+        for ref, side in ((own_ref, core), (other_ref, 1 - core)):
+            f = lax.rem(z + zs - i, zs) * 2 + side
+            a2_ref[:, pl.ds(pl.multiple_of(f * TILE, TILE), TILE)] = ref[i, :ranks, :]
+            at = pl.multiple_of(f * share, 16)
+            a1_ref[pl.ds(at, 16), :] = ref[i, ranks : ranks + 16, :ranks]
+            a1_ref[pl.ds(at + 16, 16), :] = ref[i, ranks : ranks + 16, ranks:]
+            a1_ref[pl.ds(at + 32, 16), :] = ref[i, ranks + 16 :, :ranks]
+
+
+def prepare_kernel(
+    src_ref, a1_ref, a2_ref, dst_ref, mask_ref, gate_ref, low_ref, grad_ref, hga_ref
+):
     unfold_rows(src_ref, dst_ref)
     slots = src_ref.shape[0]
     spares = slots // QUARTERS
@@ -165,13 +178,19 @@
         mask_ref[rows, :] = contract(block, tenant, 1, 0)
         gate_ref[rows, :] = contract(block, weight, 1, 0)
 
+    low = contract(dst_ref[...], a2_ref[...], 1, 1) * mask_ref[...]
+    low_ref[...] = low
+    grad = (ADAPTER_SCALE * gate_ref[...] * low).astype(bf16)
+    grad_ref[...] = grad
+    hga_ref[...] = contract(grad, a1_ref[...], 1, 1)
+
 
 def expert_kernel(
-    x_hbm, c_hbm, w_hbm, a1_hbm, mask_hbm, gate_hbm,
-    rg_hbm, hid_hbm, low_grad_hbm, lowt_hbm,
-    xs, cs, w, a1_ref, mask_ref, gate_ref,
-    rg_ref, hid, low_grad_ref, lowt_ref,
-    acc, hga, parts, spare_rows, dots, sems,
+    x_hbm, c_hbm, w_hbm, a1_hbm, mask_hbm, gate_hbm, low_hbm, hga_hbm,
+    rg_hbm, hid_hbm, lowt_hbm,
+    xs, cs, w, a1_ref, mask_ref, gate_ref, low_ref, hga,
+    rg_ref, hid, lowt_ref,
+    acc, parts, spare_rows, dots, sems,
 ):
     rows, width = xs.shape
     half = hid.shape[1]
@@ -199,7 +218,16 @@
                 begin(c_hbm.at[:, cols], cs.at[:, cols]),
             )
         )
-    small = [begin(a1_hbm, a1_ref), begin(mask_hbm, mask_ref), begin(gate_hbm, gate_ref)]
+    small = [
+        begin(src, dst)
+        for src, dst in (
+            (gate_hbm, gate_ref),
+            (hga_hbm, hga),
+            (a1_hbm, a1_ref),
+            (mask_hbm, mask_ref),
+            (low_hbm, low_ref),
+        )
+    ]
 
     for q in range(CHUNKS):
         cols = slice(q * depth, (q + 1) * depth)
@@ -214,42 +242,22 @@
     for copy in small:
         copy.wait()
 
-    step = 320
-
-    @pl.loop(0, rows // step)
-    def _(i):
-        r = pl.ds(pl.multiple_of(i * step, step), step)
-        pre_gate, pre_up = acc[r, :half], acc[r, half:wide]
-        hid[r, :] = (pre_gate * jax.nn.sigmoid(pre_gate) * pre_up).astype(bf16)
-
-    mask, gate = mask_ref[...], gate_ref[...]
-    a1 = a1_ref[...]
-    cot_low = acc[:, wide + half :] * mask
-    low_grad = (ADAPTER_SCALE * gate * cot_low).astype(bf16)
-    low_grad_ref[...] = low_grad
-    hga[...] = contract(low_grad, a1, 1, 1)
-    low = (contract(hid[...], a1, 1, 0) * mask).astype(bf16).astype(f32)
-    acc[:, wide + half :] = ADAPTER_SCALE * low * cot_low
-    lowt_ref[...] = (ADAPTER_SCALE * gate * low).astype(bf16)
-
-    @pl.loop(0, rows // step)
-    def _(i):
-        r = pl.ds(pl.multiple_of(i * step, step), step)
-        pre_gate, pre_up, cot_down = acc[r, :half], acc[r, half:wide], acc[r, wide : wide + half]
-        s = jax.nn.sigmoid(pre_gate)
-        grad = gate_ref[r, 0:1] * cot_down + hga[r, :]
-        parts[r, half:] = (grad * (pre_gate * s)).astype(bf16)
-        parts[r, :half] = (grad * pre_up * s * (1.0 + pre_gate * (1.0 - s))).astype(bf16)
-        dot = jnp.sum(hid[r, :].astype(f32) * cot_down, axis=1, keepdims=True) + jnp.sum(
-            acc[r, wide + half :], axis=1, keepdims=True
-        )
-        dots[r, :] = jnp.broadcast_to(dot, (step, LANES)).astype(bf16)
-
-    sent = [
-        begin(hid, hid_hbm),
-        begin(low_grad_ref, low_grad_hbm),
-        begin(lowt_ref, lowt_hbm),
-    ]
+    pre_gate, pre_up, cot_down = acc[:, :half], acc[:, half:wide], acc[:, wide:]
+    s = jax.nn.sigmoid(pre_gate)
+    silu = pre_gate * s
+    grad = gate_ref[:, 0:1] * cot_down + hga[...]
+    parts[:, half:] = (grad * silu).astype(bf16)
+    parts[:, :half] = (grad * pre_up * s * (1.0 + pre_gate * (1.0 - s))).astype(bf16)
+    hidden = (silu * pre_up).astype(bf16)
+    hid[...] = hidden
+    low = (contract(hid[...], a1_ref[...], 1, 0) * mask_ref[...]).astype(bf16).astype(f32)
+    lowt_ref[...] = (ADAPTER_SCALE * gate_ref[...] * low).astype(bf16)
+    dot = jnp.sum(hidden.astype(f32) * cot_down, axis=1, keepdims=True) + jnp.sum(
+        ADAPTER_SCALE * low * low_ref[...], axis=1, keepdims=True
+    )
+    dots[...] = jnp.broadcast_to(dot, dots.shape).astype(bf16)
+
+    sent = [begin(hid, hid_hbm), begin(lowt_ref, lowt_hbm)]
     lane = iota((slots, LANES), 1)
     spare_dots = contract(chosen(0, spares, slots), dots[slots:, :], 0, 0)
     rg_ref[:, width + part :] = jnp.where(
@@ -323,7 +331,7 @@
     slots = experts * MAIN
     spares = slots // QUARTERS
     rows = slots + spares
-    cols = 3 * half + ranks
+    cols = 3 * half
     shard = frozen_gate_weight.shape[1]
     zs = spread // 2
     here = lax.axis_index("fsdp")
@@ -333,20 +341,27 @@
         pack_kernel,
         name="pack_weights",
         out_shape=jax.ShapeDtypeStruct((shard, cols), bf16),
-        in_specs=[ANY] * 4,
+        in_specs=[ANY] * 3,
         out_specs=ANY,
         scratch_shapes=[
             pltpu.VMEM((half, shard), bf16),
-            pltpu.VMEM((ranks, shard), bf16),
             pltpu.VMEM((shard, cols), bf16),
-            pltpu.SemaphoreType.DMA((7,)),
+            pltpu.SemaphoreType.DMA((6,)),
         ],
         compiler_params=pltpu.CompilerParams(vmem_limit_bytes=60 << 20),
-    )(
-        frozen_gate_weight[0],
-        frozen_up_weight[0],
-        frozen_down_weight[0],
-        adapter_second_factors[0],
+    )(frozen_gate_weight[0], frozen_up_weight[0], frozen_down_weight[0])
+    packed, first_part, second_part = lax.optimization_barrier(
+        (packed, adapter_first_factors[0], adapter_second_factors[0])
+    )
+    first_rows = [first_part[a * 16 : (a + 1) * 16] for a in range(3)]
+    first_rows.append(jnp.zeros_like(first_rows[0]))
+    small = jnp.concatenate(
+        [
+            second_part,
+            jnp.concatenate(first_rows[:2], axis=1),
+            jnp.concatenate(first_rows[2:], axis=1),
+        ],
+        axis=0,
     )
     weights = lax.all_gather(packed, "fsdp", axis=0, tiled=True)
 
@@ -373,14 +388,34 @@
             rows_2d.shape
         )
 
-    first_full = lax.all_to_all(
-        jnp.broadcast_to(adapter_first_factors, (spread,) + adapter_first_factors.shape[1:]),
-        "fsdp",
-        split_axis=0,
-        concat_axis=0,
-        tiled=True,
-    ).reshape(half, ranks)
-    x_send, c_send, first_full = lax.optimization_barrier((x_send, c_send, first_full))
+    def along(block, step):
+        return lax.ppermute(
+            block, "fsdp", [(f, (f + 2 * step) % spread) for f in range(spread)]
+        )
+
+    swap = [(f, f ^ 1) for f in range(spread)]
+    low_side, high_side = [small], [small]
+    for _ in range(zs // 2 - 1):
+        low_side.append(along(low_side[-1], 1))
+    for _ in range(zs - zs // 2 - 1):
+        high_side.append(along(high_side[-1], -1))
+    x_send, c_send, low_side[3], high_side[3] = lax.optimization_barrier(
+        (x_send, c_send, low_side[3], high_side[3])
+    )
+    low_side.append(along(low_side[-1], 1))
+    near = jnp.stack(low_side + high_side[:0:-1])
+    far = lax.ppermute(near, "fsdp", swap)
+    first_full, second_full = pl.pallas_call(
+        assemble_kernel,
+        name="assemble_adapters",
+        out_shape=(
+            jax.ShapeDtypeStruct((half, ranks), bf16),
+            jax.ShapeDtypeStruct((ranks, width), bf16),
+        ),
+        in_specs=[SMEM, VMEM, VMEM],
+        out_specs=(VMEM, VMEM),
+        compiler_params=pltpu.CompilerParams(vmem_limit_bytes=16 << 20),
+    )(where, near, far)
     x_rows, c_rows = exchange(x_send), exchange(c_send)
 
     x_all = pl.pallas_call(
@@ -391,30 +426,32 @@
         out_specs=VMEM,
         compiler_params=pltpu.CompilerParams(vmem_limit_bytes=24 << 20),
     )(x_rows)
-    c_all, mask, gate = pl.pallas_call(
-        unfold_cot_kernel,
-        name="unfold_cotangent",
+    c_all, mask, gate, cot_low, low_grad, grad_low = pl.pallas_call(
+        prepare_kernel,
+        name="prepare_cotangent",
         out_shape=(
             jax.ShapeDtypeStruct((rows, width), bf16),
             jax.ShapeDtypeStruct((rows, ranks), f32),
             jax.ShapeDtypeStruct((rows, ranks), f32),
+            jax.ShapeDtypeStruct((rows, ranks), f32),
+            jax.ShapeDtypeStruct((rows, ranks), bf16),
+            jax.ShapeDtypeStruct((rows, half), f32),
         ),
-        in_specs=[VMEM],
-        out_specs=(VMEM, VMEM, VMEM),
-        compiler_params=pltpu.CompilerParams(vmem_limit_bytes=24 << 20),
-    )(c_rows)
-
-    back, hidden, low_grad, low_rank = pl.pallas_call(
+        in_specs=[VMEM, VMEM, VMEM],
+        out_specs=(VMEM,) * 6,
+        compiler_params=pltpu.CompilerParams(vmem_limit_bytes=60 << 20),
+    )(c_rows, first_full, second_full)
+
+    back, hidden, low_rank = pl.pallas_call(
         expert_kernel,
         name="expert",
         out_shape=(
             jax.ShapeDtypeStruct((slots, width + part + LANES), bf16),
             jax.ShapeDtypeStruct((rows, half), bf16),
             jax.ShapeDtypeStruct((rows, ranks), bf16),
-            jax.ShapeDtypeStruct((rows, ranks), bf16),
         ),
-        in_specs=[ANY] * 6,
-        out_specs=(ANY, ANY, ANY, ANY),
+        in_specs=[ANY] * 8,
+        out_specs=(ANY, ANY, ANY),
         scratch_shapes=[
             pltpu.VMEM((rows, width), bf16),
             pltpu.VMEM((rows, width), bf16),
@@ -422,19 +459,19 @@
             pltpu.VMEM((half, ranks), bf16),
             pltpu.VMEM((rows, ranks), f32),
             pltpu.VMEM((rows, ranks), f32),
+            pltpu.VMEM((rows, ranks), f32),
+            pltpu.VMEM((rows, half), f32),
             pltpu.VMEM((slots, width + part + LANES), bf16),
             pltpu.VMEM((rows, half), bf16),
             pltpu.VMEM((rows, ranks), bf16),
-            pltpu.VMEM((rows, ranks), bf16),
             pltpu.VMEM((rows, cols), f32),
-            pltpu.VMEM((rows, half), f32),
             pltpu.VMEM((rows, 2 * half), bf16),
             pltpu.VMEM((spares, width), bf16),
             pltpu.VMEM((rows, LANES), bf16),
-            pltpu.SemaphoreType.DMA((3 * CHUNKS + 7 + width // BACK,)),
+            pltpu.SemaphoreType.DMA((3 * CHUNKS + 8 + width // BACK,)),
         ],
         compiler_params=pltpu.CompilerParams(vmem_limit_bytes=LIMIT << 20),
-    )(x_all, c_all, weights, first_full, mask, gate)
+    )(x_all, c_all, weights, first_full, mask, gate, cot_low, grad_low)
 
     own, other = pl.pallas_call(
         adapter_kernel,
@@ -452,7 +489,6 @@
 
     returned = exchange(back)
 
-    swap = [(f, f ^ 1) for f in range(spread)]
     pair = own.astype(f32) + lax.ppermute(other, "fsdp", swap).astype(f32)
     halved = pair.astype(bf16)
     total = pair[0]

time: 200 us -> 197 us (0.985)
  waiting for transfers between devices: 66.8 us -> 53.9 us
  starting transfers between devices: 33.2 us -> 44.4 us
  Pallas kernels: 29 us -> 34.7 us
  blocking collectives: 40.9 us -> 36.6 us
  local copies, waits for them, and re-layouts: 14.4 us -> 11.9 us
    all_to_all x2, waiting for transfers between devices: 43.1 us -> 18.5 us  [exchange(): lax.all_to_all(block, 'expert', split_axis=0, concat_axis=0, tiled=True)]
    ppermute x0 -> x8, starting transfers between devices: none -> 17.4 us  [the longest x7 11.9 us: along(): lax.ppermute(block, 'fsdp', [(f, (f + 2 * step) % spread) for f in range(...]
    ppermute x0 -> x8, waiting for transfers between devices: none -> 12.1 us  [the longest x7 10.3 us: along(): lax.ppermute(block, 'fsdp', [(f, (f + 2 * step) % spread) for f in range(...]
    all_to_all x1 -> x0, starting transfers between devices: 9.98 us -> none  [shards(): lax.all_to_all(jnp.broadcast_to(adapter_first_factors, (spread,) + adapte...]
    all_gather x1, waiting for transfers between devices: 6.12 us -> 15.1 us  [shards(): weights = lax.all_gather(packed, 'fsdp', axis=0, tiled=True)]
    ppermute x7, waiting for transfers between devices: 12.8 us -> 6.54 us  [shards(): total = total + lax.ppermute(halved[dz], 'fsdp', moves).astype(f32)]
    pallas_call x1 -> x2, Pallas kernels: 0.82 us -> 6.54 us  [the longest x1 5.29 us: shards(): pl.pallas_call(prepare_kernel, name='prepare_cotangent', out_shape=(jax.S...]
    all_to_all x1, blocking collectives: 40.9 us -> 36.6 us  [exchange(): lax.all_to_all(block, 'expert', split_axis=0, concat_axis=0, tiled=True)]
  transfers between devices with their start and end apart: 12 -> 19, of which waited for: 8 -> 11; matrix products, arithmetic and copies ran while one was open for 1% -> 3% of each run, Pallas kernels for 4% -> 7%
where the time goes in v3:
time: 197 us
  waiting for transfers between devices  53.9 us (27%)
  starting transfers between devices  44.4 us (23%)
  blocking collectives  36.6 us (19%)
  Pallas kernels  34.7 us (18%)
  between operations  14.4 us (7%)
  local copies, waits for them, and re-layouts  11.9 us (6%)
    all_to_all x1, blocking collectives, exchange(): lax.all_to_all(block, 'expert', split_axis=0, concat_axis=0, tiled=True)  36.6 us
    all_to_all x2, waiting for transfers between devices, exchange(): lax.all_to_all(block, 'expert', split_axis=0, concat_axis=0, tiled=True)  18.5 us
    pallas_call x1, Pallas kernels, shards(): pl.pallas_call(expert_kernel, name='expert', out_shape=(jax.ShapeDtypeStr...  17.3 us
    all_gather x1, waiting for transfers between devices, shards(): weights = lax.all_gather(packed, 'fsdp', axis=0, tiled=True)  15.1 us
    ppermute x7, starting transfers between devices, shards(): total = total + lax.ppermute(halved[dz], 'fsdp', moves).astype(f32)  14.9 us
    ppermute x7, starting transfers between devices, along(): lax.ppermute(block, 'fsdp', [(f, (f + 2 * step) % spread) for f in range(...  11.9 us
    all_to_all x2, starting transfers between devices, exchange(): lax.all_to_all(block, 'expert', split_axis=0, concat_axis=0, tiled=True)  11.4 us
    unnamed x49, local copies, waits for them, and re-layouts  11.1 us
  transfers between devices with their start and end apart: 19, of which 11 were waited for; matrix products, arithmetic and copies ran while one was open for 3% of the time, Pallas kernels for 7%

profile of v3, /device:TPU:1, one launch (start us, length us, event | category | flops | bytes accessed | tf_op | source)
XLA Modules:
  0.0 196.9 jit_solution(7004597105424227459)
XLA Ops:
  7.3 2.4 %pack_weights.1 = bf16[256,2304]{1,0:T(8,128)(2,1)} custom-call(bf16[256,768]{1,0:T(8,128)(2,1)} %bitcast.69, bf16[256,768]{1,0:T(8,128)(2,1)} %bitcast.70, bf16[768,256]{1,0:T(8,128)(2,1)} %bitcast.71), custom_call_target="tpu_custom_call" | custom-call | tf_op jit(solution)/shard_map/pack_weights/pallas_call | solution.py:340
  9.8 2.5 %collective-permute-start = (bf16[160,256]{1,0:T(8,128)(2,1)S(1)}, bf16[160,256]{1,0:T(8,128)(2,1)S(1)}, u32[]{:S(2)}, u32[]{:S(2)}) collective-permute-start(bf16[160,256]{1,0:T(8,128)(2,1)S(1)} %fusion.8), channel_id=1, source_target_pairs={{0,32},{16,48},{32,64},{48,80},{64,96},{80,112},{96,128},{112,144}... | collective-permute-start | bytes 245768 | tf_op jit(solution)/shard_map/ppermute | solution.py:392
  12.3 4.0 %collective-permute-start.3 = (bf16[160,256]{1,0:T(8,128)(2,1)S(1)}, bf16[160,256]{1,0:T(8,128)(2,1)S(1)}, u32[]{:S(2)}, u32[]{:S(2)}) collective-permute-start(bf16[160,256]{1,0:T(8,128)(2,1)S(1)} %fusion.8), channel_id=1, source_target_pairs={{0,224},{16,240},{32,0},{48,16},{64,32},{80,48},{96,64},{112,80},{... | collective-permute-start | bytes 245768 | tf_op jit(solution)/shard_map/ppermute | solution.py:392
  16.3 2.1 %collective-permute-done = bf16[160,256]{1,0:T(8,128)(2,1)S(1)} collective-permute-done((bf16[160,256]{1,0:T(8,128)(2,1)S(1)}, bf16[160,256]{1,0:T(8,128)(2,1)S(1)}, u32[]{:S(2)}, u32[]{:S(2)}) %collective-permute-start) | collective-permute-done | bytes 81952 | tf_op jit(solution)/shard_map/ppermute | solution.py:392
  18.4 2.7 %collective-permute-start.4 = (bf16[160,256]{1,0:T(8,128)(2,1)S(1)}, bf16[160,256]{1,0:T(8,128)(2,1)S(1)}, u32[]{:S(2)}, u32[]{:S(2)}) collective-permute-start(bf16[160,256]{1,0:T(8,128)(2,1)S(1)} %collective-permute-done.3), channel_id=1, source_target_pairs={{0,224},{16,240},{32,0},{48,16},{64,32},{80,48},{96,64},{112,80},{... | collective-permute-start | bytes 245768 | tf_op jit(solution)/shard_map/ppermute | solution.py:392
  21.1 1.8 collective-permute-done.1
  22.9 2.7 %collective-permute-start.5 = (bf16[160,256]{1,0:T(8,128)(2,1)S(1)}, bf16[160,256]{1,0:T(8,128)(2,1)S(1)}, u32[]{:S(2)}, u32[]{:S(2)}) collective-permute-start(bf16[160,256]{1,0:T(8,128)(2,1)S(1)} %collective-permute-done.4), channel_id=1, source_target_pairs={{0,224},{16,240},{32,0},{48,16},{64,32},{80,48},{96,64},{112,80},{... | collective-permute-start | bytes 245768 | tf_op jit(solution)/shard_map/ppermute | solution.py:392
  26.0 2.9 %shard_map.129 = (bf16[256,5120]{1,0:T(8,128)(2,1)S(1)}, bf16[256,5248]{1,0:T(8,128)(2,1)S(1)}) custom-call(s32[128,2]{1,0:T(8,128)S(1)} %copy.17.refs_0_, bf16[128,2]{1,0:T(8,128)(2,1)S(1)} %copy.15.refs_1_, s32[128,1]{1,0:T(8,128)S(1)} %copy.16.refs_2_, bf16[128,4096]{1,0:T(8,128)(2,1)S(1)} %copy-done.3, bf16[128,4096]{1,0:T(8,128)(2,1)S(1)} %copy-done.4), custom_call_target="tpu_custom_call" | custom-call | tf_op jit(solution)/shard_map/pallas_call | solution.py:368
  29.6 36.6 %all_to_all.15 = bf16[16,16,5120]{2,1,0:T(8,128)(2,1)S(1)} all-to-all(bf16[16,16,5120]{2,1,0:T(8,128)(2,1)S(1)} %bitcast.67), channel_id=1, replica_groups=mesh['fsdp'=16,'expert'=16] {'expert'}, dimensions={0} | all-to-all | bytes 5242880 | tf_op jit(solution)/shard_map/all_to_all | solution.py:387
  66.3 4.5 %all-to-all-start.1 = ((bf16[16,16,5248]{2,1,0:T(8,128)(2,1)}), bf16[16,16,5248]{2,1,0:T(8,128)(2,1)}, u32[]{:S(2)}, u32[]{:S(2)}) async-start(bf16[16,16,5248]{2,1,0:T(8,128)(2,1)} %bitcast.66), calls=%async_computation.1 | async-start | bytes 5373952 | tf_op jit(solution)/shard_map/all_to_all | solution.py:387
  72.6 0.9 bitcast_dynamic-update-slice_fusion.4
  73.5 6.4 %collective-permute-done.6 = bf16[160,256]{1,0:T(8,128)(2,1)S(1)} collective-permute-done((bf16[160,256]{1,0:T(8,128)(2,1)}, bf16[160,256]{1,0:T(8,128)(2,1)S(1)}, u32[]{:S(2)}, u32[]{:S(2)}) %collective-permute-start.6) | collective-permute-done | bytes 81952 | tf_op jit(solution)/shard_map/ppermute | solution.py:392
  81.7 5.5 %collective-permute-start.7 = (bf16[8,160,256]{2,1,0:T(8,128)(2,1)S(1)}, bf16[8,160,256]{2,1,0:T(8,128)(2,1)}, u32[]{:S(2)}, u32[]{:S(2)}) collective-permute-start(bf16[8,160,256]{2,1,0:T(8,128)(2,1)S(1)} %bitcast_dynamic-update-slice_fusion.own_ref), channel_id=1, source_target_pairs={{0,16},{16,0},{32,48},{48,32},{64,80},{80,64},{96,112},{112,96},{1... | collective-permute-start | bytes 1966088 | tf_op jit(solution)/shard_map/ppermute | solution.py:407
  87.3 1.8 collective-permute-done.7.other_ref
  89.1 1.3 assemble_adapters.1
  90.3 1.0 copy-done.5
  92.7 1.6 copy-done.1
  94.3 7.5 %all-to-all-done.1 = bf16[16,16,5248]{2,1,0:T(8,128)(2,1)} async-done(((bf16[16,16,5248]{2,1,0:T(8,128)(2,1)}), bf16[16,16,5248]{2,1,0:T(8,128)(2,1)}, u32[]{:S(2)}, u32[]{:S(2)}) %all-to-all-start.1) | async-done | bytes 2687008 | tf_op jit(solution)/shard_map/all_to_all | solution.py:387
  101.7 5.3 %prepare_cotangent.1 = (bf16[320,4096]{1,0:T(8,128)(2,1)}, f32[320,128]{1,0:T(8,128)}, f32[320,128]{1,0:T(8,128)}, f32[320,128]{1,0:T(8,128)}, bf16[320,128]{1,0:T(8,128)(2,1)}, /*index=5*/f32[320,768]{1,0:T(8,128)}) custom-call(bf16[256,5248]{1,0:T(8,128)(2,1)} %bitcast.9.src_ref, bf16[768,128]{1,0:T(8,128)(2,1)} %copy-done.6, bf16[128,4096]{1,0:T(8,128)(2,1)} %copy-done.5), custom_call_target="tpu_custom_call" | custom-call | tf_op jit(solution)/shard_map/prepare_cotangent/pallas_call | solution.py:429
  107.0 15.1 %all-gather.2.cloned.1.call-done.w_hbm = bf16[4096,2304]{1,0:T(8,128)(2,1)} async-done(((bf16[256,2304]{1,0:T(8,128)(2,1)}), bf16[4096,2304]{1,0:T(8,128)(2,1)}) %all-gather.2.cloned.1.call-update) | async-done | bytes 18874384 | tf_op jit(solution)/shard_map/all_gather | solution.py:366
  122.1 17.3 %expert.1 = (bf16[256,5248]{1,0:T(8,128)(2,1)}, bf16[320,768]{1,0:T(8,128)(2,1)}, bf16[320,128]{1,0:T(8,128)(2,1)}) custom-call(bf16[320,4096]{1,0:T(8,128)(2,1)} %copy-done.1, bf16[320,4096]{1,0:T(8,128)(2,1)} %get-tuple-element.38.c_hbm.c_ref, bf16[4096,2304]{1,0:T(8,128)(2,1)} %all-gather.2.cloned.1.call-done.w_hbm, bf16[768,128]{1,0:T(8,128)(2,1)} %copy-done.6, ...), custom_call_target="tpu_custom_call" | custom-call | tf_op jit(solution)/shard_map/expert/pallas_call | solution.py:445
  139.5 6.9 %all-to-all-start.2 = ((bf16[16,16,5248]{2,1,0:T(8,128)(2,1)}), bf16[16,16,5248]{2,1,0:T(8,128)(2,1)S(1)}, u32[]{:S(2)}, u32[]{:S(2)}) async-start(bf16[16,16,5248]{2,1,0:T(8,128)(2,1)} %bitcast.68), calls=%async_computation.2 | async-start | bytes 5373952 | tf_op jit(solution)/shard_map/all_to_all | solution.py:387
  146.4 1.7 copy-done
  148.1 2.8 %adapters.1 = (bf16[8,160,256]{2,1,0:T(8,128)(2,1)S(1)}, bf16[8,160,256]{2,1,0:T(8,128)(2,1)S(1)}) custom-call(s32[2]{0:T(128)S(1)} %pad_add_fusion.where_ref, bf16[320,768]{1,0:T(8,128)(2,1)S(1)} %copy-done.7, bf16[320,128]{1,0:T(8,128)(2,1)S(1)} %copy-done.8, bf16[320,128]{1,0:T(8,128)(2,1)S(1)} %copy-done.9, bf16[320,4096]{1,0:T(8,128)(2,1)S(1)} %copy-done), custom_call_target="tpu_custom_call" | custom-call | flops 400000000 | bytes 6000000 | tf_op jit(solution)/shard_map/adapters/pallas_call | solution.py:476
  151.5 1.7 collective-permute-done.8
  153.6 3.8 %collective-permute-start.11 = (bf16[160,256]{1,0:T(8,128)(2,1)S(1)}, bf16[160,256]{1,0:T(8,128)(2,1)S(1)}, u32[]{:S(2)}, u32[]{:S(2)}) collective-permute-start(bf16[160,256]{1,0:T(8,128)(2,1)S(1)} %get-tuple-element.63), channel_id=1, source_target_pairs={{0,96},{16,112},{32,128},{48,144},{64,160},{80,176},{96,192},{112,... | collective-permute-start | bytes 245768 | tf_op jit(solution)/shard_map/ppermute | solution.py:497
  157.4 3.8 %collective-permute-start.13 = (bf16[160,256]{1,0:T(8,128)(2,1)S(1)}, bf16[160,256]{1,0:T(8,128)(2,1)S(1)}, u32[]{:S(2)}, u32[]{:S(2)}) collective-permute-start(bf16[160,256]{1,0:T(8,128)(2,1)S(1)} %get-tuple-element.61), channel_id=1, source_target_pairs={{0,160},{16,176},{32,192},{48,208},{64,224},{80,240},{96,0},{112,1... | collective-permute-start | bytes 245768 | tf_op jit(solution)/shard_map/ppermute | solution.py:497
  161.2 3.3 %collective-permute-start.14 = (bf16[160,256]{1,0:T(8,128)(2,1)S(1)}, bf16[160,256]{1,0:T(8,128)(2,1)S(1)}, u32[]{:S(2)}, u32[]{:S(2)}) collective-permute-start(bf16[160,256]{1,0:T(8,128)(2,1)S(1)} %get-tuple-element.60), channel_id=1, source_target_pairs={{0,192},{16,208},{32,224},{48,240},{64,0},{80,16},{96,32},{112,48}... | collective-permute-start | bytes 245768 | tf_op jit(solution)/shard_map/ppermute | solution.py:497
  164.5 4.0 %collective-permute-start.9 = (bf16[160,256]{1,0:T(8,128)(2,1)S(1)}, bf16[160,256]{1,0:T(8,128)(2,1)S(1)}, u32[]{:S(2)}, u32[]{:S(2)}) collective-permute-start(bf16[160,256]{1,0:T(8,128)(2,1)S(1)} %get-tuple-element.58), channel_id=1, source_target_pairs={{0,32},{16,48},{32,64},{48,80},{64,96},{80,112},{96,128},{112,144}... | collective-permute-start | bytes 245768 | tf_op jit(solution)/shard_map/ppermute | solution.py:497
  169.3 4.9 %collective-permute-done.14 = bf16[160,256]{1,0:T(8,128)(2,1)S(1)} collective-permute-done((bf16[160,256]{1,0:T(8,128)(2,1)S(1)}, bf16[160,256]{1,0:T(8,128)(2,1)S(1)}, u32[]{:S(2)}, u32[]{:S(2)}) %collective-permute-start.14) | collective-permute-done | bytes 81952 | tf_op jit(solution)/shard_map/ppermute | solution.py:497
  176.4 11.0 %all-to-all-done.2 = bf16[16,16,5248]{2,1,0:T(8,128)(2,1)S(1)} async-done(((bf16[16,16,5248]{2,1,0:T(8,128)(2,1)}), bf16[16,16,5248]{2,1,0:T(8,128)(2,1)S(1)}, u32[]{:S(2)}, u32[]{:S(2)}) %all-to-all-start.2) | async-done | bytes 2687008 | tf_op jit(solution)/shard_map/all_to_all | solution.py:387
  187.4 2.1 %shard_map.130 = (bf16[128,4096]{1,0:T(8,128)(2,1)}, bf16[128,2]{1,0:T(8,128)(2,1)S(1)}) custom-call(s32[128,2]{1,0:T(8,128)S(1)} %copy.17.refs_0_, bf16[256,5248]{1,0:T(8,128)(2,1)S(1)} %bitcast.64), custom_call_target="tpu_custom_call" | custom-call | tf_op jit(solution)/shard_map/pallas_call | solution.py:508
  (77 shorter events, 10.8 us)
Async XLA Ops:
  7.2 2.6 %copy-start.10 = (bf16[1,128,256]{2,1,0:T(8,128)(2,1)S(1)}, bf16[1,128,256]{2,1,0:T(8,128)(2,1)}, u32[]{:S(2)}) copy-start(bf16[1,128,256]{2,1,0:T(8,128)(2,1)} %param.19) | copy-start | bytes 196612
  7.2 18.4 %copy-start.17 = (s32[128,2]{0,1:T(2,128)S(1)}, s32[128,2]{0,1:T(2,128)}, u32[]{:S(2)}) copy-start(s32[128,2]{0,1:T(2,128)} %param.12) | copy-start | bytes 3076
  7.2 18.5 %copy-start.18 = (s32[128]{0:T(128)S(1)}, s32[128]{0:T(128)}, u32[]{:S(2)}) copy-start(s32[128]{0:T(128)} %param.14) | copy-start | bytes 1540
  7.2 18.6 %copy-start.19 = (bf16[128,2]{0,1:T(2,128)(2,1)S(1)}, bf16[128,2]{0,1:T(2,128)(2,1)}, u32[]{:S(2)}) copy-start(bf16[128,2]{0,1:T(2,128)(2,1)} %param.13) | copy-start | bytes 1540
  7.2 18.8 %copy-start.3 = (bf16[128,4096]{1,0:T(8,128)(2,1)S(1)}, bf16[128,4096]{1,0:T(8,128)(2,1)}, u32[]{:S(2)}) copy-start(bf16[128,4096]{1,0:T(8,128)(2,1)} %refs_3_.1) | copy-start | bytes 3145732
  7.2 18.8 %copy-start.4 = (bf16[128,4096]{1,0:T(8,128)(2,1)S(1)}, bf16[128,4096]{1,0:T(8,128)(2,1)}, u32[]{:S(2)}) copy-start(bf16[128,4096]{1,0:T(8,128)(2,1)} %refs_4_.1) | copy-start | bytes 3145732
  7.2 114.8 %all-gather.2.cloned.1.call-start = ((), (), s32[]{:S(2)}) async-start(), calls=%async_computation.3 | async-start | bytes 20054016 | tf_op jit(solution)/shard_map/all_gather | solution.py:366
  9.8 8.7 %collective-permute-start = (bf16[160,256]{1,0:T(8,128)(2,1)S(1)}, bf16[160,256]{1,0:T(8,128)(2,1)S(1)}, u32[]{:S(2)}, u32[]{:S(2)}) collective-permute-start(bf16[160,256]{1,0:T(8,128)(2,1)S(1)} %fusion.8), channel_id=1, source_target_pairs={{0,32},{16,48},{32,64},{48,80},{64,96},{80,112},{96,128},{112,144}... | collective-permute-start | bytes 245768 | tf_op jit(solution)/shard_map/ppermute | solution.py:392
  12.3 6.1 %collective-permute-start.3 = (bf16[160,256]{1,0:T(8,128)(2,1)S(1)}, bf16[160,256]{1,0:T(8,128)(2,1)S(1)}, u32[]{:S(2)}, u32[]{:S(2)}) collective-permute-start(bf16[160,256]{1,0:T(8,128)(2,1)S(1)} %fusion.8), channel_id=1, source_target_pairs={{0,224},{16,240},{32,0},{48,16},{64,32},{80,48},{96,64},{112,80},{... | collective-permute-start | bytes 245768 | tf_op jit(solution)/shard_map/ppermute | solution.py:392
  18.4 7.3 %copy-start.12 = (bf16[160,256]{1,0:T(8,128)(2,1)}, bf16[160,256]{1,0:T(8,128)(2,1)S(1)}, u32[]{:S(2)}) copy-start(bf16[160,256]{1,0:T(8,128)(2,1)S(1)} %collective-permute-done) | copy-start | bytes 245764
  18.4 4.5 %collective-permute-start.1 = (bf16[160,256]{1,0:T(8,128)(2,1)S(1)}, bf16[160,256]{1,0:T(8,128)(2,1)S(1)}, u32[]{:S(2)}, u32[]{:S(2)}) collective-permute-start(bf16[160,256]{1,0:T(8,128)(2,1)S(1)} %collective-permute-done), channel_id=1, source_target_pairs={{0,32},{16,48},{32,64},{48,80},{64,96},{80,112},{96,128},{112,144}... | collective-permute-start | bytes 245768 | tf_op jit(solution)/shard_map/ppermute | solution.py:392
  18.4 4.5 %collective-permute-start.4 = (bf16[160,256]{1,0:T(8,128)(2,1)S(1)}, bf16[160,256]{1,0:T(8,128)(2,1)S(1)}, u32[]{:S(2)}, u32[]{:S(2)}) collective-permute-start(bf16[160,256]{1,0:T(8,128)(2,1)S(1)} %collective-permute-done.3), channel_id=1, source_target_pairs={{0,224},{16,240},{32,0},{48,16},{64,32},{80,48},{96,64},{112,80},{... | collective-permute-start | bytes 245768 | tf_op jit(solution)/shard_map/ppermute | solution.py:392
  22.9 6.0 %copy-start.13 = (bf16[160,256]{1,0:T(8,128)(2,1)}, bf16[160,256]{1,0:T(8,128)(2,1)S(1)}, u32[]{:S(2)}) copy-start(bf16[160,256]{1,0:T(8,128)(2,1)S(1)} %collective-permute-done.1) | copy-start | bytes 245764
  22.9 6.0 %collective-permute-start.2 = (bf16[160,256]{1,0:T(8,128)(2,1)S(1)}, bf16[160,256]{1,0:T(8,128)(2,1)S(1)}, u32[]{:S(2)}, u32[]{:S(2)}) collective-permute-start(bf16[160,256]{1,0:T(8,128)(2,1)S(1)} %collective-permute-done.1), channel_id=1, source_target_pairs={{0,32},{16,48},{32,64},{48,80},{64,96},{80,112},{96,128},{112,144}... | collective-permute-start | bytes 245768 | tf_op jit(solution)/shard_map/ppermute | solution.py:392
  22.9 6.0 %copy-start.11 = (bf16[160,256]{1,0:T(8,128)(2,1)}, bf16[160,256]{1,0:T(8,128)(2,1)S(1)}, u32[]{:S(2)}) copy-start(bf16[160,256]{1,0:T(8,128)(2,1)S(1)} %collective-permute-done.4) | copy-start | bytes 245764
  22.9 6.0 %collective-permute-start.5 = (bf16[160,256]{1,0:T(8,128)(2,1)S(1)}, bf16[160,256]{1,0:T(8,128)(2,1)S(1)}, u32[]{:S(2)}, u32[]{:S(2)}) collective-permute-start(bf16[160,256]{1,0:T(8,128)(2,1)S(1)} %collective-permute-done.4), channel_id=1, source_target_pairs={{0,224},{16,240},{32,0},{48,16},{64,32},{80,48},{96,64},{112,80},{... | collective-permute-start | bytes 245768 | tf_op jit(solution)/shard_map/ppermute | solution.py:392
  28.9 37.4 %copy-start.2 = (bf16[256,5248]{1,0:T(8,128)(2,1)}, bf16[256,5248]{1,0:T(8,128)(2,1)S(1)}, u32[]{:S(2)}) copy-start(bf16[256,5248]{1,0:T(8,128)(2,1)S(1)} %get-tuple-element.33) | copy-start | bytes 8060932
  66.3 35.5 %all-to-all-start.1 = ((bf16[16,16,5248]{2,1,0:T(8,128)(2,1)}), bf16[16,16,5248]{2,1,0:T(8,128)(2,1)}, u32[]{:S(2)}, u32[]{:S(2)}) async-start(bf16[16,16,5248]{2,1,0:T(8,128)(2,1)} %bitcast.66), calls=%async_computation.1 | async-start | bytes 5373952 | tf_op jit(solution)/shard_map/all_to_all | solution.py:387
  72.6 7.3 %collective-permute-start.6 = (bf16[160,256]{1,0:T(8,128)(2,1)}, bf16[160,256]{1,0:T(8,128)(2,1)S(1)}, u32[]{:S(2)}, u32[]{:S(2)}) collective-permute-start(bf16[160,256]{1,0:T(8,128)(2,1)} %copy-done.15), channel_id=1, source_target_pairs={{0,32},{16,48},{32,64},{48,80},{64,96},{80,112},{96,128},{112,144}... | collective-permute-start | bytes 245768 | tf_op jit(solution)/shard_map/ppermute | solution.py:392
  81.7 7.4 %collective-permute-start.7 = (bf16[8,160,256]{2,1,0:T(8,128)(2,1)S(1)}, bf16[8,160,256]{2,1,0:T(8,128)(2,1)}, u32[]{:S(2)}, u32[]{:S(2)}) collective-permute-start(bf16[8,160,256]{2,1,0:T(8,128)(2,1)S(1)} %bitcast_dynamic-update-slice_fusion.own_ref), channel_id=1, source_target_pairs={{0,16},{16,0},{32,48},{48,32},{64,80},{80,64},{96,112},{112,96},{1... | collective-permute-start | bytes 1966088 | tf_op jit(solution)/shard_map/ppermute | solution.py:407
  139.4 6.9 %copy-start.7 = (bf16[320,768]{1,0:T(8,128)(2,1)S(1)}, bf16[320,768]{1,0:T(8,128)(2,1)}, u32[]{:S(2)}) copy-start(bf16[320,768]{1,0:T(8,128)(2,1)} %get-tuple-element.47.hid_ref) | copy-start | bytes 1474564
  139.4 6.9 %copy-start.8 = (bf16[320,128]{1,0:T(8,128)(2,1)S(1)}, bf16[320,128]{1,0:T(8,128)(2,1)}, u32[]{:S(2)}) copy-start(bf16[320,128]{1,0:T(8,128)(2,1)} %get-tuple-element.48.low_grad_ref) | copy-start | bytes 245764
  139.5 6.9 %copy-start.9 = (bf16[320,128]{1,0:T(8,128)(2,1)S(1)}, bf16[320,128]{1,0:T(8,128)(2,1)}, u32[]{:S(2)}) copy-start(bf16[320,128]{1,0:T(8,128)(2,1)} %get-tuple-element.49.lowt_ref) | copy-start | bytes 245764
  139.5 47.9 %all-to-all-start.2 = ((bf16[16,16,5248]{2,1,0:T(8,128)(2,1)}), bf16[16,16,5248]{2,1,0:T(8,128)(2,1)S(1)}, u32[]{:S(2)}, u32[]{:S(2)}) async-start(bf16[16,16,5248]{2,1,0:T(8,128)(2,1)} %bitcast.68), calls=%async_computation.2 | async-start | bytes 5373952 | tf_op jit(solution)/shard_map/all_to_all | solution.py:387
  150.9 2.3 %collective-permute-start.8 = (bf16[8,160,256]{2,1,0:T(8,128)(2,1)S(1)}, bf16[8,160,256]{2,1,0:T(8,128)(2,1)S(1)}, u32[]{:S(2)}, u32[]{:S(2)}) collective-permute-start(bf16[8,160,256]{2,1,0:T(8,128)(2,1)S(1)} %get-tuple-element.51), channel_id=1, source_target_pairs={{0,16},{16,0},{32,48},{48,32},{64,80},{80,64},{96,112},{112,96},{1... | collective-permute-start | bytes 1966088 | tf_op jit(solution)/shard_map/ppermute | solution.py:492
  153.5 11.0 %collective-permute-start.10 = (bf16[160,256]{1,0:T(8,128)(2,1)S(1)}, bf16[160,256]{1,0:T(8,128)(2,1)S(1)}, u32[]{:S(2)}, u32[]{:S(2)}) collective-permute-start(bf16[160,256]{1,0:T(8,128)(2,1)S(1)} %get-tuple-element.64), channel_id=1, source_target_pairs={{0,64},{16,80},{32,96},{48,112},{64,128},{80,144},{96,160},{112,17... | collective-permute-start | bytes 245768 | tf_op jit(solution)/shard_map/ppermute | solution.py:497
  153.6 10.9 %collective-permute-start.11 = (bf16[160,256]{1,0:T(8,128)(2,1)S(1)}, bf16[160,256]{1,0:T(8,128)(2,1)S(1)}, u32[]{:S(2)}, u32[]{:S(2)}) collective-permute-start(bf16[160,256]{1,0:T(8,128)(2,1)S(1)} %get-tuple-element.63), channel_id=1, source_target_pairs={{0,96},{16,112},{32,128},{48,144},{64,160},{80,176},{96,192},{112,... | collective-permute-start | bytes 245768 | tf_op jit(solution)/shard_map/ppermute | solution.py:497
  157.4 11.1 %collective-permute-start.12 = (bf16[160,256]{1,0:T(8,128)(2,1)S(1)}, bf16[160,256]{1,0:T(8,128)(2,1)S(1)}, u32[]{:S(2)}, u32[]{:S(2)}) collective-permute-start(bf16[160,256]{1,0:T(8,128)(2,1)S(1)} %get-tuple-element.62), channel_id=1, source_target_pairs={{0,128},{16,144},{32,160},{48,176},{64,192},{80,208},{96,224},{112... | collective-permute-start | bytes 245768 | tf_op jit(solution)/shard_map/ppermute | solution.py:497
  157.4 11.9 %collective-permute-start.13 = (bf16[160,256]{1,0:T(8,128)(2,1)S(1)}, bf16[160,256]{1,0:T(8,128)(2,1)S(1)}, u32[]{:S(2)}, u32[]{:S(2)}) collective-permute-start(bf16[160,256]{1,0:T(8,128)(2,1)S(1)} %get-tuple-element.61), channel_id=1, source_target_pairs={{0,160},{16,176},{32,192},{48,208},{64,224},{80,240},{96,0},{112,1... | collective-permute-start | bytes 245768 | tf_op jit(solution)/shard_map/ppermute | solution.py:497
  161.2 13.1 %collective-permute-start.14 = (bf16[160,256]{1,0:T(8,128)(2,1)S(1)}, bf16[160,256]{1,0:T(8,128)(2,1)S(1)}, u32[]{:S(2)}, u32[]{:S(2)}) collective-permute-start(bf16[160,256]{1,0:T(8,128)(2,1)S(1)} %get-tuple-element.60), channel_id=1, source_target_pairs={{0,192},{16,208},{32,224},{48,240},{64,0},{80,16},{96,32},{112,48}... | collective-permute-start | bytes 245768 | tf_op jit(solution)/shard_map/ppermute | solution.py:497
  164.5 10.5 %collective-permute-start.15 = (bf16[160,256]{1,0:T(8,128)(2,1)S(1)}, bf16[160,256]{1,0:T(8,128)(2,1)S(1)}, u32[]{:S(2)}, u32[]{:S(2)}) collective-permute-start(bf16[160,256]{1,0:T(8,128)(2,1)S(1)} %get-tuple-element.59), channel_id=1, source_target_pairs={{0,224},{16,240},{32,0},{48,16},{64,32},{80,48},{96,64},{112,80},{... | collective-permute-start | bytes 245768 | tf_op jit(solution)/shard_map/ppermute | solution.py:497
  164.5 10.5 %collective-permute-start.9 = (bf16[160,256]{1,0:T(8,128)(2,1)S(1)}, bf16[160,256]{1,0:T(8,128)(2,1)S(1)}, u32[]{:S(2)}, u32[]{:S(2)}) collective-permute-start(bf16[160,256]{1,0:T(8,128)(2,1)S(1)} %get-tuple-element.58), channel_id=1, source_target_pairs={{0,32},{16,48},{32,64},{48,80},{64,96},{80,112},{96,128},{112,144}... | collective-permute-start | bytes 245768 | tf_op jit(solution)/shard_map/ppermute | solution.py:497
  (7 other events, 9.0 us)
Sparse Core Ops, SparseCore 0:
  9.9 112.1 all-gather.1

commit v4 on v3

--- a/solution.py
+++ b/solution.py
@@ -57,9 +57,10 @@
 
 def pack_kernel(gate_hbm, up_hbm, down_hbm, out_hbm, down, held, sems):
     half = gate_hbm.shape[1]
-    spans = [pl.ds(a * half, half) for a in range(3)]
+    most = down.shape[0]
+    spans = [pl.ds(0, half), pl.ds(half, half), pl.ds(2 * half, most)]
     loads = [
-        pltpu.make_async_copy(down_hbm, down, sems.at[0]),
+        pltpu.make_async_copy(down_hbm.at[pl.ds(0, most), :], down, sems.at[0]),
         pltpu.make_async_copy(gate_hbm, held.at[:, spans[0]], sems.at[1]),
         pltpu.make_async_copy(up_hbm, held.at[:, spans[1]], sems.at[2]),
     ]
@@ -150,20 +151,20 @@
 def assemble_kernel(where_ref, own_ref, other_ref, a1_ref, a2_ref):
     z, core = where_ref[0], where_ref[1]
     zs = own_ref.shape[0]
-    ranks = a2_ref.shape[0]
+    ranks, tall = a1_ref.shape[1], a2_ref.shape[0]
     share = a1_ref.shape[0] // (2 * zs)
     for i in range(zs):
         for ref, side in ((own_ref, core), (other_ref, 1 - core)):
             f = lax.rem(z + zs - i, zs) * 2 + side
-            a2_ref[:, pl.ds(pl.multiple_of(f * TILE, TILE), TILE)] = ref[i, :ranks, :]
+            a2_ref[:, pl.ds(pl.multiple_of(f * TILE, TILE), TILE)] = ref[i, :tall, :]
             at = pl.multiple_of(f * share, 16)
-            a1_ref[pl.ds(at, 16), :] = ref[i, ranks : ranks + 16, :ranks]
-            a1_ref[pl.ds(at + 16, 16), :] = ref[i, ranks : ranks + 16, ranks:]
-            a1_ref[pl.ds(at + 32, 16), :] = ref[i, ranks + 16 :, :ranks]
+            a1_ref[pl.ds(at, 16), :] = ref[i, tall : tall + 16, :ranks]
+            a1_ref[pl.ds(at + 16, 16), :] = ref[i, tall : tall + 16, ranks:]
+            a1_ref[pl.ds(at + 32, 16), :] = ref[i, tall + 16 :, :ranks]
 
 
 def prepare_kernel(
-    src_ref, a1_ref, a2_ref, dst_ref, mask_ref, gate_ref, low_ref, grad_ref, hga_ref
+    src_ref, a1_ref, a2_ref, dst_ref, mask_ref, gate_ref, low_ref, grad_ref, hga_ref, tail_ref
 ):
     unfold_rows(src_ref, dst_ref)
     slots = src_ref.shape[0]
@@ -178,7 +179,9 @@
         mask_ref[rows, :] = contract(block, tenant, 1, 0)
         gate_ref[rows, :] = contract(block, weight, 1, 0)
 
-    low = contract(dst_ref[...], a2_ref[...], 1, 1) * mask_ref[...]
+    both = contract(dst_ref[...], a2_ref[...], 1, 1)
+    tail_ref[...] = both[:, lanes:]
+    low = both[:, :lanes] * mask_ref[...]
     low_ref[...] = low
     grad = (ADAPTER_SCALE * gate_ref[...] * low).astype(bf16)
     grad_ref[...] = grad
@@ -186,7 +189,7 @@
 
 
 def expert_kernel(
-    x_hbm, c_hbm, w_hbm, a1_hbm, mask_hbm, gate_hbm, low_hbm, hga_hbm,
+    x_hbm, c_hbm, w_hbm, a1_hbm, mask_hbm, gate_hbm, low_hbm, hga_hbm, tail_hbm,
     rg_hbm, hid_hbm, lowt_hbm,
     xs, cs, w, a1_ref, mask_ref, gate_ref, low_ref, hga,
     rg_ref, hid, lowt_ref,
@@ -199,6 +202,7 @@
     spares = rows - slots
     wide = 2 * half
     depth = width // CHUNKS
+    packed = w.shape[1]
 
     pending = []
 
@@ -226,6 +230,7 @@
             (a1_hbm, a1_ref),
             (mask_hbm, mask_ref),
             (low_hbm, low_ref),
+            (tail_hbm, acc.at[:, pl.ds(packed, acc.shape[1] - packed)]),
         )
     ]
 
@@ -233,7 +238,7 @@
         cols = slice(q * depth, (q + 1) * depth)
         for copy in chunks[q]:
             copy.wait()
-        for rows_ref, out in ((xs, slice(0, wide)), (cs, slice(wide, None))):
+        for rows_ref, out in ((xs, slice(0, wide)), (cs, slice(wide, packed))):
             got = contract(rows_ref[:, cols], w[cols, out], 1, 0)
             if q == 0:
                 acc[:, out] = got
@@ -331,7 +336,7 @@
     slots = experts * MAIN
     spares = slots // QUARTERS
     rows = slots + spares
-    cols = 3 * half
+    cols = 3 * half - LANES
     shard = frozen_gate_weight.shape[1]
     zs = spread // 2
     here = lax.axis_index("fsdp")
@@ -344,20 +349,26 @@
         in_specs=[ANY] * 3,
         out_specs=ANY,
         scratch_shapes=[
-            pltpu.VMEM((half, shard), bf16),
+            pltpu.VMEM((half - LANES, shard), bf16),
             pltpu.VMEM((shard, cols), bf16),
             pltpu.SemaphoreType.DMA((6,)),
         ],
         compiler_params=pltpu.CompilerParams(vmem_limit_bytes=60 << 20),
     )(frozen_gate_weight[0], frozen_up_weight[0], frozen_down_weight[0])
-    packed, first_part, second_part = lax.optimization_barrier(
-        (packed, adapter_first_factors[0], adapter_second_factors[0])
+    packed, first_part, second_part, down_part = lax.optimization_barrier(
+        (
+            packed,
+            adapter_first_factors[0],
+            adapter_second_factors[0],
+            frozen_down_weight[0, half - LANES :],
+        )
     )
     first_rows = [first_part[a * 16 : (a + 1) * 16] for a in range(3)]
     first_rows.append(jnp.zeros_like(first_rows[0]))
     small = jnp.concatenate(
         [
             second_part,
+            down_part,
             jnp.concatenate(first_rows[:2], axis=1),
             jnp.concatenate(first_rows[2:], axis=1),
         ],
@@ -410,7 +421,7 @@
         name="assemble_adapters",
         out_shape=(
             jax.ShapeDtypeStruct((half, ranks), bf16),
-            jax.ShapeDtypeStruct((ranks, width), bf16),
+            jax.ShapeDtypeStruct((ranks + LANES, width), bf16),
         ),
         in_specs=[SMEM, VMEM, VMEM],
         out_specs=(VMEM, VMEM),
@@ -426,7 +437,7 @@
         out_specs=VMEM,
         compiler_params=pltpu.CompilerParams(vmem_limit_bytes=24 << 20),
     )(x_rows)
-    c_all, mask, gate, cot_low, low_grad, grad_low = pl.pallas_call(
+    c_all, mask, gate, cot_low, low_grad, grad_low, cot_tail = pl.pallas_call(
         prepare_kernel,
         name="prepare_cotangent",
         out_shape=(
@@ -436,9 +447,10 @@
             jax.ShapeDtypeStruct((rows, ranks), f32),
             jax.ShapeDtypeStruct((rows, ranks), bf16),
             jax.ShapeDtypeStruct((rows, half), f32),
+            jax.ShapeDtypeStruct((rows, LANES), f32),
         ),
         in_specs=[VMEM, VMEM, VMEM],
-        out_specs=(VMEM,) * 6,
+        out_specs=(VMEM,) * 7,
         compiler_params=pltpu.CompilerParams(vmem_limit_bytes=60 << 20),
     )(c_rows, first_full, second_full)
 
@@ -450,7 +462,7 @@
             jax.ShapeDtypeStruct((rows, half), bf16),
             jax.ShapeDtypeStruct((rows, ranks), bf16),
         ),
-        in_specs=[ANY] * 8,
+        in_specs=[ANY] * 9,
         out_specs=(ANY, ANY, ANY),
         scratch_shapes=[
             pltpu.VMEM((rows, width), bf16),
@@ -464,14 +476,14 @@
             pltpu.VMEM((slots, width + part + LANES), bf16),
             pltpu.VMEM((rows, half), bf16),
             pltpu.VMEM((rows, ranks), bf16),
-            pltpu.VMEM((rows, cols), f32),
+            pltpu.VMEM((rows, 3 * half), f32),
             pltpu.VMEM((rows, 2 * half), bf16),
             pltpu.VMEM((spares, width), bf16),
             pltpu.VMEM((rows, LANES), bf16),
-            pltpu.SemaphoreType.DMA((3 * CHUNKS + 8 + width // BACK,)),
+            pltpu.SemaphoreType.DMA((3 * CHUNKS + 9 + width // BACK,)),
         ],
         compiler_params=pltpu.CompilerParams(vmem_limit_bytes=LIMIT << 20),
-    )(x_all, c_all, weights, first_full, mask, gate, cot_low, grad_low)
+    )(x_all, c_all, weights, first_full, mask, gate, cot_low, grad_low, cot_tail)
 
     own, other = pl.pallas_call(
         adapter_kernel,

time: 197 us -> 197 us (level)
  blocking collectives: 36.6 us -> 0 us
  waiting for transfers between devices: 53.9 us -> 74 us
  starting transfers between devices: 44.4 us -> 53.4 us
  local copies, waits for them, and re-layouts: 11.9 us -> 16.4 us
    all_to_all x1 -> x0, blocking collectives: 36.6 us -> none  [exchange(): lax.all_to_all(block, 'expert', split_axis=0, concat_axis=0, tiled=True)]
    all_to_all x2 -> x3, waiting for transfers between devices: 18.5 us -> 39 us  [exchange(): lax.all_to_all(block, 'expert', split_axis=0, concat_axis=0, tiled=True)]
    all_to_all x2 -> x3, starting transfers between devices: 11.4 us -> 19.4 us  [exchange(): lax.all_to_all(block, 'expert', split_axis=0, concat_axis=0, tiled=True)]
    all_gather x1, waiting for transfers between devices: 15.1 us -> 7.21 us  [shards(): weights = lax.all_gather(packed, 'fsdp', axis=0, tiled=True)]
    ppermute x7, waiting for transfers between devices: 10.3 us -> 14.1 us  [along(): lax.ppermute(block, 'fsdp', [(f, (f + 2 * step) % spread) for f in range(...]
    unnamed x49 -> x51, local copies, waits for them, and re-layouts: 11.1 us -> 14 us
    ppermute x7, waiting for transfers between devices: 6.54 us -> 9.17 us  [shards(): total = total + lax.ppermute(halved[dz], 'fsdp', moves).astype(f32)]
    ppermute x1, starting transfers between devices: 5.53 us -> 7.64 us  [shards(): far = lax.ppermute(near, 'fsdp', swap)]
  transfers between devices with their start and end apart: 19 -> 20, of which waited for: 11 -> 14; matrix products, arithmetic and copies ran while one was open for 3% -> 4% of each run, Pallas kernels for 7% -> 7%
where the time goes in v4:
time: 197 us; the launch traced here: 196 us
  waiting for transfers between devices  74 us (38%)
  starting transfers between devices  53.4 us (27%)
  Pallas kernels  35.8 us (18%)
  local copies, waits for them, and re-layouts  16.4 us (8%)
  between operations  14.4 us (7%)
  other arithmetic  2.37 us (1%)
    all_to_all x3, waiting for transfers between devices, exchange(): lax.all_to_all(block, 'expert', split_axis=0, concat_axis=0, tiled=True)  39 us
    all_to_all x3, starting transfers between devices, exchange(): lax.all_to_all(block, 'expert', split_axis=0, concat_axis=0, tiled=True)  19.4 us
    pallas_call x1, Pallas kernels, shards(): pl.pallas_call(expert_kernel, name='expert', out_shape=(jax.ShapeDtypeStr...  17.5 us
    ppermute x7, waiting for transfers between devices, along(): lax.ppermute(block, 'fsdp', [(f, (f + 2 * step) % spread) for f in range(...  14.1 us
    unnamed x51, local copies, waits for them, and re-layouts  14 us
    ppermute x7, starting transfers between devices, shards(): total = total + lax.ppermute(halved[dz], 'fsdp', moves).astype(f32)  13.7 us
    ppermute x7, starting transfers between devices, along(): lax.ppermute(block, 'fsdp', [(f, (f + 2 * step) % spread) for f in range(...  12 us
    ppermute x7, waiting for transfers between devices, shards(): total = total + lax.ppermute(halved[dz], 'fsdp', moves).astype(f32)  9.17 us
  transfers between devices with their start and end apart: 20, of which 14 were waited for; matrix products, arithmetic and copies ran while one was open for 4% of the time, Pallas kernels for 7%

profile of v4, /device:TPU:1, one launch (start us, length us, event | category | flops | bytes accessed | tf_op | source)
XLA Modules:
  0.0 196.3 jit_solution(4440581294649022246)
XLA Ops:
  8.1 2.3 %pack_weights.1 = bf16[256,2176]{1,0:T(8,128)(2,1)} custom-call(bf16[256,768]{1,0:T(8,128)(2,1)} %bitcast.72, bf16[256,768]{1,0:T(8,128)(2,1)} %bitcast.73, bf16[768,256]{1,0:T(8,128)(2,1)} %bitcast.71), custom_call_target="tpu_custom_call" | custom-call | tf_op jit(solution)/shard_map/pack_weights/pallas_call | solution.py:345
  10.5 2.5 %collective-permute-start = (bf16[288,256]{1,0:T(8,128)(2,1)S(1)}, bf16[288,256]{1,0:T(8,128)(2,1)S(1)}, u32[]{:S(2)}, u32[]{:S(2)}) collective-permute-start(bf16[288,256]{1,0:T(8,128)(2,1)S(1)} %fusion.8), channel_id=1, source_target_pairs={{0,32},{16,48},{32,64},{48,80},{64,96},{80,112},{96,128},{112,144}... | collective-permute-start | bytes 442376 | tf_op jit(solution)/shard_map/ppermute | solution.py:403
  13.1 4.0 %collective-permute-start.3 = (bf16[288,256]{1,0:T(8,128)(2,1)S(1)}, bf16[288,256]{1,0:T(8,128)(2,1)S(1)}, u32[]{:S(2)}, u32[]{:S(2)}) collective-permute-start(bf16[288,256]{1,0:T(8,128)(2,1)S(1)} %fusion.8), channel_id=1, source_target_pairs={{0,224},{16,240},{32,0},{48,16},{64,32},{80,48},{96,64},{112,80},{... | collective-permute-start | bytes 442376 | tf_op jit(solution)/shard_map/ppermute | solution.py:403
  17.1 3.5 %collective-permute-done = bf16[288,256]{1,0:T(8,128)(2,1)S(1)} collective-permute-done((bf16[288,256]{1,0:T(8,128)(2,1)S(1)}, bf16[288,256]{1,0:T(8,128)(2,1)S(1)}, u32[]{:S(2)}, u32[]{:S(2)}) %collective-permute-start) | collective-permute-done | bytes 147488 | tf_op jit(solution)/shard_map/ppermute | solution.py:403
  20.6 2.7 %collective-permute-start.4 = (bf16[288,256]{1,0:T(8,128)(2,1)S(1)}, bf16[288,256]{1,0:T(8,128)(2,1)S(1)}, u32[]{:S(2)}, u32[]{:S(2)}) collective-permute-start(bf16[288,256]{1,0:T(8,128)(2,1)S(1)} %collective-permute-done.3), channel_id=1, source_target_pairs={{0,224},{16,240},{32,0},{48,16},{64,32},{80,48},{96,64},{112,80},{... | collective-permute-start | bytes 442376 | tf_op jit(solution)/shard_map/ppermute | solution.py:403
  23.3 2.5 %collective-permute-done.1 = bf16[288,256]{1,0:T(8,128)(2,1)S(1)} collective-permute-done((bf16[288,256]{1,0:T(8,128)(2,1)S(1)}, bf16[288,256]{1,0:T(8,128)(2,1)S(1)}, u32[]{:S(2)}, u32[]{:S(2)}) %collective-permute-start.1) | collective-permute-done | bytes 147488 | tf_op jit(solution)/shard_map/ppermute | solution.py:403
  25.8 2.7 %collective-permute-start.5 = (bf16[288,256]{1,0:T(8,128)(2,1)S(1)}, bf16[288,256]{1,0:T(8,128)(2,1)S(1)}, u32[]{:S(2)}, u32[]{:S(2)}) collective-permute-start(bf16[288,256]{1,0:T(8,128)(2,1)S(1)} %collective-permute-done.4), channel_id=1, source_target_pairs={{0,224},{16,240},{32,0},{48,16},{64,32},{80,48},{96,64},{112,80},{... | collective-permute-start | bytes 442376 | tf_op jit(solution)/shard_map/ppermute | solution.py:403
  29.0 2.9 %shard_map.129 = (bf16[256,5120]{1,0:T(8,128)(2,1)S(1)}, bf16[256,5248]{1,0:T(8,128)(2,1)S(1)}) custom-call(s32[128,2]{1,0:T(8,128)S(1)} %copy.17.refs_0_, bf16[128,2]{1,0:T(8,128)(2,1)S(1)} %copy.15.refs_1_, s32[128,1]{1,0:T(8,128)S(1)} %copy.16.refs_2_, bf16[128,4096]{1,0:T(8,128)(2,1)S(1)} %copy-done.5, bf16[128,4096]{1,0:T(8,128)(2,1)S(1)} %copy-done.6), custom_call_target="tpu_custom_call" | custom-call | tf_op jit(solution)/shard_map/pallas_call | solution.py:379
  31.9 1.5 copy-done.2
  35.6 6.7 %all-to-all-start = ((bf16[16,16,5120]{2,1,0:T(8,128)(2,1)}), bf16[16,16,5120]{2,1,0:T(8,128)(2,1)S(1)}, u32[]{:S(2)}, u32[]{:S(2)}) async-start(bf16[16,16,5120]{2,1,0:T(8,128)(2,1)} %bitcast.69), calls=%async_computation | async-start | bytes 5242880 | tf_op jit(solution)/shard_map/all_to_all | solution.py:398
  44.4 27.7 %all-to-all-done = bf16[16,16,5120]{2,1,0:T(8,128)(2,1)S(1)} async-done(((bf16[16,16,5120]{2,1,0:T(8,128)(2,1)}), bf16[16,16,5120]{2,1,0:T(8,128)(2,1)S(1)}, u32[]{:S(2)}, u32[]{:S(2)}) %all-to-all-start) | async-done | bytes 2621472 | tf_op jit(solution)/shard_map/all_to_all | solution.py:398
  72.2 6.0 %all-to-all-start.1 = ((bf16[16,16,5248]{2,1,0:T(8,128)(2,1)}), bf16[16,16,5248]{2,1,0:T(8,128)(2,1)}, u32[]{:S(2)}, u32[]{:S(2)}) async-start(bf16[16,16,5248]{2,1,0:T(8,128)(2,1)} %bitcast.68), calls=%async_computation.1 | async-start | bytes 5373952 | tf_op jit(solution)/shard_map/all_to_all | solution.py:398
  79.6 8.1 %collective-permute-done.6 = bf16[288,256]{1,0:T(8,128)(2,1)S(1)} collective-permute-done((bf16[288,256]{1,0:T(8,128)(2,1)S(1)}, bf16[288,256]{1,0:T(8,128)(2,1)S(1)}, u32[]{:S(2)}, u32[]{:S(2)}) %collective-permute-start.6) | collective-permute-done | bytes 147488 | tf_op jit(solution)/shard_map/ppermute | solution.py:403
  90.3 7.6 %collective-permute-start.7 = (bf16[8,288,256]{2,1,0:T(8,128)(2,1)}, bf16[8,288,256]{2,1,0:T(8,128)(2,1)}, u32[]{:S(2)}, u32[]{:S(2)}) collective-permute-start(bf16[8,288,256]{2,1,0:T(8,128)(2,1)} %bitcast_dynamic-update-slice_fusion.own_ref), channel_id=1, source_target_pairs={{0,16},{16,0},{32,48},{48,32},{64,80},{80,64},{96,112},{112,96},{1... | collective-permute-start | bytes 3538952 | tf_op jit(solution)/shard_map/ppermute | solution.py:418
  98.0 2.7 %collective-permute-done.7.other_ref = bf16[8,288,256]{2,1,0:T(8,128)(2,1)} collective-permute-done((bf16[8,288,256]{2,1,0:T(8,128)(2,1)}, bf16[8,288,256]{2,1,0:T(8,128)(2,1)}, u32[]{:S(2)}, u32[]{:S(2)}) %collective-permute-start.7) | collective-permute-done | bytes 1179680 | tf_op jit(solution)/shard_map/ppermute | solution.py:418
  100.7 1.9 assemble_adapters.1
  105.5 1.6 copy-done.1
  107.0 1.6 all-to-all-done.1
  108.6 5.7 %prepare_cotangent.1 = (bf16[320,4096]{1,0:T(8,128)(2,1)}, f32[320,128]{1,0:T(8,128)}, f32[320,128]{1,0:T(8,128)}, f32[320,128]{1,0:T(8,128)}, bf16[320,128]{1,0...) custom-call(bf16[256,5248]{1,0:T(8,128)(2,1)} %bitcast.10.src_ref, bf16[768,128]{1,0:T(8,128)(2,1)} %copy-done.7, ...), custom_call_target="tpu_custom_call" | custom-call | tf_op jit(solution)/shard_map/prepare_cotangent/pallas_call | solution.py:440
  114.3 7.2 %all-gather.2.cloned.1.call-done.w_hbm = bf16[4096,2176]{1,0:T(8,128)(2,1)} async-done(((bf16[256,2176]{1,0:T(8,128)(2,1)}), bf16[4096,2176]{1,0:T(8,128)(2,1)}) %all-gather.2.cloned.1.call-update) | async-done | bytes 17825808 | tf_op jit(solution)/shard_map/all_gather | solution.py:377
  121.5 17.5 %expert.1 = (bf16[256,5248]{1,0:T(8,128)(2,1)}, bf16[320,768]{1,0:T(8,128)(2,1)}, bf16[320,128]{1,0:T(8,128)(2,1)}) custom-call(bf16[320,4096]{1,0:T(8,128)(2,1)} %copy-done.1, bf16[320,4096]{1,0:T(8,128)(2,1)} %get-tuple-element.41.c_hbm.c_ref, bf16[4096,2176]{1,0:T(8,128)(2,1)} %all-gather.2.cloned.1.call-done.w_hbm, bf16[768,128]{1,0:T(8,128)(2,1)} %copy-done.7, ...), custom_call_target="tpu_custom_call" | custom-call | tf_op jit(solution)/shard_map/expert/pallas_call | solution.py:457
  139.0 6.7 %all-to-all-start.2 = ((bf16[16,16,5248]{2,1,0:T(8,128)(2,1)}), bf16[16,16,5248]{2,1,0:T(8,128)(2,1)S(1)}, u32[]{:S(2)}, u32[]{:S(2)}) async-start(bf16[16,16,5248]{2,1,0:T(8,128)(2,1)} %bitcast.70), calls=%async_computation.2 | async-start | bytes 5373952 | tf_op jit(solution)/shard_map/all_to_all | solution.py:398
  145.7 1.7 copy-done
  147.5 2.8 %adapters.1 = (bf16[8,160,256]{2,1,0:T(8,128)(2,1)S(1)}, bf16[8,160,256]{2,1,0:T(8,128)(2,1)S(1)}) custom-call(s32[2]{0:T(128)S(1)} %pad_add_fusion.where_ref, bf16[320,768]{1,0:T(8,128)(2,1)S(1)} %copy-done.8, bf16[320,128]{1,0:T(8,128)(2,1)S(1)} %copy-done.9, bf16[320,128]{1,0:T(8,128)(2,1)S(1)} %copy-done.10, bf16[320,4096]{1,0:T(8,128)(2,1)S(1)} %copy-done), custom_call_target="tpu_custom_call" | custom-call | flops 400000000 | bytes 6000000 | tf_op jit(solution)/shard_map/adapters/pallas_call | solution.py:488
  150.9 1.7 collective-permute-done.8
  154.3 3.5 %collective-permute-start.11 = (bf16[160,256]{1,0:T(8,128)(2,1)S(1)}, bf16[160,256]{1,0:T(8,128)(2,1)S(1)}, u32[]{:S(2)}, u32[]{:S(2)}) collective-permute-start(bf16[160,256]{1,0:T(8,128)(2,1)S(1)} %get-tuple-element.67), channel_id=1, source_target_pairs={{0,96},{16,112},{32,128},{48,144},{64,160},{80,176},{96,192},{112,... | collective-permute-start | bytes 245768 | tf_op jit(solution)/shard_map/ppermute | solution.py:509
  157.9 4.4 %collective-permute-start.13 = (bf16[160,256]{1,0:T(8,128)(2,1)S(1)}, bf16[160,256]{1,0:T(8,128)(2,1)S(1)}, u32[]{:S(2)}, u32[]{:S(2)}) collective-permute-start(bf16[160,256]{1,0:T(8,128)(2,1)S(1)} %get-tuple-element.65), channel_id=1, source_target_pairs={{0,160},{16,176},{32,192},{48,208},{64,224},{80,240},{96,0},{112,1... | collective-permute-start | bytes 245768 | tf_op jit(solution)/shard_map/ppermute | solution.py:509
  162.2 3.5 %collective-permute-start.14 = (bf16[160,256]{1,0:T(8,128)(2,1)S(1)}, bf16[160,256]{1,0:T(8,128)(2,1)S(1)}, u32[]{:S(2)}, u32[]{:S(2)}) collective-permute-start(bf16[160,256]{1,0:T(8,128)(2,1)S(1)} %get-tuple-element.64), channel_id=1, source_target_pairs={{0,192},{16,208},{32,224},{48,240},{64,0},{80,16},{96,32},{112,48}... | collective-permute-start | bytes 245768 | tf_op jit(solution)/shard_map/ppermute | solution.py:509
  168.2 1.7 collective-permute-done.13
  169.9 5.8 %collective-permute-done.14 = bf16[160,256]{1,0:T(8,128)(2,1)S(1)} collective-permute-done((bf16[160,256]{1,0:T(8,128)(2,1)S(1)}, bf16[160,256]{1,0:T(8,128)(2,1)S(1)}, u32[]{:S(2)}, u32[]{:S(2)}) %collective-permute-start.14) | collective-permute-done | bytes 81952 | tf_op jit(solution)/shard_map/ppermute | solution.py:509
  177.1 9.7 %all-to-all-done.2 = bf16[16,16,5248]{2,1,0:T(8,128)(2,1)S(1)} async-done(((bf16[16,16,5248]{2,1,0:T(8,128)(2,1)}), bf16[16,16,5248]{2,1,0:T(8,128)(2,1)S(1)}, u32[]{:S(2)}, u32[]{:S(2)}) %all-to-all-start.2) | async-done | bytes 2687008 | tf_op jit(solution)/shard_map/all_to_all | solution.py:398
  186.8 2.1 %shard_map.130 = (bf16[128,4096]{1,0:T(8,128)(2,1)}, bf16[128,2]{1,0:T(8,128)(2,1)S(1)}) custom-call(s32[128,2]{1,0:T(8,128)S(1)} %copy.17.refs_0_, bf16[256,5248]{1,0:T(8,128)(2,1)S(1)} %bitcast.66), custom_call_target="tpu_custom_call" | custom-call | tf_op jit(solution)/shard_map/pallas_call | solution.py:520
  (81 shorter events, 19.4 us)
Async XLA Ops:
  7.2 114.3 %all-gather.2.cloned.1.call-start = ((), (), s32[]{:S(2)}) async-start(), calls=%async_computation.3 | async-start | bytes 18939904 | tf_op jit(solution)/shard_map/all_gather | solution.py:377
  8.1 20.9 %copy-start.6 = (bf16[128,4096]{1,0:T(8,128)(2,1)S(1)}, bf16[128,4096]{1,0:T(8,128)(2,1)}, u32[]{:S(2)}) copy-start(bf16[128,4096]{1,0:T(8,128)(2,1)} %refs_4_.1) | copy-start | bytes 3145732
  10.4 18.2 %copy-start.18 = (s32[128,2]{0,1:T(2,128)S(1)}, s32[128,2]{0,1:T(2,128)}, u32[]{:S(2)}) copy-start(s32[128,2]{0,1:T(2,128)} %param.12) | copy-start | bytes 3076
  10.4 18.3 %copy-start.19 = (s32[128]{0:T(128)S(1)}, s32[128]{0:T(128)}, u32[]{:S(2)}) copy-start(s32[128]{0:T(128)} %param.14) | copy-start | bytes 1540
  10.4 18.4 %copy-start.20 = (bf16[128,2]{0,1:T(2,128)(2,1)S(1)}, bf16[128,2]{0,1:T(2,128)(2,1)}, u32[]{:S(2)}) copy-start(bf16[128,2]{0,1:T(2,128)(2,1)} %param.13) | copy-start | bytes 1540
  10.4 18.5 %copy-start.5 = (bf16[128,4096]{1,0:T(8,128)(2,1)S(1)}, bf16[128,4096]{1,0:T(8,128)(2,1)}, u32[]{:S(2)}) copy-start(bf16[128,4096]{1,0:T(8,128)(2,1)} %refs_3_.1) | copy-start | bytes 3145732
  10.5 15.3 %copy-start.14 = (bf16[16,128]{1,0:T(8,128)(2,1)}, bf16[16,128]{1,0:T(8,128)(2,1)S(1)}, u32[]{:S(2)}) copy-start(bf16[16,128]{1,0:T(8,128)(2,1)S(1)} %get-tuple-element.72) | copy-start | bytes 12292
  10.5 15.3 %copy-start.15 = (bf16[16,128]{1,0:T(8,128)(2,1)}, bf16[16,128]{1,0:T(8,128)(2,1)S(1)}, u32[]{:S(2)}) copy-start(bf16[16,128]{1,0:T(8,128)(2,1)S(1)} %get-tuple-element.73) | copy-start | bytes 12292
  10.5 15.3 %copy-start.16 = (bf16[16,128]{1,0:T(8,128)(2,1)}, bf16[16,128]{1,0:T(8,128)(2,1)S(1)}, u32[]{:S(2)}) copy-start(bf16[16,128]{1,0:T(8,128)(2,1)S(1)} %get-tuple-element.74) | copy-start | bytes 12292
  10.5 10.1 %collective-permute-start = (bf16[288,256]{1,0:T(8,128)(2,1)S(1)}, bf16[288,256]{1,0:T(8,128)(2,1)S(1)}, u32[]{:S(2)}, u32[]{:S(2)}) collective-permute-start(bf16[288,256]{1,0:T(8,128)(2,1)S(1)} %fusion.8), channel_id=1, source_target_pairs={{0,32},{16,48},{32,64},{48,80},{64,96},{80,112},{96,128},{112,144}... | collective-permute-start | bytes 442376 | tf_op jit(solution)/shard_map/ppermute | solution.py:403
  13.1 7.5 %collective-permute-start.3 = (bf16[288,256]{1,0:T(8,128)(2,1)S(1)}, bf16[288,256]{1,0:T(8,128)(2,1)S(1)}, u32[]{:S(2)}, u32[]{:S(2)}) collective-permute-start(bf16[288,256]{1,0:T(8,128)(2,1)S(1)} %fusion.8), channel_id=1, source_target_pairs={{0,224},{16,240},{32,0},{48,16},{64,32},{80,48},{96,64},{112,80},{... | collective-permute-start | bytes 442376 | tf_op jit(solution)/shard_map/ppermute | solution.py:403
  20.6 5.2 %collective-permute-start.1 = (bf16[288,256]{1,0:T(8,128)(2,1)S(1)}, bf16[288,256]{1,0:T(8,128)(2,1)S(1)}, u32[]{:S(2)}, u32[]{:S(2)}) collective-permute-start(bf16[288,256]{1,0:T(8,128)(2,1)S(1)} %collective-permute-done), channel_id=1, source_target_pairs={{0,32},{16,48},{32,64},{48,80},{64,96},{80,112},{96,128},{112,144}... | collective-permute-start | bytes 442376 | tf_op jit(solution)/shard_map/ppermute | solution.py:403
  20.6 5.2 %collective-permute-start.4 = (bf16[288,256]{1,0:T(8,128)(2,1)S(1)}, bf16[288,256]{1,0:T(8,128)(2,1)S(1)}, u32[]{:S(2)}, u32[]{:S(2)}) collective-permute-start(bf16[288,256]{1,0:T(8,128)(2,1)S(1)} %collective-permute-done.3), channel_id=1, source_target_pairs={{0,224},{16,240},{32,0},{48,16},{64,32},{80,48},{96,64},{112,80},{... | collective-permute-start | bytes 442376 | tf_op jit(solution)/shard_map/ppermute | solution.py:403
  25.8 9.2 %collective-permute-start.2 = (bf16[288,256]{1,0:T(8,128)(2,1)S(1)}, bf16[288,256]{1,0:T(8,128)(2,1)S(1)}, u32[]{:S(2)}, u32[]{:S(2)}) collective-permute-start(bf16[288,256]{1,0:T(8,128)(2,1)S(1)} %collective-permute-done.1), channel_id=1, source_target_pairs={{0,32},{16,48},{32,64},{48,80},{64,96},{80,112},{96,128},{112,144}... | collective-permute-start | bytes 442376 | tf_op jit(solution)/shard_map/ppermute | solution.py:403
  25.8 9.1 %collective-permute-start.5 = (bf16[288,256]{1,0:T(8,128)(2,1)S(1)}, bf16[288,256]{1,0:T(8,128)(2,1)S(1)}, u32[]{:S(2)}, u32[]{:S(2)}) collective-permute-start(bf16[288,256]{1,0:T(8,128)(2,1)S(1)} %collective-permute-done.4), channel_id=1, source_target_pairs={{0,224},{16,240},{32,0},{48,16},{64,32},{80,48},{96,64},{112,80},{... | collective-permute-start | bytes 442376 | tf_op jit(solution)/shard_map/ppermute | solution.py:403
  35.6 36.5 %all-to-all-start = ((bf16[16,16,5120]{2,1,0:T(8,128)(2,1)}), bf16[16,16,5120]{2,1,0:T(8,128)(2,1)S(1)}, u32[]{:S(2)}, u32[]{:S(2)}) async-start(bf16[16,16,5120]{2,1,0:T(8,128)(2,1)} %bitcast.69), calls=%async_computation | async-start | bytes 5242880 | tf_op jit(solution)/shard_map/all_to_all | solution.py:398
  72.2 6.7 %copy-start.13 = (bf16[288,256]{1,0:T(8,128)(2,1)S(1)}, bf16[288,256]{1,0:T(8,128)(2,1)}, u32[]{:S(2)}) copy-start(bf16[288,256]{1,0:T(8,128)(2,1)} %copy-done.12) | copy-start | bytes 442372
  72.2 36.5 %all-to-all-start.1 = ((bf16[16,16,5248]{2,1,0:T(8,128)(2,1)}), bf16[16,16,5248]{2,1,0:T(8,128)(2,1)}, u32[]{:S(2)}, u32[]{:S(2)}) async-start(bf16[16,16,5248]{2,1,0:T(8,128)(2,1)} %bitcast.68), calls=%async_computation.1 | async-start | bytes 5373952 | tf_op jit(solution)/shard_map/all_to_all | solution.py:398
  78.9 8.7 %collective-permute-start.6 = (bf16[288,256]{1,0:T(8,128)(2,1)S(1)}, bf16[288,256]{1,0:T(8,128)(2,1)S(1)}, u32[]{:S(2)}, u32[]{:S(2)}) collective-permute-start(bf16[288,256]{1,0:T(8,128)(2,1)S(1)} %copy-done.13), channel_id=1, source_target_pairs={{0,32},{16,48},{32,64},{48,80},{64,96},{80,112},{96,128},{112,144}... | collective-permute-start | bytes 442376 | tf_op jit(solution)/shard_map/ppermute | solution.py:403
  90.3 10.5 %collective-permute-start.7 = (bf16[8,288,256]{2,1,0:T(8,128)(2,1)}, bf16[8,288,256]{2,1,0:T(8,128)(2,1)}, u32[]{:S(2)}, u32[]{:S(2)}) collective-permute-start(bf16[8,288,256]{2,1,0:T(8,128)(2,1)} %bitcast_dynamic-update-slice_fusion.own_ref), channel_id=1, source_target_pairs={{0,16},{16,0},{32,48},{48,32},{64,80},{80,64},{96,112},{112,96},{1... | collective-permute-start | bytes 3538952 | tf_op jit(solution)/shard_map/ppermute | solution.py:418
  139.0 6.7 %copy-start.8 = (bf16[320,768]{1,0:T(8,128)(2,1)S(1)}, bf16[320,768]{1,0:T(8,128)(2,1)}, u32[]{:S(2)}) copy-start(bf16[320,768]{1,0:T(8,128)(2,1)} %get-tuple-element.51.hid_ref) | copy-start | bytes 1474564
  139.0 6.7 %copy-start.9 = (bf16[320,128]{1,0:T(8,128)(2,1)S(1)}, bf16[320,128]{1,0:T(8,128)(2,1)}, u32[]{:S(2)}) copy-start(bf16[320,128]{1,0:T(8,128)(2,1)} %get-tuple-element.52.low_grad_ref) | copy-start | bytes 245764
  139.0 6.7 %copy-start.10 = (bf16[320,128]{1,0:T(8,128)(2,1)S(1)}, bf16[320,128]{1,0:T(8,128)(2,1)}, u32[]{:S(2)}) copy-start(bf16[320,128]{1,0:T(8,128)(2,1)} %get-tuple-element.53.lowt_ref) | copy-start | bytes 245764
  139.0 47.7 %all-to-all-start.2 = ((bf16[16,16,5248]{2,1,0:T(8,128)(2,1)}), bf16[16,16,5248]{2,1,0:T(8,128)(2,1)S(1)}, u32[]{:S(2)}, u32[]{:S(2)}) async-start(bf16[16,16,5248]{2,1,0:T(8,128)(2,1)} %bitcast.70), calls=%async_computation.2 | async-start | bytes 5373952 | tf_op jit(solution)/shard_map/all_to_all | solution.py:398
  150.3 2.3 %collective-permute-start.8 = (bf16[8,160,256]{2,1,0:T(8,128)(2,1)S(1)}, bf16[8,160,256]{2,1,0:T(8,128)(2,1)S(1)}, u32[]{:S(2)}, u32[]{:S(2)}) collective-permute-start(bf16[8,160,256]{2,1,0:T(8,128)(2,1)S(1)} %get-tuple-element.55), channel_id=1, source_target_pairs={{0,16},{16,0},{32,48},{48,32},{64,80},{80,64},{96,112},{112,96},{1... | collective-permute-start | bytes 1966088 | tf_op jit(solution)/shard_map/ppermute | solution.py:504
  152.8 12.9 %collective-permute-start.10 = (bf16[160,256]{1,0:T(8,128)(2,1)S(1)}, bf16[160,256]{1,0:T(8,128)(2,1)S(1)}, u32[]{:S(2)}, u32[]{:S(2)}) collective-permute-start(bf16[160,256]{1,0:T(8,128)(2,1)S(1)} %get-tuple-element.68), channel_id=1, source_target_pairs={{0,64},{16,80},{32,96},{48,112},{64,128},{80,144},{96,160},{112,17... | collective-permute-start | bytes 245768 | tf_op jit(solution)/shard_map/ppermute | solution.py:509
  154.3 12.8 %collective-permute-start.11 = (bf16[160,256]{1,0:T(8,128)(2,1)S(1)}, bf16[160,256]{1,0:T(8,128)(2,1)S(1)}, u32[]{:S(2)}, u32[]{:S(2)}) collective-permute-start(bf16[160,256]{1,0:T(8,128)(2,1)S(1)} %get-tuple-element.67), channel_id=1, source_target_pairs={{0,96},{16,112},{32,128},{48,144},{64,160},{80,176},{96,192},{112,... | collective-permute-start | bytes 245768 | tf_op jit(solution)/shard_map/ppermute | solution.py:509
  157.9 10.3 %collective-permute-start.12 = (bf16[160,256]{1,0:T(8,128)(2,1)S(1)}, bf16[160,256]{1,0:T(8,128)(2,1)S(1)}, u32[]{:S(2)}, u32[]{:S(2)}) collective-permute-start(bf16[160,256]{1,0:T(8,128)(2,1)S(1)} %get-tuple-element.66), channel_id=1, source_target_pairs={{0,128},{16,144},{32,160},{48,176},{64,192},{80,208},{96,224},{112... | collective-permute-start | bytes 245768 | tf_op jit(solution)/shard_map/ppermute | solution.py:509
  157.9 12.1 %collective-permute-start.13 = (bf16[160,256]{1,0:T(8,128)(2,1)S(1)}, bf16[160,256]{1,0:T(8,128)(2,1)S(1)}, u32[]{:S(2)}, u32[]{:S(2)}) collective-permute-start(bf16[160,256]{1,0:T(8,128)(2,1)S(1)} %get-tuple-element.65), channel_id=1, source_target_pairs={{0,160},{16,176},{32,192},{48,208},{64,224},{80,240},{96,0},{112,1... | collective-permute-start | bytes 245768 | tf_op jit(solution)/shard_map/ppermute | solution.py:509
  162.2 13.5 %collective-permute-start.14 = (bf16[160,256]{1,0:T(8,128)(2,1)S(1)}, bf16[160,256]{1,0:T(8,128)(2,1)S(1)}, u32[]{:S(2)}, u32[]{:S(2)}) collective-permute-start(bf16[160,256]{1,0:T(8,128)(2,1)S(1)} %get-tuple-element.64), channel_id=1, source_target_pairs={{0,192},{16,208},{32,224},{48,240},{64,0},{80,16},{96,32},{112,48}... | collective-permute-start | bytes 245768 | tf_op jit(solution)/shard_map/ppermute | solution.py:509
  165.7 10.0 %collective-permute-start.15 = (bf16[160,256]{1,0:T(8,128)(2,1)S(1)}, bf16[160,256]{1,0:T(8,128)(2,1)S(1)}, u32[]{:S(2)}, u32[]{:S(2)}) collective-permute-start(bf16[160,256]{1,0:T(8,128)(2,1)S(1)} %get-tuple-element.63), channel_id=1, source_target_pairs={{0,224},{16,240},{32,0},{48,16},{64,32},{80,48},{96,64},{112,80},{... | collective-permute-start | bytes 245768 | tf_op jit(solution)/shard_map/ppermute | solution.py:509
  167.2 8.5 %collective-permute-start.9 = (bf16[160,256]{1,0:T(8,128)(2,1)S(1)}, bf16[160,256]{1,0:T(8,128)(2,1)S(1)}, u32[]{:S(2)}, u32[]{:S(2)}) collective-permute-start(bf16[160,256]{1,0:T(8,128)(2,1)S(1)} %get-tuple-element.62), channel_id=1, source_target_pairs={{0,32},{16,48},{32,64},{48,80},{64,96},{80,112},{96,128},{112,144}... | collective-permute-start | bytes 245768 | tf_op jit(solution)/shard_map/ppermute | solution.py:509
  (9 other events, 14.0 us)
Sparse Core Ops, SparseCore 0:
  10.6 110.8 all-gather.1

commit v5 on v4

--- a/solution.py
+++ b/solution.py
@@ -360,7 +360,7 @@
             packed,
             adapter_first_factors[0],
             adapter_second_factors[0],
-            frozen_down_weight[0, half - LANES :],
+            frozen_down_weight[0],
         )
     )
     first_rows = [first_part[a * 16 : (a + 1) * 16] for a in range(3)]
@@ -368,7 +368,7 @@
     small = jnp.concatenate(
         [
             second_part,
-            down_part,
+            down_part[half - LANES :],
             jnp.concatenate(first_rows[:2], axis=1),
             jnp.concatenate(first_rows[2:], axis=1),
         ],
@@ -406,14 +406,16 @@
 
     swap = [(f, f ^ 1) for f in range(spread)]
     low_side, high_side = [small], [small]
-    for _ in range(zs // 2 - 1):
+    for _ in range(2):
         low_side.append(along(low_side[-1], 1))
-    for _ in range(zs - zs // 2 - 1):
         high_side.append(along(high_side[-1], -1))
-    x_send, c_send, low_side[3], high_side[3] = lax.optimization_barrier(
-        (x_send, c_send, low_side[3], high_side[3])
-    )
-    low_side.append(along(low_side[-1], 1))
+    x_send, c_send, low_side[2], high_side[2] = lax.optimization_barrier(
+        (x_send, c_send, low_side[2], high_side[2])
+    )
+    for _ in range(zs // 2 - 2):
+        low_side.append(along(low_side[-1], 1))
+    for _ in range(zs - zs // 2 - 3):
+        high_side.append(along(high_side[-1], -1))
     near = jnp.stack(low_side + high_side[:0:-1])
     far = lax.ppermute(near, "fsdp", swap)
     first_full, second_full = pl.pallas_call(

time: 197 us -> 196 us (level)
  starting transfers between devices: 53.4 us -> 48.3 us
  waiting for transfers between devices: 74 us -> 78.9 us
    all_to_all x3, waiting for transfers between devices: 39 us -> 52.9 us  [exchange(): lax.all_to_all(block, 'expert', split_axis=0, concat_axis=0, tiled=True)]
    all_gather x1, waiting for transfers between devices: 7.21 us -> 1.64 us  [shards(): weights = lax.all_gather(packed, 'fsdp', axis=0, tiled=True)]
    ppermute x1, starting transfers between devices: 7.64 us -> 2.8 us  [shards(): far = lax.ppermute(near, 'fsdp', swap)]
    unnamed x51 -> x43, local copies, waits for them, and re-layouts: 14 us -> 14.5 us
  transfers between devices with their start and end apart: 20 -> 20, of which waited for: 14 -> 11; matrix products, arithmetic and copies ran while one was open for 4% -> 4% of each run, Pallas kernels for 7% -> 7%
where the time goes in v5:
time: 196 us; the launch traced here: 195 us
  waiting for transfers between devices  78.9 us (40%)
  starting transfers between devices  48.3 us (25%)
  Pallas kernels  35.3 us (18%)
  local copies, waits for them, and re-layouts  16.9 us (9%)
  between operations  14.3 us (7%)
    all_to_all x3, waiting for transfers between devices, exchange(): lax.all_to_all(block, 'expert', split_axis=0, concat_axis=0, tiled=True)  52.9 us
    all_to_all x3, starting transfers between devices, exchange(): lax.all_to_all(block, 'expert', split_axis=0, concat_axis=0, tiled=True)  19.1 us
    pallas_call x1, Pallas kernels, shards(): pl.pallas_call(expert_kernel, name='expert', out_shape=(jax.ShapeDtypeStr...  17.4 us
    unnamed x43, local copies, waits for them, and re-layouts  14.5 us
    ppermute x7, starting transfers between devices, shards(): total = total + lax.ppermute(halved[dz], 'fsdp', moves).astype(f32)  13.9 us
    ppermute x7, waiting for transfers between devices, along(): lax.ppermute(block, 'fsdp', [(f, (f + 2 * step) % spread) for f in range(...  12.3 us
    ppermute x7, starting transfers between devices, along(): lax.ppermute(block, 'fsdp', [(f, (f + 2 * step) % spread) for f in range(...  11.9 us
    ppermute x7, waiting for transfers between devices, shards(): total = total + lax.ppermute(halved[dz], 'fsdp', moves).astype(f32)  7.34 us
  transfers between devices with their start and end apart: 20, of which 11 were waited for; matrix products, arithmetic and copies ran while one was open for 4% of the time, Pallas kernels for 7%

profile of v5, /device:TPU:1, one launch (start us, length us, event | category | flops | bytes accessed | tf_op | source)
XLA Modules:
  0.0 195.4 jit_solution(5482765027192357680)
XLA Ops:
  7.2 2.3 %pack_weights.1 = bf16[256,2176]{1,0:T(8,128)(2,1)} custom-call(bf16[256,768]{1,0:T(8,128)(2,1)} %bitcast.71, bf16[256,768]{1,0:T(8,128)(2,1)} %bitcast.72, bf16[768,256]{1,0:T(8,128)(2,1)} %bitcast.69), custom_call_target="tpu_custom_call" | custom-call | tf_op jit(solution)/shard_map/pack_weights/pallas_call | solution.py:345
  10.6 2.5 %collective-permute-start = (bf16[288,256]{1,0:T(8,128)(2,1)S(1)}, bf16[288,256]{1,0:T(8,128)(2,1)S(1)}, u32[]{:S(2)}, u32[]{:S(2)}) collective-permute-start(bf16[288,256]{1,0:T(8,128)(2,1)S(1)} %fusion.8), channel_id=1, source_target_pairs={{0,32},{16,48},{32,64},{48,80},{64,96},{80,112},{96,128},{112,144}... | collective-permute-start | bytes 442376 | tf_op jit(solution)/shard_map/ppermute | solution.py:403
  13.1 4.0 %collective-permute-start.2 = (bf16[288,256]{1,0:T(8,128)(2,1)S(1)}, bf16[288,256]{1,0:T(8,128)(2,1)S(1)}, u32[]{:S(2)}, u32[]{:S(2)}) collective-permute-start(bf16[288,256]{1,0:T(8,128)(2,1)S(1)} %fusion.8), channel_id=1, source_target_pairs={{0,224},{16,240},{32,0},{48,16},{64,32},{80,48},{96,64},{112,80},{... | collective-permute-start | bytes 442376 | tf_op jit(solution)/shard_map/ppermute | solution.py:403
  17.2 3.5 %collective-permute-done = bf16[288,256]{1,0:T(8,128)(2,1)S(1)} collective-permute-done((bf16[288,256]{1,0:T(8,128)(2,1)S(1)}, bf16[288,256]{1,0:T(8,128)(2,1)S(1)}, u32[]{:S(2)}, u32[]{:S(2)}) %collective-permute-start) | collective-permute-done | bytes 147488 | tf_op jit(solution)/shard_map/ppermute | solution.py:403
  20.7 2.7 %collective-permute-start.3 = (bf16[288,256]{1,0:T(8,128)(2,1)S(1)}, bf16[288,256]{1,0:T(8,128)(2,1)S(1)}, u32[]{:S(2)}, u32[]{:S(2)}) collective-permute-start(bf16[288,256]{1,0:T(8,128)(2,1)S(1)} %collective-permute-done.2), channel_id=1, source_target_pairs={{0,224},{16,240},{32,0},{48,16},{64,32},{80,48},{96,64},{112,80},{... | collective-permute-start | bytes 442376 | tf_op jit(solution)/shard_map/ppermute | solution.py:403
  23.7 2.9 %shard_map.129 = (bf16[256,5120]{1,0:T(8,128)(2,1)S(1)}, bf16[256,5248]{1,0:T(8,128)(2,1)S(1)}) custom-call(s32[128,2]{1,0:T(8,128)S(1)} %copy.17.refs_0_, bf16[128,2]{1,0:T(8,128)(2,1)S(1)} %copy.15.refs_1_, s32[128,1]{1,0:T(8,128)S(1)} %copy.16.refs_2_, bf16[128,4096]{1,0:T(8,128)(2,1)S(1)} %copy-done.6, bf16[128,4096]{1,0:T(8,128)(2,1)S(1)} %copy-done.7), custom_call_target="tpu_custom_call" | custom-call | tf_op jit(solution)/shard_map/pallas_call | solution.py:379
  26.6 1.5 copy-done.2
  29.6 6.8 %all-to-all-start = ((bf16[16,16,5120]{2,1,0:T(8,128)(2,1)}), bf16[16,16,5120]{2,1,0:T(8,128)(2,1)S(1)}, u32[]{:S(2)}, u32[]{:S(2)}) async-start(bf16[16,16,5120]{2,1,0:T(8,128)(2,1)} %bitcast.67), calls=%async_computation | async-start | bytes 5242880 | tf_op jit(solution)/shard_map/all_to_all | solution.py:398
  37.7 2.7 %collective-permute-start.6 = (bf16[288,256]{1,0:T(8,128)(2,1)S(1)}, bf16[288,256]{1,0:T(8,128)(2,1)S(1)}, u32[]{:S(2)}, u32[]{:S(2)}) collective-permute-start(bf16[288,256]{1,0:T(8,128)(2,1)S(1)} %collective-permute-done.3), channel_id=1, source_target_pairs={{0,224},{16,240},{32,0},{48,16},{64,32},{80,48},{96,64},{112,80},{... | collective-permute-start | bytes 442376 | tf_op jit(solution)/shard_map/ppermute | solution.py:403
  40.4 31.1 %all-to-all-done = bf16[16,16,5120]{2,1,0:T(8,128)(2,1)S(1)} async-done(((bf16[16,16,5120]{2,1,0:T(8,128)(2,1)}), bf16[16,16,5120]{2,1,0:T(8,128)(2,1)S(1)}, u32[]{:S(2)}, u32[]{:S(2)}) %all-to-all-start) | async-done | bytes 2621472 | tf_op jit(solution)/shard_map/all_to_all | solution.py:398
  71.4 5.7 %all-to-all-start.1 = ((bf16[16,16,5248]{2,1,0:T(8,128)(2,1)}), bf16[16,16,5248]{2,1,0:T(8,128)(2,1)}, u32[]{:S(2)}, u32[]{:S(2)}) async-start(bf16[16,16,5248]{2,1,0:T(8,128)(2,1)} %bitcast.66), calls=%async_computation.1 | async-start | bytes 5373952 | tf_op jit(solution)/shard_map/all_to_all | solution.py:398
  78.5 8.8 %collective-permute-done.5 = bf16[288,256]{1,0:T(8,128)(2,1)S(1)} collective-permute-done((bf16[288,256]{1,0:T(8,128)(2,1)S(1)}, bf16[288,256]{1,0:T(8,128)(2,1)S(1)}, u32[]{:S(2)}, u32[]{:S(2)}) %collective-permute-start.5) | collective-permute-done | bytes 147488 | tf_op jit(solution)/shard_map/ppermute | solution.py:403
  90.0 2.8 %collective-permute-start.7 = (bf16[8,288,256]{2,1,0:T(8,128)(2,1)}, bf16[8,288,256]{2,1,0:T(8,128)(2,1)}, u32[]{:S(2)}, u32[]{:S(2)}) collective-permute-start(bf16[8,288,256]{2,1,0:T(8,128)(2,1)} %bitcast_dynamic-update-slice_fusion.own_ref), channel_id=1, source_target_pairs={{0,16},{16,0},{32,48},{48,32},{64,80},{80,64},{96,112},{112,96},{1... | collective-permute-start | bytes 3538952 | tf_op jit(solution)/shard_map/ppermute | solution.py:420
  92.9 3.0 %collective-permute-done.7.other_ref = bf16[8,288,256]{2,1,0:T(8,128)(2,1)} collective-permute-done((bf16[8,288,256]{2,1,0:T(8,128)(2,1)}, bf16[8,288,256]{2,1,0:T(8,128)(2,1)}, u32[]{:S(2)}, u32[]{:S(2)}) %collective-permute-start.7) | collective-permute-done | bytes 1179680 | tf_op jit(solution)/shard_map/ppermute | solution.py:420
  97.2 1.6 assemble_adapters.1
  101.4 1.6 copy-done.1
  103.0 10.5 %all-to-all-done.1 = bf16[16,16,5248]{2,1,0:T(8,128)(2,1)} async-done(((bf16[16,16,5248]{2,1,0:T(8,128)(2,1)}), bf16[16,16,5248]{2,1,0:T(8,128)(2,1)}, u32[]{:S(2)}, u32[]{:S(2)}) %all-to-all-start.1) | async-done | bytes 2687008 | tf_op jit(solution)/shard_map/all_to_all | solution.py:398
  113.5 5.6 %prepare_cotangent.1 = (bf16[320,4096]{1,0:T(8,128)(2,1)}, f32[320,128]{1,0:T(8,128)}, f32[320,128]{1,0:T(8,128)}, f32[320,128]{1,0:T(8,128)}, bf16[320,128]{1,0...) custom-call(bf16[256,5248]{1,0:T(8,128)(2,1)} %bitcast.9.src_ref, bf16[768,128]{1,0:T(8,128)(2,1)} %copy-done.8, ...), custom_call_target="tpu_custom_call" | custom-call | tf_op jit(solution)/shard_map/prepare_cotangent/pallas_call | solution.py:442
  119.1 1.6 all-gather.2.cloned.1.call-done.w_hbm
  120.8 17.4 %expert.1 = (bf16[256,5248]{1,0:T(8,128)(2,1)}, bf16[320,768]{1,0:T(8,128)(2,1)}, bf16[320,128]{1,0:T(8,128)(2,1)}) custom-call(bf16[320,4096]{1,0:T(8,128)(2,1)} %copy-done.1, bf16[320,4096]{1,0:T(8,128)(2,1)} %get-tuple-element.41.c_hbm.c_ref, bf16[4096,2176]{1,0:T(8,128)(2,1)} %all-gather.2.cloned.1.call-done.w_hbm, bf16[768,128]{1,0:T(8,128)(2,1)} %copy-done.8, ...), custom_call_target="tpu_custom_call" | custom-call | tf_op jit(solution)/shard_map/expert/pallas_call | solution.py:459
  138.2 6.7 %all-to-all-start.2 = ((bf16[16,16,5248]{2,1,0:T(8,128)(2,1)}), bf16[16,16,5248]{2,1,0:T(8,128)(2,1)S(1)}, u32[]{:S(2)}, u32[]{:S(2)}) async-start(bf16[16,16,5248]{2,1,0:T(8,128)(2,1)} %bitcast.68), calls=%async_computation.2 | async-start | bytes 5373952 | tf_op jit(solution)/shard_map/all_to_all | solution.py:398
  144.9 1.7 copy-done
  146.7 2.8 %adapters.1 = (bf16[8,160,256]{2,1,0:T(8,128)(2,1)S(1)}, bf16[8,160,256]{2,1,0:T(8,128)(2,1)S(1)}) custom-call(s32[2]{0:T(128)S(1)} %pad_add_fusion.where_ref, bf16[320,768]{1,0:T(8,128)(2,1)S(1)} %copy-done.9, bf16[320,128]{1,0:T(8,128)(2,1)S(1)} %copy-done.10, bf16[320,128]{1,0:T(8,128)(2,1)S(1)} %copy-done.11, bf16[320,4096]{1,0:T(8,128)(2,1)S(1)} %copy-done), custom_call_target="tpu_custom_call" | custom-call | flops 400000000 | bytes 6000000 | tf_op jit(solution)/shard_map/adapters/pallas_call | solution.py:490
  150.1 1.7 collective-permute-done.8
  152.1 3.9 %collective-permute-start.11 = (bf16[160,256]{1,0:T(8,128)(2,1)S(1)}, bf16[160,256]{1,0:T(8,128)(2,1)S(1)}, u32[]{:S(2)}, u32[]{:S(2)}) collective-permute-start(bf16[160,256]{1,0:T(8,128)(2,1)S(1)} %get-tuple-element.67), channel_id=1, source_target_pairs={{0,96},{16,112},{32,128},{48,144},{64,160},{80,176},{96,192},{112,... | collective-permute-start | bytes 245768 | tf_op jit(solution)/shard_map/ppermute | solution.py:511
  156.3 4.3 %collective-permute-start.13 = (bf16[160,256]{1,0:T(8,128)(2,1)S(1)}, bf16[160,256]{1,0:T(8,128)(2,1)S(1)}, u32[]{:S(2)}, u32[]{:S(2)}) collective-permute-start(bf16[160,256]{1,0:T(8,128)(2,1)S(1)} %get-tuple-element.65), channel_id=1, source_target_pairs={{0,160},{16,176},{32,192},{48,208},{64,224},{80,240},{96,0},{112,1... | collective-permute-start | bytes 245768 | tf_op jit(solution)/shard_map/ppermute | solution.py:511
  160.6 2.8 %collective-permute-start.14 = (bf16[160,256]{1,0:T(8,128)(2,1)S(1)}, bf16[160,256]{1,0:T(8,128)(2,1)S(1)}, u32[]{:S(2)}, u32[]{:S(2)}) collective-permute-start(bf16[160,256]{1,0:T(8,128)(2,1)S(1)} %get-tuple-element.64), channel_id=1, source_target_pairs={{0,192},{16,208},{32,224},{48,240},{64,0},{80,16},{96,32},{112,48}... | collective-permute-start | bytes 245768 | tf_op jit(solution)/shard_map/ppermute | solution.py:511
  163.4 1.9 collective-permute-done.11
  165.3 2.5 %collective-permute-start.9 = (bf16[160,256]{1,0:T(8,128)(2,1)S(1)}, bf16[160,256]{1,0:T(8,128)(2,1)S(1)}, u32[]{:S(2)}, u32[]{:S(2)}) collective-permute-start(bf16[160,256]{1,0:T(8,128)(2,1)S(1)} %get-tuple-element.62), channel_id=1, source_target_pairs={{0,32},{16,48},{32,64},{48,80},{64,96},{80,112},{96,128},{112,144}... | collective-permute-start | bytes 245768 | tf_op jit(solution)/shard_map/ppermute | solution.py:511
  168.3 5.0 %collective-permute-done.14 = bf16[160,256]{1,0:T(8,128)(2,1)S(1)} collective-permute-done((bf16[160,256]{1,0:T(8,128)(2,1)S(1)}, bf16[160,256]{1,0:T(8,128)(2,1)S(1)}, u32[]{:S(2)}, u32[]{:S(2)}) %collective-permute-start.14) | collective-permute-done | bytes 81952 | tf_op jit(solution)/shard_map/ppermute | solution.py:511
  174.6 11.3 %all-to-all-done.2 = bf16[16,16,5248]{2,1,0:T(8,128)(2,1)S(1)} async-done(((bf16[16,16,5248]{2,1,0:T(8,128)(2,1)}), bf16[16,16,5248]{2,1,0:T(8,128)(2,1)S(1)}, u32[]{:S(2)}, u32[]{:S(2)}) %all-to-all-start.2) | async-done | bytes 2687008 | tf_op jit(solution)/shard_map/all_to_all | solution.py:398
  185.9 2.1 %shard_map.130 = (bf16[128,4096]{1,0:T(8,128)(2,1)}, bf16[128,2]{1,0:T(8,128)(2,1)S(1)}) custom-call(s32[128,2]{1,0:T(8,128)S(1)} %copy.17.refs_0_, bf16[256,5248]{1,0:T(8,128)(2,1)S(1)} %bitcast.64), custom_call_target="tpu_custom_call" | custom-call | tf_op jit(solution)/shard_map/pallas_call | solution.py:522
  (73 shorter events, 16.0 us)
Async XLA Ops:
  7.2 113.6 %all-gather.2.cloned.1.call-start = ((), (), s32[]{:S(2)}) async-start(), calls=%async_computation.3 | async-start | bytes 18939904 | tf_op jit(solution)/shard_map/all_gather | solution.py:377
  7.2 16.5 %copy-start.7 = (bf16[128,4096]{1,0:T(8,128)(2,1)S(1)}, bf16[128,4096]{1,0:T(8,128)(2,1)}, u32[]{:S(2)}) copy-start(bf16[128,4096]{1,0:T(8,128)(2,1)} %refs_4_.1) | copy-start | bytes 3145732
  9.5 13.8 %copy-start.14 = (s32[128,2]{0,1:T(2,128)S(1)}, s32[128,2]{0,1:T(2,128)}, u32[]{:S(2)}) copy-start(s32[128,2]{0,1:T(2,128)} %param.12) | copy-start | bytes 3076
  9.6 13.9 %copy-start.15 = (s32[128]{0:T(128)S(1)}, s32[128]{0:T(128)}, u32[]{:S(2)}) copy-start(s32[128]{0:T(128)} %param.14) | copy-start | bytes 1540
  9.6 14.0 %copy-start.16 = (bf16[128,2]{0,1:T(2,128)(2,1)S(1)}, bf16[128,2]{0,1:T(2,128)(2,1)}, u32[]{:S(2)}) copy-start(bf16[128,2]{0,1:T(2,128)(2,1)} %param.13) | copy-start | bytes 1540
  9.6 14.1 %copy-start.6 = (bf16[128,4096]{1,0:T(8,128)(2,1)S(1)}, bf16[128,4096]{1,0:T(8,128)(2,1)}, u32[]{:S(2)}) copy-start(bf16[128,4096]{1,0:T(8,128)(2,1)} %refs_3_.1) | copy-start | bytes 3145732
  10.6 10.1 %collective-permute-start = (bf16[288,256]{1,0:T(8,128)(2,1)S(1)}, bf16[288,256]{1,0:T(8,128)(2,1)S(1)}, u32[]{:S(2)}, u32[]{:S(2)}) collective-permute-start(bf16[288,256]{1,0:T(8,128)(2,1)S(1)} %fusion.8), channel_id=1, source_target_pairs={{0,32},{16,48},{32,64},{48,80},{64,96},{80,112},{96,128},{112,144}... | collective-permute-start | bytes 442376 | tf_op jit(solution)/shard_map/ppermute | solution.py:403
  13.1 7.5 %collective-permute-start.2 = (bf16[288,256]{1,0:T(8,128)(2,1)S(1)}, bf16[288,256]{1,0:T(8,128)(2,1)S(1)}, u32[]{:S(2)}, u32[]{:S(2)}) collective-permute-start(bf16[288,256]{1,0:T(8,128)(2,1)S(1)} %fusion.8), channel_id=1, source_target_pairs={{0,224},{16,240},{32,0},{48,16},{64,32},{80,48},{96,64},{112,80},{... | collective-permute-start | bytes 442376 | tf_op jit(solution)/shard_map/ppermute | solution.py:403
  20.6 8.9 %collective-permute-start.1 = (bf16[288,256]{1,0:T(8,128)(2,1)S(1)}, bf16[288,256]{1,0:T(8,128)(2,1)S(1)}, u32[]{:S(2)}, u32[]{:S(2)}) collective-permute-start(bf16[288,256]{1,0:T(8,128)(2,1)S(1)} %collective-permute-done), channel_id=1, source_target_pairs={{0,32},{16,48},{32,64},{48,80},{64,96},{80,112},{96,128},{112,144}... | collective-permute-start | bytes 442376 | tf_op jit(solution)/shard_map/ppermute | solution.py:403
  20.7 8.9 %collective-permute-start.3 = (bf16[288,256]{1,0:T(8,128)(2,1)S(1)}, bf16[288,256]{1,0:T(8,128)(2,1)S(1)}, u32[]{:S(2)}, u32[]{:S(2)}) collective-permute-start(bf16[288,256]{1,0:T(8,128)(2,1)S(1)} %collective-permute-done.2), channel_id=1, source_target_pairs={{0,224},{16,240},{32,0},{48,16},{64,32},{80,48},{96,64},{112,80},{... | collective-permute-start | bytes 442376 | tf_op jit(solution)/shard_map/ppermute | solution.py:403
  26.6 1.5 copy-start.2
  28.1 1.5 copy-start.3
  29.6 41.9 %all-to-all-start = ((bf16[16,16,5120]{2,1,0:T(8,128)(2,1)}), bf16[16,16,5120]{2,1,0:T(8,128)(2,1)S(1)}, u32[]{:S(2)}, u32[]{:S(2)}) async-start(bf16[16,16,5120]{2,1,0:T(8,128)(2,1)} %bitcast.67), calls=%async_computation | async-start | bytes 5242880 | tf_op jit(solution)/shard_map/all_to_all | solution.py:398
  37.7 40.1 %collective-permute-start.4 = (bf16[288,256]{1,0:T(8,128)(2,1)S(1)}, bf16[288,256]{1,0:T(8,128)(2,1)S(1)}, u32[]{:S(2)}, u32[]{:S(2)}) collective-permute-start(bf16[288,256]{1,0:T(8,128)(2,1)S(1)} %collective-permute-done.1), channel_id=1, source_target_pairs={{0,32},{16,48},{32,64},{48,80},{64,96},{80,112},{96,128},{112,144}... | collective-permute-start | bytes 442376 | tf_op jit(solution)/shard_map/ppermute | solution.py:403
  37.7 50.2 %collective-permute-start.6 = (bf16[288,256]{1,0:T(8,128)(2,1)S(1)}, bf16[288,256]{1,0:T(8,128)(2,1)S(1)}, u32[]{:S(2)}, u32[]{:S(2)}) collective-permute-start(bf16[288,256]{1,0:T(8,128)(2,1)S(1)} %collective-permute-done.3), channel_id=1, source_target_pairs={{0,224},{16,240},{32,0},{48,16},{64,32},{80,48},{96,64},{112,80},{... | collective-permute-start | bytes 442376 | tf_op jit(solution)/shard_map/ppermute | solution.py:403
  71.4 42.0 %all-to-all-start.1 = ((bf16[16,16,5248]{2,1,0:T(8,128)(2,1)}), bf16[16,16,5248]{2,1,0:T(8,128)(2,1)}, u32[]{:S(2)}, u32[]{:S(2)}) async-start(bf16[16,16,5248]{2,1,0:T(8,128)(2,1)} %bitcast.66), calls=%async_computation.1 | async-start | bytes 5373952 | tf_op jit(solution)/shard_map/all_to_all | solution.py:398
  77.8 9.5 %collective-permute-start.5 = (bf16[288,256]{1,0:T(8,128)(2,1)S(1)}, bf16[288,256]{1,0:T(8,128)(2,1)S(1)}, u32[]{:S(2)}, u32[]{:S(2)}) collective-permute-start(bf16[288,256]{1,0:T(8,128)(2,1)S(1)} %collective-permute-done.4), channel_id=1, source_target_pairs={{0,32},{16,48},{32,64},{48,80},{64,96},{80,112},{96,128},{112,144}... | collective-permute-start | bytes 442376 | tf_op jit(solution)/shard_map/ppermute | solution.py:403
  90.0 5.9 %collective-permute-start.7 = (bf16[8,288,256]{2,1,0:T(8,128)(2,1)}, bf16[8,288,256]{2,1,0:T(8,128)(2,1)}, u32[]{:S(2)}, u32[]{:S(2)}) collective-permute-start(bf16[8,288,256]{2,1,0:T(8,128)(2,1)} %bitcast_dynamic-update-slice_fusion.own_ref), channel_id=1, source_target_pairs={{0,16},{16,0},{32,48},{48,32},{64,80},{80,64},{96,112},{112,96},{1... | collective-permute-start | bytes 3538952 | tf_op jit(solution)/shard_map/ppermute | solution.py:420
  101.4 1.6 copy-start.1
  138.2 6.7 %copy-start.9 = (bf16[320,768]{1,0:T(8,128)(2,1)S(1)}, bf16[320,768]{1,0:T(8,128)(2,1)}, u32[]{:S(2)}) copy-start(bf16[320,768]{1,0:T(8,128)(2,1)} %get-tuple-element.51.hid_ref) | copy-start | bytes 1474564
  138.2 6.7 %copy-start.10 = (bf16[320,128]{1,0:T(8,128)(2,1)S(1)}, bf16[320,128]{1,0:T(8,128)(2,1)}, u32[]{:S(2)}) copy-start(bf16[320,128]{1,0:T(8,128)(2,1)} %get-tuple-element.52.low_grad_ref) | copy-start | bytes 245764
  138.2 6.7 %copy-start.11 = (bf16[320,128]{1,0:T(8,128)(2,1)S(1)}, bf16[320,128]{1,0:T(8,128)(2,1)}, u32[]{:S(2)}) copy-start(bf16[320,128]{1,0:T(8,128)(2,1)} %get-tuple-element.53.lowt_ref) | copy-start | bytes 245764
  138.2 47.7 %all-to-all-start.2 = ((bf16[16,16,5248]{2,1,0:T(8,128)(2,1)}), bf16[16,16,5248]{2,1,0:T(8,128)(2,1)S(1)}, u32[]{:S(2)}, u32[]{:S(2)}) async-start(bf16[16,16,5248]{2,1,0:T(8,128)(2,1)} %bitcast.68), calls=%async_computation.2 | async-start | bytes 5373952 | tf_op jit(solution)/shard_map/all_to_all | solution.py:398
  144.9 1.7 copy-start
  149.4 2.4 %collective-permute-start.8 = (bf16[8,160,256]{2,1,0:T(8,128)(2,1)S(1)}, bf16[8,160,256]{2,1,0:T(8,128)(2,1)S(1)}, u32[]{:S(2)}, u32[]{:S(2)}) collective-permute-start(bf16[8,160,256]{2,1,0:T(8,128)(2,1)S(1)} %get-tuple-element.55), channel_id=1, source_target_pairs={{0,16},{16,0},{32,48},{48,32},{64,80},{80,64},{96,112},{112,96},{1... | collective-permute-start | bytes 1966088 | tf_op jit(solution)/shard_map/ppermute | solution.py:506
  152.0 11.4 %collective-permute-start.10 = (bf16[160,256]{1,0:T(8,128)(2,1)S(1)}, bf16[160,256]{1,0:T(8,128)(2,1)S(1)}, u32[]{:S(2)}, u32[]{:S(2)}) collective-permute-start(bf16[160,256]{1,0:T(8,128)(2,1)S(1)} %get-tuple-element.68), channel_id=1, source_target_pairs={{0,64},{16,80},{32,96},{48,112},{64,128},{80,144},{96,160},{112,17... | collective-permute-start | bytes 245768 | tf_op jit(solution)/shard_map/ppermute | solution.py:511
  152.1 13.2 %collective-permute-start.11 = (bf16[160,256]{1,0:T(8,128)(2,1)S(1)}, bf16[160,256]{1,0:T(8,128)(2,1)S(1)}, u32[]{:S(2)}, u32[]{:S(2)}) collective-permute-start(bf16[160,256]{1,0:T(8,128)(2,1)S(1)} %get-tuple-element.67), channel_id=1, source_target_pairs={{0,96},{16,112},{32,128},{48,144},{64,160},{80,176},{96,192},{112,... | collective-permute-start | bytes 245768 | tf_op jit(solution)/shard_map/ppermute | solution.py:511
  156.0 11.8 %collective-permute-start.12 = (bf16[160,256]{1,0:T(8,128)(2,1)S(1)}, bf16[160,256]{1,0:T(8,128)(2,1)S(1)}, u32[]{:S(2)}, u32[]{:S(2)}) collective-permute-start(bf16[160,256]{1,0:T(8,128)(2,1)S(1)} %get-tuple-element.66), channel_id=1, source_target_pairs={{0,128},{16,144},{32,160},{48,176},{64,192},{80,208},{96,224},{112... | collective-permute-start | bytes 245768 | tf_op jit(solution)/shard_map/ppermute | solution.py:511
  156.3 12.0 %collective-permute-start.13 = (bf16[160,256]{1,0:T(8,128)(2,1)S(1)}, bf16[160,256]{1,0:T(8,128)(2,1)S(1)}, u32[]{:S(2)}, u32[]{:S(2)}) collective-permute-start(bf16[160,256]{1,0:T(8,128)(2,1)S(1)} %get-tuple-element.65), channel_id=1, source_target_pairs={{0,160},{16,176},{32,192},{48,208},{64,224},{80,240},{96,0},{112,1... | collective-permute-start | bytes 245768 | tf_op jit(solution)/shard_map/ppermute | solution.py:511
  160.6 12.7 %collective-permute-start.14 = (bf16[160,256]{1,0:T(8,128)(2,1)S(1)}, bf16[160,256]{1,0:T(8,128)(2,1)S(1)}, u32[]{:S(2)}, u32[]{:S(2)}) collective-permute-start(bf16[160,256]{1,0:T(8,128)(2,1)S(1)} %get-tuple-element.64), channel_id=1, source_target_pairs={{0,192},{16,208},{32,224},{48,240},{64,0},{80,16},{96,32},{112,48}... | collective-permute-start | bytes 245768 | tf_op jit(solution)/shard_map/ppermute | solution.py:511
  163.4 9.8 %collective-permute-start.15 = (bf16[160,256]{1,0:T(8,128)(2,1)S(1)}, bf16[160,256]{1,0:T(8,128)(2,1)S(1)}, u32[]{:S(2)}, u32[]{:S(2)}) collective-permute-start(bf16[160,256]{1,0:T(8,128)(2,1)S(1)} %get-tuple-element.63), channel_id=1, source_target_pairs={{0,224},{16,240},{32,0},{48,16},{64,32},{80,48},{96,64},{112,80},{... | collective-permute-start | bytes 245768 | tf_op jit(solution)/shard_map/ppermute | solution.py:511
  165.3 8.0 %collective-permute-start.9 = (bf16[160,256]{1,0:T(8,128)(2,1)S(1)}, bf16[160,256]{1,0:T(8,128)(2,1)S(1)}, u32[]{:S(2)}, u32[]{:S(2)}) collective-permute-start(bf16[160,256]{1,0:T(8,128)(2,1)S(1)} %get-tuple-element.62), channel_id=1, source_target_pairs={{0,32},{16,48},{32,64},{48,80},{64,96},{80,112},{96,128},{112,144}... | collective-permute-start | bytes 245768 | tf_op jit(solution)/shard_map/ppermute | solution.py:511
  (5 other events, 5.4 us)
Sparse Core Ops, SparseCore 0:
  9.8 110.8 all-gather.1
